TPU v7x, 256 devices: a whole 4x4x8 slice. The times are simulated.
256 devices in a mesh: rep: 2 (over y_hi), brick: 128 (over x, y_lo, z, core).
Axes of the slice: x: 4, y: 4 (y_hi: 2, y_lo: 2; y = y_hi * 2 + y_lo), z: 8, core: 2. Of those that a mesh axis runs over, the one named last changes fastest.
Arguments:
- noisy: bfloat16 [2, 128, 32, 256], P(None, 'brick'), may hold values from -6 to 6
- w2_in: bfloat16 [16, 1, 3, 3], replicated, may hold values from -3 to 3
- w2_mid: bfloat16 [16, 16, 3, 3], replicated, may hold values from -0.75 to 0.75
- w2_low: bfloat16 [16, 16, 3, 3], replicated, may hold values from -0.75 to 0.75
- w2_deep: bfloat16 [16, 16, 3, 3], replicated, may hold values from -0.75 to 0.75
- w2_up: bfloat16 [16, 32, 3, 3], replicated, may hold values from -0.5 to 0.5
- w2_out: bfloat16 [1, 16], replicated, may hold values from -2 to 2
- w3_in: bfloat16 [8, 1, 3, 3, 3], replicated, may hold values from -1.75 to 1.75
- w3_mid: bfloat16 [8, 8, 3, 3, 3], replicated, may hold values from -0.625 to 0.625
- w3_low: bfloat16 [8, 8, 3, 3, 3], replicated, may hold values from -0.625 to 0.625
- w3_up: bfloat16 [8, 16, 3, 3, 3], replicated, may hold values from -0.4375 to 0.4375
- w3_out: bfloat16 [8, 8], replicated, may hold values from -3 to 3
Outputs:
- organelle_logits: float32 [128, 8, 4, 32, 128], P('brick', 'rep')
All inputs are finite; a program needn't handle non-finite values.
Results may differ from a plain program's by a relative error of at most 0.025.
Values may be sent and summed in bfloat16 or wider, within the bound.
No kernel may reach another device: no remote copies, remote signals or barrier semaphores. Data moves between devices by JAX's collectives and lax.ppermute only.
A program may use at most 64 MiB of HBM per device.

v0:
```python
import jax
import jax.numpy as jnp
from jax import lax
from jax.experimental import pallas as pl
from jax.experimental.pallas import tpu as pltpu
from jax.sharding import Mesh
from jax.sharding import PartitionSpec as P

BF = jnp.bfloat16
F32 = jnp.float32
NI, NZ, NC = 8, 8, 2
VMEM_BYTES = 56 * 1024 * 1024


def iota(shape, dim):
    return lax.broadcasted_iota(jnp.int32, shape, dim)


def nn(a, b):
    return lax.dot_general(a, b, (((1,), (0,)), ((), ())), preferred_element_type=F32)


def nt(a, b):
    return lax.dot_general(a, b, (((1,), (1,)), ((), ())), preferred_element_type=F32)


def lane_spread(rows, channels, first, lanes):
    return (iota((rows, lanes), 1) % channels + first == iota((rows, lanes), 0)).astype(
        F32
    ).astype(BF)


def stacked(taps, at, channels):
    return jnp.concatenate([taps[at * channels : (at + 1) * channels]] * (128 // channels), axis=0)


def same_level(ref, lead, at, blocks, taps, channels):
    cells = 128 // channels
    gap = iota((128, 128), 1) // channels - iota((128, 128), 0) // channels
    zero = jnp.zeros((128, 128), F32)
    own = jnp.where(
        gap == 0, taps[1], jnp.where(gap == -1, taps[0], jnp.where(gap == 1, taps[2], zero))
    ).astype(BF)
    if blocks > 1:
        later = jnp.where(gap == 1 - cells, taps[2], zero).astype(BF)
        earlier = jnp.where(gap == cells - 1, taps[0], zero).astype(BF)
    for out in range(blocks):
        for inp in range(blocks):
            if inp == out:
                block = own
            elif inp == out + 1:
                block = later
            elif inp == out - 1:
                block = earlier
            else:
                block = jnp.zeros((128, 128), BF)
            ref[lead + (pl.ds(out * 128, 128), pl.ds(at + inp * 128, 128))] = block


def from_coarse(ref, lead, at, out_blocks, in_blocks, taps, channels):
    cells = 128 // channels
    lane_cell = iota((128, 128), 1) // channels
    row_cell = iota((128, 128), 0) // channels
    zero = jnp.zeros((128, 128), F32)
    for out in range(out_blocks):
        for inp in range(in_blocks):
            total = zero
            for kx in range(3):
                meets = (row_cell + (out * cells + kx - 1)) >> 1 == lane_cell + inp * cells
                total = total + jnp.where(meets, taps[kx], zero)
            ref[lead + (pl.ds(out * 128, 128), pl.ds(at + inp * 128, 128))] = total.astype(BF)


def pool_matrix(channels, half):
    cells = 128 // channels
    lane, row = iota((128, 128), 1), iota((128, 128), 0)
    meets = ((lane // channels + half * cells) >> 1 == row // channels) & (
        lane % channels == row % channels
    )
    return meets.astype(F32).astype(BF)


def rolled(v, steps):
    return pltpu.roll(v, steps % v.shape[0], 0)


def denoise_kernel(
    planes_ref,
    w_in_ref,
    w_mid_ref,
    w_low_ref,
    w_deep_ref,
    w_up_ref,
    w_out_ref,
    out_ref,
    b_in,
    b_mid,
    b_low,
    b_deep,
    b_up,
    b_pool,
    lhs,
    wide,
    coarse,
    half,
    raised,
    vol,
):
    planes = planes_ref.shape[0]
    rows = planes * 256
    low_rows = planes * 128
    w9 = nn(w_in_ref[...], lane_spread(16, 16, 0, 512))
    xi = iota((32, 512), 0)
    xo = iota((32, 512), 1) // 16
    for ky in range(3):
        total = jnp.zeros((32, 512), F32)
        for kx in range(3):
            total = jnp.where(xi == xo + (kx - 1), w9[kx * 3 + ky : kx * 3 + ky + 1], total)
        b_in[ky * 32 : (ky + 1) * 32] = total.astype(BF)
    b_in[96:128] = jnp.zeros((32, 512), BF)
    spread = lane_spread(16, 16, 0, 128)
    for w_ref, b_ref, blocks in ((w_mid_ref, b_mid, 4), (w_low_ref, b_low, 2), (w_deep_ref, b_deep, 2)):
        w = nn(w_ref[...], spread)
        for ky in range(3):
            taps = [stacked(w, kx * 3 + ky, 16) for kx in range(3)]
            same_level(b_ref, (), ky * blocks * 128, blocks, taps, 16)
    w_skip = nn(w_up_ref[...], lane_spread(32, 16, 0, 128))
    w_rise = nn(w_up_ref[...], lane_spread(32, 16, 16, 128))
    for ky in range(3):
        taps = [stacked(w_skip, kx * 3 + ky, 16) for kx in range(3)]
        same_level(b_up, (), ky * 512, 4, taps, 16)
        taps = [stacked(w_rise, kx * 3 + ky, 16) for kx in range(3)]
        from_coarse(b_up, (), 1536 + ky * 256, 4, 2, taps, 16)
    none = jnp.zeros((128, 128), BF)
    for out in range(2):
        for inp in range(4):
            b_pool[out * 128 : (out + 1) * 128, inp * 128 : (inp + 1) * 128] = (
                pool_matrix(16, inp % 2) if inp // 2 == out else none
            )

    def place(ref, at, width, v, length):
        n = v.shape[0]
        row = iota(v.shape, 0) % length
        ref[:n, at : at + width] = jnp.where(row == 0, 0.0, rolled(v, 1)).astype(BF)
        ref[:n, at + width : at + 2 * width] = v.astype(BF)
        ref[:n, at + 2 * width : at + 3 * width] = jnp.where(
            row == length - 1, 0.0, rolled(v, -1)
        ).astype(BF)

    turned = planes_ref[...].astype(F32).reshape(planes * 32, 256).T
    if planes < 4:
        turned = jnp.concatenate([turned, jnp.zeros((256, 128 - planes * 32), F32)], axis=1)
    row = iota((256, 128), 0)
    lane = iota((256, 128), 1)
    before = jnp.where(row == 0, 0.0, rolled(turned, 1))
    after = jnp.where(row == 255, 0.0, rolled(turned, -1))
    for q in range(planes):
        three = jnp.zeros((256, 128), F32)
        for g, v in enumerate((before, turned, after)):
            three = jnp.where(lane // 32 == g, pltpu.roll(v, ((g - q) * 32) % 128, 1), three)
        first = jnp.maximum(nn(three.astype(BF), b_in[...]), 0.0)
        place(lhs.at[q * 256 : (q + 1) * 256], 0, 512, first, 256)
    skip = jnp.maximum(nt(lhs[...], b_mid[...]), 0.0)
    place(wide, 0, 512, skip, 256)
    fine = nt(skip.astype(BF), b_pool[...])
    for c in range(2):
        half[...] = fine[:, c * 128 : (c + 1) * 128]
        coarse[:, c * 128 : (c + 1) * 128] = 0.25 * (
            half[pl.ds(0, low_rows, stride=2), :] + half[pl.ds(1, low_rows, stride=2), :]
        )
    place(lhs.at[:low_rows], 0, 256, coarse[...], 128)
    low = jnp.maximum(nt(lhs[:low_rows, :768], b_low[...]), 0.0)
    place(lhs.at[:low_rows], 768, 256, low, 128)
    deep = jnp.maximum(nt(lhs[:low_rows, 768:1536], b_deep[...]), 0.0)
    for c in range(2):
        part = deep[:, c * 128 : (c + 1) * 128]
        half[pl.ds(0, low_rows, stride=2), :] = part
        half[pl.ds(1, low_rows, stride=2), :] = part
        raised[:, c * 128 : (c + 1) * 128] = half[...]
    place(wide, 1536, 256, raised[...], 256)
    joined = jnp.maximum(nt(wide[...], b_up[...]), 0.0).astype(BF)
    w_row = nn(w_out_ref[...], lane_spread(16, 16, 0, 512))
    to_lane, cell = iota((128, 512), 0), iota((128, 512), 1) // 16
    total = jnp.zeros((256, 128), F32)
    for q in range(planes):
        b_out = jnp.where(to_lane == q * 32 + cell, w_row, 0.0).astype(BF)
        total = total + nt(joined[q * 256 : (q + 1) * 256], b_out)
    vol[0:8] = jnp.zeros((8, 128), F32)
    vol[264:272] = jnp.zeros((8, 128), F32)
    vol[8:264] = total
    for z in range(NZ):
        out_ref[z] = vol[z * 32 : z * 32 + 48].astype(BF)


def segment_kernel(
    v_ref,
    w_in_ref,
    w_mid_ref,
    w_low_ref,
    w_up_ref,
    w_out_ref,
    out_ref,
    b_in,
    b_mid,
    b_low,
    b_up,
    vz,
    vl,
    h1l,
    pool,
    ql,
    rise,
    l4,
):
    rep, at_i, at_z, at_c = (lax.axis_index(name) for name in ("rep", "i", "z", "c"))
    w27 = nn(w_in_ref[...], lane_spread(8, 8, 0, 256))
    xi = iota((32, 256), 0)
    xo = iota((32, 256), 1) // 8
    for ky in range(3):
        for kz in range(3):
            plain = jnp.zeros((32, 256), F32)
            mirror = jnp.zeros((32, 256), F32)
            for kx in range(3):
                tap = (kx * 3 + ky) * 3 + kz
                plain = jnp.where(xi == xo + (kx - 1), w27[tap : tap + 1], plain)
                mirror = jnp.where(xi == (32 - kx) - xo, w27[tap : tap + 1], mirror)
            at = ky * 128 + kz * 32
            b_in[at : at + 32, :256] = plain.astype(BF)
            b_in[at : at + 32, 256:] = mirror.astype(BF)
        b_in[ky * 128 + 96 : ky * 128 + 128] = jnp.zeros((32, 512), BF)
    spread = lane_spread(8, 8, 0, 128)
    w_mid = nn(w_mid_ref[...], spread)
    w_low = nn(w_low_ref[...], spread)
    w_skip = nn(w_up_ref[...], lane_spread(16, 8, 0, 128))
    w_rise = nn(w_up_ref[...], lane_spread(16, 8, 8, 128))
    for ky in range(3):
        for kz in range(3):
            for w, b_ref, at, blocks in (
                (w_mid, b_mid, kz * 256, 2),
                (w_low, b_low, kz * 128, 1),
                (w_skip, b_up, kz * 256, 2),
            ):
                taps = [stacked(w, (kx * 3 + ky) * 3 + kz, 8) for kx in range(3)]
                same_level(b_ref, (ky,), at, blocks, taps, 8)
            taps = [stacked(w_rise, (kx * 3 + ky) * 3 + kz, 8) for kx in range(3)]
            from_coarse(b_up, (ky,), 768 + kz * 128, 2, 1, taps, 8)

    out_lane = iota((128, 512), 1)
    select = (
        (iota((128, 512), 0) == (out_lane // 128) * 32 + out_lane % 32) & (out_lane % 128 < 96)
    ).astype(F32).astype(BF)
    vz[...] = jnp.zeros(vz.shape, F32)
    for src in range(NZ):
        spread_v = nn(v_ref[src], select)
        for q in range(4):
            z_row = 8 + 2 * src + q
            if q >= 2:
                if src >= 5:
                    z_row = 2 * src + (q - 2) - 8
                elif src <= 2:
                    z_row = 24 + 2 * src + (q - 2)
                else:
                    continue
            vz[pl.ds(z_row, 48, stride=32), :] = spread_v[:, q * 128 : (q + 1) * 128]
    v = vz[...]
    lane = iota(v.shape, 1)
    v = jnp.where(lane < 32, rolled(v, 1), jnp.where(lane < 64, v, rolled(v, -1)))
    v = v.astype(BF).reshape(48, 32, 128)
    for ky in range(3):
        vl[:, :, ky * 128 : (ky + 1) * 128] = v[2 + ky : 44 + ky]

    z_base = 128 * at_c + 16 * at_i - 8
    y_base = 32 * at_z

    def inside(y_count, y_first, z_count, z_first, limit_y, limit_z):
        r = iota((y_count * z_count, 128), 0)
        y = r // z_count + y_first
        z = r % z_count + z_first
        return ((y >= 0) & (y < limit_y) & (z >= 0) & (z < limit_z)).astype(F32)

    def masked(v, mask):
        return jnp.maximum(v, 0.0) * jnp.concatenate([mask] * (v.shape[1] // 128), axis=1)

    part = 14
    for step in range(3):
        y0 = step * part
        n = part * 32
        h1 = nn(vl[y0 : y0 + part].reshape(n, 384), b_in[...])
        mask = inside(part, y_base - 5 + y0, 32, z_base, 256, 256)
        for copy in range(2):
            h = masked(h1[:, copy * 256 : (copy + 1) * 256], mask)
            for kz, steps in enumerate((1, 0, -1)):
                moved = rolled(h, steps) if steps else h
                h1l[copy, y0 : y0 + part, :, kz * 256 : (kz + 1) * 256] = moved.astype(BF).reshape(
                    part, 32, 256
                )

    pool_t = jnp.concatenate([pool_matrix(8, 0), pool_matrix(8, 1)], axis=1)
    lane_r = iota((128, 256), 1)
    row_r = iota((128, 256), 0)
    w_out = nn(w_out_ref[...], lane_spread(8, 8, 0, 256)).astype(BF)
    pick = (iota((128, 8), 1) == (iota((128, 8), 0) // 4) % 4 + 4 * rep).astype(F32).astype(BF)
    w_rows = nn(pick, w_out)
    x_row = (row_r // 16) * 4 + row_r % 4
    logits = jnp.zeros((128, 512), F32)
    for copy in range(2):
        part = 20
        n = part * 32
        for step in range(2):
            y0 = step * part
            acc = jnp.zeros((n, 256), F32)
            for ky in range(3):
                acc = acc + nt(h1l[copy, y0 + ky : y0 + ky + part].reshape(n, 768), b_mid[ky])
            h2 = masked(acc, inside(part, y_base - 4 + y0, 32, z_base, 256, 256))
            fine = nt(h2.astype(BF), pool_t).reshape(part // 2, 2, 32, 128)
            pool[y0 * 16 : y0 * 16 + n // 2] = (fine[:, 0] + fine[:, 1]).reshape(n // 2, 128)
            first, last = max(y0, 3), min(y0 + part, 37)
            for kz in range(3):
                moved = rolled(h2, -(7 + kz)).reshape(part, 32, 256)
                l4[copy, first - 3 : last - 3, :, kz * 256 : (kz + 1) * 256] = moved[
                    first - y0 : last - y0, :16
                ].astype(BF)
        q = 0.125 * (pool[pl.ds(0, 320, stride=2), :] + pool[pl.ds(1, 320, stride=2), :])
        for kz, steps in enumerate((1, 0, -1)):
            moved = rolled(q, steps) if steps else q
            ql[:, :, kz * 128 : (kz + 1) * 128] = moved.astype(BF).reshape(20, 16, 128)
        acc = jnp.zeros((288, 128), F32)
        for ky in range(3):
            acc = acc + nt(ql[ky : ky + 18].reshape(288, 384), b_low[ky])
        h3 = masked(
            acc, inside(18, 16 * at_z - 1, 16, 64 * at_c + 8 * at_i - 4, 128, 128)
        )
        rise[pl.ds(0, 288, stride=2), :] = h3
        rise[pl.ds(1, 288, stride=2), :] = h3
        r = rise[...]
        for kz in range(3):
            moved = rolled(r, -(7 + kz)).reshape(18, 32, 128)[:, :16].astype(BF)
            for slot in range(34):
                l4[copy, slot, :, 768 + kz * 128 : 896 + kz * 128] = moved[(slot + 3) // 2 - 1]
        acc = jnp.zeros((512, 256), F32)
        for ky in range(3):
            acc = acc + nt(l4[copy, ky : ky + 32].reshape(512, 1152), b_up[ky])
        h4 = jnp.maximum(acc, 0.0).astype(BF)
        x_lane = lane_r // 8 if copy == 0 else 31 - lane_r // 8
        b_out = jnp.where(x_lane == x_row, w_rows, 0.0).astype(BF)
        logits = logits + nt(b_out, h4)
    out_ref[...] = (0.5 * logits).astype(BF).reshape(NI, 16, 512)


def arrange_kernel(parts_ref, out_ref):
    lane = iota((16, 128), 1) // 16
    for o in range(4):
        parts = [parts_ref[src, :, o * 128 : (o + 1) * 128].astype(F32) for src in range(NI)]
        for y in range(8):
            total = jnp.zeros((16, 128), F32)
            for src in range(NI):
                moved = parts[src]
                if src != y:
                    moved = pltpu.roll(moved, ((src - y) * 16) % 128, 1)
                total = jnp.where(lane == src, moved, total)
            out_ref[pl.ds(o * 8 + y, 16, stride=32), :] = total


def call(kernel, out_shape, scratch, *args):
    return pl.pallas_call(
        kernel,
        out_shape=out_shape,
        in_specs=[pl.BlockSpec(memory_space=pltpu.VMEM)] * len(args),
        out_specs=pl.BlockSpec(memory_space=pltpu.VMEM),
        scratch_shapes=scratch,
        compiler_params=pltpu.CompilerParams(vmem_limit_bytes=VMEM_BYTES),
    )(*args)


def flat2(w):
    return w.transpose(2, 3, 0, 1).reshape(-1, w.shape[1])


def flat3(w):
    return w.transpose(2, 3, 4, 0, 1).reshape(-1, w.shape[1])


def rim_pairs():
    pairs = []

    def index(i, z, c):
        return (i * NZ + z) * NC + c

    for c in range(NC):
        for z in range(NZ):
            for i in range(NI):
                if z >= 5:
                    if i < NI - 1:
                        pairs.append((index(i, z, c), index(i + 1, z, c)))
                    elif c == 0:
                        pairs.append((index(i, z, 0), index(0, z, 1)))
                if z <= 2:
                    if i > 0:
                        pairs.append((index(i, z, c), index(i - 1, z, c)))
                    elif c == 1:
                        pairs.append((index(i, z, 1), index(NI - 1, z, 0)))
    return pairs


def per_device(
    noisy, w2_in, w2_mid, w2_low, w2_deep, w2_up, w2_out, w3_in, w3_mid, w3_low, w3_up, w3_out
):
    second = lax.axis_index("c") == 1
    low_half, high_half = noisy[0, 0], noisy[1, 0]
    sent = jnp.where(second, low_half, high_half)
    got = lax.ppermute(sent, "c", [(0, 1), (1, 0)])
    own = jnp.stack([jnp.where(second, got, low_half), jnp.where(second, high_half, got)])
    rim = lax.ppermute(own, ("i", "z", "c"), rim_pairs())
    planes = jnp.concatenate([own, rim], axis=0)
    count = planes.shape[0]
    vmem = pltpu.VMEM
    volume = call(
        denoise_kernel,
        jax.ShapeDtypeStruct((NZ, 48, 128), BF),
        [
            vmem((128, 512), BF),
            vmem((512, 1536), BF),
            vmem((256, 768), BF),
            vmem((256, 768), BF),
            vmem((512, 2304), BF),
            vmem((256, 512), BF),
            vmem((count * 256, 1536), BF),
            vmem((count * 256, 2304), BF),
            vmem((count * 128, 256), F32),
            vmem((count * 256, 128), F32),
            vmem((count * 256, 256), F32),
            vmem((272, 128), F32),
        ],
        planes,
        w2_in.transpose(2, 3, 1, 0).reshape(9, 16),
        flat2(w2_mid),
        flat2(w2_low),
        flat2(w2_deep),
        flat2(w2_up),
        w2_out,
    )
    window = lax.all_to_all(volume, "z", 0, 0, tiled=True)
    logits = call(
        segment_kernel,
        jax.ShapeDtypeStruct((NI, 16, 512), BF),
        [
            vmem((384, 512), BF),
            vmem((3, 256, 768), BF),
            vmem((3, 128, 384), BF),
            vmem((3, 256, 1152), BF),
            vmem((48 * 32, 128), F32),
            vmem((42, 32, 384), BF),
            vmem((2, 42, 32, 768), BF),
            vmem((640, 128), F32),
            vmem((20, 16, 384), BF),
            vmem((576, 128), F32),
            vmem((2, 34, 16, 1152), BF),
        ],
        window,
        w3_in.transpose(2, 3, 4, 1, 0).reshape(27, 8),
        flat3(w3_mid),
        flat3(w3_low),
        flat3(w3_up),
        w3_out,
    )
    parts = lax.all_to_all(logits, "i", 0, 0, tiled=True)
    out = call(arrange_kernel, jax.ShapeDtypeStruct((512, 128), F32), [], parts)
    return out.reshape(1, 4, 4, 32, 128)


def solution(mesh):
    finer = Mesh(mesh.devices.reshape(2, NI, NZ, NC), ("rep", "i", "z", "c"))
    brick = ("i", "z", "c")
    placed = (P(None, brick, None, None),) + (P(),) * 11
    return jax.shard_map(
        per_device,
        mesh=finer,
        in_specs=placed,
        out_specs=P(brick, "rep", None, None, None),
        check_vma=False,
    )
```

profile of v0, /device:TPU:16, one launch (start us, length us, event | category | flops | bytes accessed | tf_op | source)
XLA Modules:
  0.0 61.8 jit_solution(7666077375110446142)
XLA Ops:
  0.0 0.0 copy-start.1
  0.0 0.8 %bitcast_select_fusion.1 = bf16[32,256]{1,0:T(8,128)(2,1)S(1)} fusion(pred[]{:T(512)S(6)} %eq.3, bf16[2,1,32,256]{3,2,1,0:T(8,128)(2,1)} %param.12), kind=kLoop, calls=%fused_computation.3 | loop fusion | flops 8192 | bytes 49153 | tf_op jit(solution)/shard_map/jit(_where)/select_n | solution.py:410
  0.8 0.0 collective-permute-start
  0.8 1.2 %collective-permute-done = bf16[32,256]{1,0:T(8,128)(2,1)S(1)} collective-permute-done((bf16[32,256]{1,0:T(8,128)(2,1)S(1)}, bf16[32,256]{1,0:T(8,128)(2,1)S(1)}, u32[]{:S(2)}, u32[]{:S(2)}) %collective-permute-start) | collective-permute-done | bytes 16416 | tf_op jit(solution)/shard_map/ppermute | solution.py:411
  2.0 0.0 copy-done.1
  2.0 0.0 copy-start.3
  2.0 1.3 %collective-permute-start.1 = (bf16[2,32,256]{2,1,0:T(8,128)(2,1)S(1)}, bf16[2,32,256]{2,1,0:T(8,128)(2,1)S(1)}, u32[]{:S(2)}, u32[]{:S(2)}) collective-permute-start(bf16[2,32,256]{2,1,0:T(8,128)(2,1)S(1)} %pad_maximum_fusion.1), channel_id=1, source_target_pairs={{16,0},{32,16},{48,32},{64,48},{80,64},{96,80},{112,96},{18,2},{34... | collective-permute-start | bytes 98312 | tf_op jit(solution)/shard_map/ppermute | solution.py:413
  3.3 0.0 copy-done.3
  3.3 0.6 reshape.30.w_in_ref
  3.9 3.9 %collective-permute-done.1 = bf16[2,32,256]{2,1,0:T(8,128)(2,1)S(1)} collective-permute-done((bf16[2,32,256]{2,1,0:T(8,128)(2,1)S(1)}, bf16[2,32,256]{2,1,0:T(8,128)(2,1)S(1)}, u32[]{:S(2)}, u32[]{:S(2)}) %collective-permute-start.1) | collective-permute-done | bytes 32800 | tf_op jit(solution)/shard_map/ppermute | solution.py:413
  7.8 0.6 %pad_maximum_fusion.planes_ref = bf16[4,32,256]{2,1,0:T(8,128)(2,1)} fusion(bf16[2,32,256]{2,1,0:T(8,128)(2,1)S(1)} %collective-permute-done.1, bf16[1,32,256]{2,1,0:T(8,128)(2,1)S(1)} %get-tuple-element.6, bf16[1,32,256]{2,1,0:T(8,128)(2,1)S(1)} %get-tuple-element.5), kind=kLoop, calls=%fused_computation | loop fusion | flops 65536 | bytes 131072 | tf_op jit(solution)/shard_map/concatenate | solution.py:414
  8.5 9.0 %shard_map.118 = bf16[8,48,128]{2,1,0:T(8,128)(2,1)} custom-call(bf16[4,32,256]{2,1,0:T(8,128)(2,1)} %pad_maximum_fusion.planes_ref, bf16[9,16]{1,0:T(8,128)(2,1)} %reshape.30.w_in_ref, bf16[144,16]{1,0:T(8,128)(2,1)} %bitcast.45, bf16[144,16]{1,0:T(8,128)(2,1)} %bitcast.46, bf16[144,16]{1,0:T(8,128)(2,1)} %bitcast.47, bf16[144,32]{1,0:T(8,128)(2,1)} %bitcast.48, ...), custom_call_target="tpu_custom_call" | custom-call | tf_op jit(solution)/shard_map/pallas_call | solution.py:365
  17.4 0.0 copy-start.2
  17.4 7.1 %all-to-all-start = ((bf16[8,48,128]{2,1,0:T(8,128)(2,1)}), bf16[8,48,128]{2,1,0:T(8,128)(2,1)S(1)}, u32[]{:S(2)}, u32[]{:S(2)}) async-start(bf16[8,48,128]{2,1,0:T(8,128)(2,1)} %shard_map.118), calls=%async_computation | async-start | bytes 196608 | tf_op jit(solution)/shard_map/all_to_all | solution.py:442
  24.5 0.0 copy-done.2
  24.6 0.6 reshape.35.w_in_ref
  25.2 8.1 %all-to-all-done.v_ref = bf16[8,48,128]{2,1,0:T(8,128)(2,1)S(1)} async-done(((bf16[8,48,128]{2,1,0:T(8,128)(2,1)}), bf16[8,48,128]{2,1,0:T(8,128)(2,1)S(1)}, u32[]{:S(2)}, u32[]{:S(2)}) %all-to-all-start) | async-done | bytes 98336 | tf_op jit(solution)/shard_map/all_to_all | solution.py:442
  33.3 0.0 copy-start
  33.3 0.6 %copy-done = bf16[8,48,128]{2,1,0:T(8,128)(2,1)} copy-done((bf16[8,48,128]{2,1,0:T(8,128)(2,1)}, bf16[8,48,128]{2,1,0:T(8,128)(2,1)S(1)}, u32[]{:S(2)}) %copy-start) | copy-done | bytes 98328
  33.9 13.2 %shard_map.119 = bf16[8,16,512]{2,1,0:T(8,128)(2,1)} custom-call(bf16[8,48,128]{2,1,0:T(8,128)(2,1)} %copy-done, bf16[27,8]{1,0:T(8,128)(2,1)} %reshape.35.w_in_ref, bf16[216,8]{1,0:T(8,128)(2,1)} %bitcast.42, bf16[216,8]{1,0:T(8,128)(2,1)} %bitcast.43, bf16[216,16]{1,0:T(8,128)(2,1)} %bitcast.44, bf16[8,8]{1,0:T(8,128)(2,1)} %w_out_ref.3), custom_call_target="tpu_custom_call" | custom-call | tf_op jit(solution)/shard_map/pallas_call | solution.py:365
  47.1 12.7 %all_to_all.10.parts_ref = bf16[8,16,512]{2,1,0:T(8,128)(2,1)} all-to-all(bf16[8,16,512]{2,1,0:T(8,128)(2,1)} %shard_map.119), channel_id=1, replica_groups=mesh['rep'=2,'i'=8,'z'=8,'c'=2] {'i'}, dimensions={0} | all-to-all | bytes 262144 | tf_op jit(solution)/shard_map/all_to_all | solution.py:466
  59.8 2.0 %shard_map.120 = f32[512,128]{1,0:T(8,128)} custom-call(bf16[8,16,512]{2,1,0:T(8,128)(2,1)} %all_to_all.10.parts_ref), custom_call_target="tpu_custom_call" | custom-call | tf_op jit(solution)/shard_map/pallas_call | solution.py:365
  (2 shorter events, 0.0 us)
Async XLA Ops:
  0.0 2.0 %copy-start.1 = (bf16[2,1,32,256]{3,2,1,0:T(8,128)(2,1)S(1)}, bf16[2,1,32,256]{3,2,1,0:T(8,128)(2,1)}, u32[]{:S(2)}) copy-start(bf16[2,1,32,256]{3,2,1,0:T(8,128)(2,1)} %param.12) | copy-start | bytes 98308
  0.8 1.2 %collective-permute-start = (bf16[32,256]{1,0:T(8,128)(2,1)S(1)}, bf16[32,256]{1,0:T(8,128)(2,1)S(1)}, u32[]{:S(2)}, u32[]{:S(2)}) collective-permute-start(bf16[32,256]{1,0:T(8,128)(2,1)S(1)} %bitcast_select_fusion.1), channel_id=1, source_target_pairs={{0,1},{1,0},{2,3},{3,2},{4,5},{5,4},{6,7},{7,6},{8,9},{9,8},{10,11... | collective-permute-start | bytes 49160 | tf_op jit(solution)/shard_map/ppermute | solution.py:411
  2.0 1.3 %copy-start.3 = (bf16[16,1,3,3]{0,3,2,1:T(4,128)(2,1)S(1)}, bf16[16,1,3,3]{0,3,2,1:T(4,128)(2,1)}, u32[]{:S(2)}) copy-start(bf16[16,1,3,3]{0,3,2,1:T(4,128)(2,1)} %param.13) | copy-start | bytes 868
  2.0 5.8 %collective-permute-start.1 = (bf16[2,32,256]{2,1,0:T(8,128)(2,1)S(1)}, bf16[2,32,256]{2,1,0:T(8,128)(2,1)S(1)}, u32[]{:S(2)}, u32[]{:S(2)}) collective-permute-start(bf16[2,32,256]{2,1,0:T(8,128)(2,1)S(1)} %pad_maximum_fusion.1), channel_id=1, source_target_pairs={{16,0},{32,16},{48,32},{64,48},{80,64},{96,80},{112,96},{18,2},{34... | collective-permute-start | bytes 98312 | tf_op jit(solution)/shard_map/ppermute | solution.py:413
  17.4 7.1 %copy-start.2 = (bf16[8,1,3,3,3]{0,4,3,2,1:T(4,128)(2,1)S(1)}, bf16[8,1,3,3,3]{0,4,3,2,1:T(4,128)(2,1)}, u32[]{:S(2)}) copy-start(bf16[8,1,3,3,3]{0,4,3,2,1:T(4,128)(2,1)} %param.19) | copy-start | bytes 1300
  17.4 15.8 %all-to-all-start = ((bf16[8,48,128]{2,1,0:T(8,128)(2,1)}), bf16[8,48,128]{2,1,0:T(8,128)(2,1)S(1)}, u32[]{:S(2)}, u32[]{:S(2)}) async-start(bf16[8,48,128]{2,1,0:T(8,128)(2,1)} %shard_map.118), calls=%async_computation | async-start | bytes 196608 | tf_op jit(solution)/shard_map/all_to_all | solution.py:442
  33.3 0.6 %copy-start = (bf16[8,48,128]{2,1,0:T(8,128)(2,1)}, bf16[8,48,128]{2,1,0:T(8,128)(2,1)S(1)}, u32[]{:S(2)}) copy-start(bf16[8,48,128]{2,1,0:T(8,128)(2,1)S(1)} %all-to-all-done.v_ref) | copy-start | bytes 294916
where the time goes:
time: 62.3 us; the launch traced here: 61.8 us
  Pallas kernels  24.1 us (39%)
  waiting for transfers between devices  13.2 us (21%)
  blocking collectives  12.7 us (20%)
  starting transfers between devices  8.4 us (13%)
  local copies, waits for them, and re-layouts  1.86 us (3%)
  other arithmetic  1.45 us (2%)
    pallas_call x3, Pallas kernels, call(): pl.pallas_call(kernel, out_shape=out_shape, in_specs=[pl.BlockSpec(memory...  24.1 us
    all_to_all x1, blocking collectives, per_device(): parts = lax.all_to_all(logits, 'i', 0, 0, tiled=True)  12.7 us
    all_to_all x1, waiting for transfers between devices, per_device(): window = lax.all_to_all(volume, 'z', 0, 0, tiled=True)  8.12 us
    all_to_all x1, starting transfers between devices, per_device(): window = lax.all_to_all(volume, 'z', 0, 0, tiled=True)  7.11 us
    ppermute x1, waiting for transfers between devices, per_device(): rim = lax.ppermute(own, ('i', 'z', 'c'), rim_pairs())  3.9 us
    ppermute x1, starting transfers between devices, per_device(): rim = lax.ppermute(own, ('i', 'z', 'c'), rim_pairs())  1.29 us
  transfers between devices with their start and end apart: 3, of which 3 were waited for; matrix products, arithmetic and copies ran while one was open for 2% of the time, Pallas kernels for 0%

commit v1 on v0

--- a/solution.py
+++ b/solution.py
@@ -1,3 +1,5 @@
+import functools
+
 import jax
 import jax.numpy as jnp
 from jax import lax
@@ -9,7 +11,6 @@
 BF = jnp.bfloat16
 F32 = jnp.float32
 NI, NZ, NC = 8, 8, 2
-VMEM_BYTES = 56 * 1024 * 1024
 
 
 def iota(shape, dim):
@@ -84,43 +85,23 @@
     return pltpu.roll(v, steps % v.shape[0], 0)
 
 
-def denoise_kernel(
-    planes_ref,
-    w_in_ref,
-    w_mid_ref,
-    w_low_ref,
-    w_deep_ref,
-    w_up_ref,
-    w_out_ref,
-    out_ref,
-    b_in,
-    b_mid,
-    b_low,
-    b_deep,
-    b_up,
-    b_pool,
-    lhs,
-    wide,
-    coarse,
-    half,
-    raised,
-    vol,
-):
-    planes = planes_ref.shape[0]
-    rows = planes * 256
-    low_rows = planes * 128
-    w9 = nn(w_in_ref[...], lane_spread(16, 16, 0, 512))
+def plane_weights_kernel(w_ref, b_in, b_mid, b_low, b_deep, b_up, b_pool, b_last):
+    w_mid_ref, w_low_ref, w_deep_ref, w_up_ref = (
+        w_ref.at[at * 144 : (at + 1) * 144] for at in range(4)
+    )
+    edge = nn(w_ref[576:640], lane_spread(32, 16, 0, 512))
+    w9, w_row = [edge[kx * 16 : kx * 16 + 3] for kx in range(3)], edge[48:49]
     xi = iota((32, 512), 0)
     xo = iota((32, 512), 1) // 16
     for ky in range(3):
         total = jnp.zeros((32, 512), F32)
         for kx in range(3):
-            total = jnp.where(xi == xo + (kx - 1), w9[kx * 3 + ky : kx * 3 + ky + 1], total)
+            total = jnp.where(xi == xo + (kx - 1), w9[kx][ky : ky + 1], total)
         b_in[ky * 32 : (ky + 1) * 32] = total.astype(BF)
     b_in[96:128] = jnp.zeros((32, 512), BF)
-    spread = lane_spread(16, 16, 0, 128)
-    for w_ref, b_ref, blocks in ((w_mid_ref, b_mid, 4), (w_low_ref, b_low, 2), (w_deep_ref, b_deep, 2)):
-        w = nn(w_ref[...], spread)
+    spread = lane_spread(32, 16, 0, 128)
+    for taps_ref, b_ref, blocks in ((w_mid_ref, b_mid, 4), (w_low_ref, b_low, 2), (w_deep_ref, b_deep, 2)):
+        w = nn(taps_ref[...], spread)
         for ky in range(3):
             taps = [stacked(w, kx * 3 + ky, 16) for kx in range(3)]
             same_level(b_ref, (), ky * blocks * 128, blocks, taps, 16)
@@ -137,6 +118,18 @@
             b_pool[out * 128 : (out + 1) * 128, inp * 128 : (inp + 1) * 128] = (
                 pool_matrix(16, inp % 2) if inp // 2 == out else none
             )
+    to_lane, cell = iota((128, 512), 0), iota((128, 512), 1) // 16
+    for q in range(4):
+        b_last[q] = jnp.where(to_lane == q * 32 + cell, w_row, 0.0).astype(BF)
+
+
+def denoise_kernel(first_plane, continues, planes_ref, *refs):
+    before_ref = refs[0] if continues else None
+    refs = refs[continues:]
+    b_in, b_mid, b_low, b_deep, b_up, b_pool, b_last, out_ref = refs[:8]
+    lhs, wide, coarse, half, raised, vol = refs[8:]
+    planes = planes_ref.shape[0]
+    low_rows = planes * 128
 
     def place(ref, at, width, v, length):
         n = v.shape[0]
@@ -179,41 +172,24 @@
         raised[:, c * 128 : (c + 1) * 128] = half[...]
     place(wide, 1536, 256, raised[...], 256)
     joined = jnp.maximum(nt(wide[...], b_up[...]), 0.0).astype(BF)
-    w_row = nn(w_out_ref[...], lane_spread(16, 16, 0, 512))
-    to_lane, cell = iota((128, 512), 0), iota((128, 512), 1) // 16
     total = jnp.zeros((256, 128), F32)
     for q in range(planes):
-        b_out = jnp.where(to_lane == q * 32 + cell, w_row, 0.0).astype(BF)
-        total = total + nt(joined[q * 256 : (q + 1) * 256], b_out)
+        total = total + nt(joined[q * 256 : (q + 1) * 256], b_last[first_plane + q])
     vol[0:8] = jnp.zeros((8, 128), F32)
     vol[264:272] = jnp.zeros((8, 128), F32)
     vol[8:264] = total
     for z in range(NZ):
-        out_ref[z] = vol[z * 32 : z * 32 + 48].astype(BF)
-
-
-def segment_kernel(
-    v_ref,
-    w_in_ref,
-    w_mid_ref,
-    w_low_ref,
-    w_up_ref,
-    w_out_ref,
-    out_ref,
-    b_in,
-    b_mid,
-    b_low,
-    b_up,
-    vz,
-    vl,
-    h1l,
-    pool,
-    ql,
-    rise,
-    l4,
-):
-    rep, at_i, at_z, at_c = (lax.axis_index(name) for name in ("rep", "i", "z", "c"))
-    w27 = nn(w_in_ref[...], lane_spread(8, 8, 0, 256))
+        window = vol[z * 32 : z * 32 + 48]
+        if before_ref is not None:
+            window = window + before_ref[z].astype(F32)
+        out_ref[z] = window.astype(BF)
+
+
+def volume_weights_kernel(w_ref, b_rest, b_mid, b_up):
+    edge = nn(w_ref[648:800], lane_spread(16, 8, 0, 256))
+    spread = lane_spread(16, 8, 0, 128)
+    w_mid, w_low, w_skip = (nn(w_ref[at * 216 : (at + 1) * 216], spread) for at in range(3))
+    w_rise = nn(w_ref[432:648], lane_spread(16, 8, 8, 128))
     xi = iota((32, 256), 0)
     xo = iota((32, 256), 1) // 8
     for ky in range(3):
@@ -221,30 +197,37 @@
             plain = jnp.zeros((32, 256), F32)
             mirror = jnp.zeros((32, 256), F32)
             for kx in range(3):
-                tap = (kx * 3 + ky) * 3 + kz
-                plain = jnp.where(xi == xo + (kx - 1), w27[tap : tap + 1], plain)
-                mirror = jnp.where(xi == (32 - kx) - xo, w27[tap : tap + 1], mirror)
+                at = (kx * 3 + ky) * 16 + kz
+                tap = edge[at : at + 1]
+                plain = jnp.where(xi == xo + (kx - 1), tap, plain)
+                mirror = jnp.where(xi == (32 - kx) - xo, tap, mirror)
             at = ky * 128 + kz * 32
-            b_in[at : at + 32, :256] = plain.astype(BF)
-            b_in[at : at + 32, 256:] = mirror.astype(BF)
-        b_in[ky * 128 + 96 : ky * 128 + 128] = jnp.zeros((32, 512), BF)
-    spread = lane_spread(8, 8, 0, 128)
-    w_mid = nn(w_mid_ref[...], spread)
-    w_low = nn(w_low_ref[...], spread)
-    w_skip = nn(w_up_ref[...], lane_spread(16, 8, 0, 128))
-    w_rise = nn(w_up_ref[...], lane_spread(16, 8, 8, 128))
+            b_rest[at : at + 32, :256] = plain.astype(BF)
+            b_rest[at : at + 32, 256:512] = mirror.astype(BF)
+        b_rest[ky * 128 + 96 : ky * 128 + 128, :512] = jnp.zeros((32, 512), BF)
     for ky in range(3):
         for kz in range(3):
             for w, b_ref, at, blocks in (
-                (w_mid, b_mid, kz * 256, 2),
-                (w_low, b_low, kz * 128, 1),
-                (w_skip, b_up, kz * 256, 2),
+                (w_mid, b_mid.at[ky], kz * 256, 2),
+                (w_low, b_rest.at[ky * 128 : ky * 128 + 128], 512 + kz * 128, 1),
+                (w_skip, b_up.at[ky], kz * 256, 2),
             ):
                 taps = [stacked(w, (kx * 3 + ky) * 3 + kz, 8) for kx in range(3)]
-                same_level(b_ref, (ky,), at, blocks, taps, 8)
+                same_level(b_ref, (), at, blocks, taps, 8)
             taps = [stacked(w_rise, (kx * 3 + ky) * 3 + kz, 8) for kx in range(3)]
             from_coarse(b_up, (ky,), 768 + kz * 128, 2, 1, taps, 8)
-
+    w_out = edge[144:152].astype(BF)
+    row_r = iota((128, 256), 0)
+    cell = iota((128, 256), 1) // 8
+    pick = (iota((128, 8), 1) == (iota((128, 8), 0) // 4) % 4 + 4 * lax.axis_index("rep"))
+    w_rows = nn(pick.astype(F32).astype(BF), w_out)
+    x_row = (row_r // 16) * 4 + row_r % 4
+    b_rest[:128, 896:] = jnp.where(cell == x_row, w_rows, 0.0).astype(BF)
+    b_rest[128:256, 896:] = jnp.where(31 - cell == x_row, w_rows, 0.0).astype(BF)
+
+
+def segment_kernel(v_ref, b_rest, b_mid, b_up, out_ref, vz, vl, h1l, pool, ql, rise, l4):
+    at_i, at_z, at_c = (lax.axis_index(name) for name in ("i", "z", "c"))
     out_lane = iota((128, 512), 1)
     select = (
         (iota((128, 512), 0) == (out_lane // 128) * 32 + out_lane % 32) & (out_lane % 128 < 96)
@@ -272,11 +255,16 @@
     z_base = 128 * at_c + 16 * at_i - 8
     y_base = 32 * at_z
 
-    def inside(y_count, y_first, z_count, z_first, limit_y, limit_z):
-        r = iota((y_count * z_count, 128), 0)
-        y = r // z_count + y_first
-        z = r % z_count + z_first
-        return ((y >= 0) & (y < limit_y) & (z >= 0) & (z < limit_z)).astype(F32)
+    def inside(y_count, y_first, z_count, z_first, limit):
+        z = iota((z_count, 128), 0) + z_first
+        rows = ((z >= 0) & (z < limit)).astype(F32)
+        return jnp.concatenate(
+            [
+                rows * jnp.where((y_first + y >= 0) & (y_first + y < limit), 1.0, 0.0)
+                for y in range(y_count)
+            ],
+            axis=0,
+        )
 
     def masked(v, mask):
         return jnp.maximum(v, 0.0) * jnp.concatenate([mask] * (v.shape[1] // 128), axis=1)
@@ -285,8 +273,8 @@
     for step in range(3):
         y0 = step * part
         n = part * 32
-        h1 = nn(vl[y0 : y0 + part].reshape(n, 384), b_in[...])
-        mask = inside(part, y_base - 5 + y0, 32, z_base, 256, 256)
+        h1 = nn(vl[y0 : y0 + part].reshape(n, 384), b_rest[:, :512])
+        mask = inside(part, y_base - 5 + y0, 32, z_base, 256)
         for copy in range(2):
             h = masked(h1[:, copy * 256 : (copy + 1) * 256], mask)
             for kz, steps in enumerate((1, 0, -1)):
@@ -296,12 +284,6 @@
                 )
 
     pool_t = jnp.concatenate([pool_matrix(8, 0), pool_matrix(8, 1)], axis=1)
-    lane_r = iota((128, 256), 1)
-    row_r = iota((128, 256), 0)
-    w_out = nn(w_out_ref[...], lane_spread(8, 8, 0, 256)).astype(BF)
-    pick = (iota((128, 8), 1) == (iota((128, 8), 0) // 4) % 4 + 4 * rep).astype(F32).astype(BF)
-    w_rows = nn(pick, w_out)
-    x_row = (row_r // 16) * 4 + row_r % 4
     logits = jnp.zeros((128, 512), F32)
     for copy in range(2):
         part = 20
@@ -311,7 +293,7 @@
             acc = jnp.zeros((n, 256), F32)
             for ky in range(3):
                 acc = acc + nt(h1l[copy, y0 + ky : y0 + ky + part].reshape(n, 768), b_mid[ky])
-            h2 = masked(acc, inside(part, y_base - 4 + y0, 32, z_base, 256, 256))
+            h2 = masked(acc, inside(part, y_base - 4 + y0, 32, z_base, 256))
             fine = nt(h2.astype(BF), pool_t).reshape(part // 2, 2, 32, 128)
             pool[y0 * 16 : y0 * 16 + n // 2] = (fine[:, 0] + fine[:, 1]).reshape(n // 2, 128)
             first, last = max(y0, 3), min(y0 + part, 37)
@@ -326,9 +308,9 @@
             ql[:, :, kz * 128 : (kz + 1) * 128] = moved.astype(BF).reshape(20, 16, 128)
         acc = jnp.zeros((288, 128), F32)
         for ky in range(3):
-            acc = acc + nt(ql[ky : ky + 18].reshape(288, 384), b_low[ky])
+            acc = acc + nt(ql[ky : ky + 18].reshape(288, 384), b_rest[ky * 128 : ky * 128 + 128, 512:896])
         h3 = masked(
-            acc, inside(18, 16 * at_z - 1, 16, 64 * at_c + 8 * at_i - 4, 128, 128)
+            acc, inside(18, 16 * at_z - 1, 16, 64 * at_c + 8 * at_i - 4, 128)
         )
         rise[pl.ds(0, 288, stride=2), :] = h3
         rise[pl.ds(1, 288, stride=2), :] = h3
@@ -341,9 +323,7 @@
         for ky in range(3):
             acc = acc + nt(l4[copy, ky : ky + 32].reshape(512, 1152), b_up[ky])
         h4 = jnp.maximum(acc, 0.0).astype(BF)
-        x_lane = lane_r // 8 if copy == 0 else 31 - lane_r // 8
-        b_out = jnp.where(x_lane == x_row, w_rows, 0.0).astype(BF)
-        logits = logits + nt(b_out, h4)
+        logits = logits + nt(b_rest[copy * 128 : copy * 128 + 128, 896:], h4)
     out_ref[...] = (0.5 * logits).astype(BF).reshape(NI, 16, 512)
 
 
@@ -351,29 +331,45 @@
     lane = iota((16, 128), 1) // 16
     for o in range(4):
         parts = [parts_ref[src, :, o * 128 : (o + 1) * 128].astype(F32) for src in range(NI)]
+        for bit in (1, 2, 4):
+            upper = (lane & bit) != 0
+            for low in range(NI):
+                if low & bit == 0:
+                    first, second = parts[low], parts[low | bit]
+                    parts[low] = jnp.where(upper, pltpu.roll(second, 16 * bit, 1), first)
+                    parts[low | bit] = jnp.where(upper, second, pltpu.roll(first, 128 - 16 * bit, 1))
         for y in range(8):
-            total = jnp.zeros((16, 128), F32)
-            for src in range(NI):
-                moved = parts[src]
-                if src != y:
-                    moved = pltpu.roll(moved, ((src - y) * 16) % 128, 1)
-                total = jnp.where(lane == src, moved, total)
-            out_ref[pl.ds(o * 8 + y, 16, stride=32), :] = total
-
-
-def call(kernel, out_shape, scratch, *args):
+            out_ref[pl.ds(o * 8 + y, 16, stride=32), :] = parts[y]
+
+
+def call(kernel, out_shape, scratch, megabytes, *args):
+    spec = pl.BlockSpec(memory_space=pltpu.VMEM)
     return pl.pallas_call(
         kernel,
         out_shape=out_shape,
-        in_specs=[pl.BlockSpec(memory_space=pltpu.VMEM)] * len(args),
-        out_specs=pl.BlockSpec(memory_space=pltpu.VMEM),
+        in_specs=[spec] * len(args),
+        out_specs=jax.tree.map(lambda _: spec, out_shape),
         scratch_shapes=scratch,
-        compiler_params=pltpu.CompilerParams(vmem_limit_bytes=VMEM_BYTES),
+        compiler_params=pltpu.CompilerParams(vmem_limit_bytes=megabytes * 1024 * 1024),
     )(*args)
+
+
+def bf(*shape):
+    return jax.ShapeDtypeStruct(shape, BF)
 
 
 def flat2(w):
     return w.transpose(2, 3, 0, 1).reshape(-1, w.shape[1])
+
+
+def table(rows, width, *weights):
+    total, at = None, 0
+    for w in weights:
+        n = w.shape[0]
+        filled = jnp.pad(w, ((at, rows - at - n), (0, width - w.shape[1])))
+        total = filled if total is None else total + filled
+        at += n
+    return total
 
 
 def flat3(w):
@@ -402,6 +398,27 @@
     return pairs
 
 
+def denoise(first_plane, planes, before, *weights):
+    count = planes.shape[0]
+    args = (planes,) if before is None else (planes, before)
+    vmem = pltpu.VMEM
+    return call(
+        functools.partial(denoise_kernel, first_plane, before is not None),
+        bf(NZ, 48, 128),
+        [
+            vmem((count * 256, 1536), BF),
+            vmem((count * 256, 2304), BF),
+            vmem((count * 128, 256), F32),
+            vmem((count * 256, 128), F32),
+            vmem((count * 256, 256), F32),
+            vmem((272, 128), F32),
+        ],
+        24,
+        *args,
+        *weights,
+    )
+
+
 def per_device(
     noisy, w2_in, w2_mid, w2_low, w2_deep, w2_up, w2_out, w3_in, w3_mid, w3_low, w3_up, w3_out
 ):
@@ -409,45 +426,42 @@
     low_half, high_half = noisy[0, 0], noisy[1, 0]
     sent = jnp.where(second, low_half, high_half)
     got = lax.ppermute(sent, "c", [(0, 1), (1, 0)])
+    w_in = jnp.pad(w2_in.transpose(1, 2, 3, 0)[0], ((0, 0), (0, 13), (0, 0))).reshape(48, 16)
+    taps = (flat2(w2_mid), flat2(w2_low), flat2(w2_deep), flat2(w2_up), w_in, w2_out)
+    weights = call(
+        plane_weights_kernel,
+        [
+            bf(128, 512),
+            bf(512, 1536),
+            bf(256, 768),
+            bf(256, 768),
+            bf(512, 2304),
+            bf(256, 512),
+            bf(4, 128, 512),
+        ],
+        [],
+        16,
+        table(640, 32, *taps),
+    )
     own = jnp.stack([jnp.where(second, got, low_half), jnp.where(second, high_half, got)])
     rim = lax.ppermute(own, ("i", "z", "c"), rim_pairs())
-    planes = jnp.concatenate([own, rim], axis=0)
-    count = planes.shape[0]
+    volume = denoise(0, own, None, *weights)
+    volume = denoise(2, rim, volume, *weights)
+    window = lax.all_to_all(volume, "z", 0, 0, tiled=True)
+    w_in = jnp.pad(w3_in.transpose(1, 2, 3, 4, 0)[0], ((0, 0), (0, 0), (0, 13), (0, 0)))
+    taps = (flat3(w3_mid), flat3(w3_low), flat3(w3_up), w_in.reshape(144, 8), w3_out)
+    volume_weights = call(
+        volume_weights_kernel,
+        [bf(384, 1152), bf(3, 256, 768), bf(3, 256, 1152)],
+        [],
+        16,
+        table(800, 16, *taps),
+    )
     vmem = pltpu.VMEM
-    volume = call(
-        denoise_kernel,
-        jax.ShapeDtypeStruct((NZ, 48, 128), BF),
-        [
-            vmem((128, 512), BF),
-            vmem((512, 1536), BF),
-            vmem((256, 768), BF),
-            vmem((256, 768), BF),
-            vmem((512, 2304), BF),
-            vmem((256, 512), BF),
-            vmem((count * 256, 1536), BF),
-            vmem((count * 256, 2304), BF),
-            vmem((count * 128, 256), F32),
-            vmem((count * 256, 128), F32),
-            vmem((count * 256, 256), F32),
-            vmem((272, 128), F32),
-        ],
-        planes,
-        w2_in.transpose(2, 3, 1, 0).reshape(9, 16),
-        flat2(w2_mid),
-        flat2(w2_low),
-        flat2(w2_deep),
-        flat2(w2_up),
-        w2_out,
-    )
-    window = lax.all_to_all(volume, "z", 0, 0, tiled=True)
     logits = call(
         segment_kernel,
-        jax.ShapeDtypeStruct((NI, 16, 512), BF),
+        bf(NI, 16, 512),
         [
-            vmem((384, 512), BF),
-            vmem((3, 256, 768), BF),
-            vmem((3, 128, 384), BF),
-            vmem((3, 256, 1152), BF),
             vmem((48 * 32, 128), F32),
             vmem((42, 32, 384), BF),
             vmem((2, 42, 32, 768), BF),
@@ -456,15 +470,12 @@
             vmem((576, 128), F32),
             vmem((2, 34, 16, 1152), BF),
         ],
+        24,
         window,
-        w3_in.transpose(2, 3, 4, 1, 0).reshape(27, 8),
-        flat3(w3_mid),
-        flat3(w3_low),
-        flat3(w3_up),
-        w3_out,
+        *volume_weights,
     )
     parts = lax.all_to_all(logits, "i", 0, 0, tiled=True)
-    out = call(arrange_kernel, jax.ShapeDtypeStruct((512, 128), F32), [], parts)
+    out = call(arrange_kernel, jax.ShapeDtypeStruct((512, 128), F32), [], 4, parts)
     return out.reshape(1, 4, 4, 32, 128)
 
 

time: 62.3 us -> 57.7 us (0.926)
  waiting for transfers between devices: 13.2 us -> 6.86 us
  starting transfers between devices: 8.4 us -> 11.2 us
  Pallas kernels: 24.1 us -> 22.3 us
  blocking collectives: 12.7 us -> 11.3 us
  other arithmetic: 1.45 us -> 2.41 us
  local copies, waits for them, and re-layouts: 1.86 us -> 2.81 us
    ppermute x1, waiting for transfers between devices: 3.9 us -> 0.01 us  [per_device(): rim = lax.ppermute(own, ('i', 'z', 'c'), rim_pairs())]
    all_to_all x1, starting transfers between devices: 7.11 us -> 9.92 us  [per_device(): window = lax.all_to_all(volume, 'z', 0, 0, tiled=True)]
    pallas_call x3 -> x6, Pallas kernels: 24.1 us -> 22.3 us  [call(): pl.pallas_call(kernel, out_shape=out_shape, in_specs=[spec] * len(args),...]
    all_to_all x1, waiting for transfers between devices: 8.12 us -> 6.36 us  [per_device(): window = lax.all_to_all(volume, 'z', 0, 0, tiled=True)]
    unnamed x8 -> x14, local copies, waits for them, and re-layouts: 0.65 us -> 2.11 us
    all_to_all x1, blocking collectives: 12.7 us -> 11.3 us  [per_device(): parts = lax.all_to_all(logits, 'i', 0, 0, tiled=True)]
    reshape x2 -> x0, local copies, waits for them, and re-layouts: 1.21 us -> none  [the longest x1 0.61 us: per_device(): w3_in.transpose(2, 3, 4, 1, 0).reshape(27, 8)]
    add x0 -> x2, other arithmetic: none -> 0.92 us  [table(): total = filled if total is None else total + filled]
  transfers between devices with their start and end apart: 3 -> 3, of which waited for: 3 -> 2; matrix products, arithmetic and copies ran while one was open for 2% -> 3% of each run, Pallas kernels for 0% -> 11%
where the time goes in v1:
time: 57.7 us; the launch traced here: 57.1 us
  Pallas kernels  22.3 us (39%)
  blocking collectives  11.3 us (20%)
  starting transfers between devices  11.2 us (19%)
  waiting for transfers between devices  6.86 us (12%)
  local copies, waits for them, and re-layouts  2.81 us (5%)
  other arithmetic  2.41 us (4%)
    pallas_call x6, Pallas kernels, call(): pl.pallas_call(kernel, out_shape=out_shape, in_specs=[spec] * len(args),...  22.3 us
    all_to_all x1, blocking collectives, per_device(): parts = lax.all_to_all(logits, 'i', 0, 0, tiled=True)  11.3 us
    all_to_all x1, starting transfers between devices, per_device(): window = lax.all_to_all(volume, 'z', 0, 0, tiled=True)  9.92 us
    all_to_all x1, waiting for transfers between devices, per_device(): window = lax.all_to_all(volume, 'z', 0, 0, tiled=True)  6.36 us
    unnamed x14, local copies, waits for them, and re-layouts  2.11 us
    ppermute x1, starting transfers between devices, per_device(): rim = lax.ppermute(own, ('i', 'z', 'c'), rim_pairs())  1.29 us
  transfers between devices with their start and end apart: 3, of which 2 were waited for; matrix products, arithmetic and copies ran while one was open for 3% of the time, Pallas kernels for 11%

profile of v1, /device:TPU:16, one launch (start us, length us, event | category | flops | bytes accessed | tf_op | source)
XLA Modules:
  0.0 57.1 jit_solution(3488366160910163850)
XLA Ops:
  0.0 0.7 %bitcast_select_fusion.1 = bf16[32,256]{1,0:T(8,128)(2,1)S(1)} fusion(pred[]{:T(512)S(6)} %eq.3, bf16[2,1,32,256]{3,2,1,0:T(8,128)(2,1)} %param.12), kind=kLoop, calls=%fused_computation.4 | loop fusion | flops 8192 | bytes 49153 | tf_op jit(solution)/shard_map/jit(_where)/select_n | solution.py:427
  0.7 0.0 collective-permute-start
  0.7 0.7 %pad.56 = bf16[3,16,16]{2,1,0:T(8,128)(2,1)S(1)} pad(bf16[3,3,16]{2,1,0:T(4,128)(2,1)} %bitcast.54, bf16[]{:T(256)} %constant.8.clone.1), padding=0_0x0_13x0_0 | pad | bytes 1826 | tf_op jit(solution)/shard_map/jit(_pad)/pad | solution.py:429
  1.4 0.5 collective-permute-done
  1.9 0.7 %fusion.1 = (bf16[1,32,256]{2,1,0:T(8,128)(2,1)S(1)}, bf16[1,32,256]{2,1,0:T(8,128)(2,1)S(1)}) fusion(bf16[32,256]{1,0:T(8,128)(2,1)S(1)} %collective-permute-done, pred[]{:T(512)S(6)} %eq.3, bf16[2,1,32,256]{3,2,1,0:T(8,128)(2,1)} %param.12), kind=kLoop, calls=%fused_computation.7 | loop fusion | flops 16384 | bytes 81921 | tf_op jit(solution)/shard_map/stack | solution.py:446
  2.7 1.3 %collective-permute-start.1 = (bf16[2,32,256]{2,1,0:T(8,128)(2,1)S(1)}, bf16[2,32,256]{2,1,0:T(8,128)(2,1)S(1)}, u32[]{:S(2)}, u32[]{:S(2)}) collective-permute-start(bf16[2,32,256]{2,1,0:T(8,128)(2,1)S(1)} %pad_maximum_fusion.planes_ref), channel_id=1, source_target_pairs={{16,0},{32,16},{48,32},{64,48},{80,64},{96,80},{112,96},{18,2},{34... | collective-permute-start | bytes 98312 | tf_op jit(solution)/shard_map/ppermute | solution.py:447
  4.0 0.9 %pad_add_fusion.1.w_ref = bf16[640,32]{1,0:T(8,128)(2,1)S(1)} fusion(bf16[1,16]{1,0:T(2,128)(2,1)} %param.18, bf16[48,16]{1,0:T(8,128)(2,1)S(1)} %bitcast.48, bf16[144,32]{1,0:T(8,128)(2,1)} %bitcast.49, bf16[144,16]{1,0:T(8,128)(2,1)} %bitcast.50, bf16[144,16]{1,0:T(8,128)(2,1)} %bitcast.51, bf16[144,16]{1,0:T(8,128)(2,1)} %bitcast.52), kind=kLoop, calls=%fused_computation.1 | loop fusion | flops 245760 | bytes 65568 | tf_op jit(solution)/shard_map/add | solution.py:370
  4.9 1.4 %shard_map.118 = (bf16[128,512]{1,0:T(8,128)(2,1)S(1)}, bf16[512,1536]{1,0:T(8,128)(2,1)S(1)}, bf16[256,768]{1,0:T(8,128)(2,1)S(1)}, bf16[256,768]{1,0:T(8,128)(...) custom-call(bf16[640,32]{1,0:T(8,128)(2,1)S(1)} %pad_add_fusion.1.w_ref), custom_call_target="tpu_custom_call" | custom-call | tf_op jit(solution)/shard_map/pallas_call | solution.py:347
  6.3 3.7 %shard_map.119.refs_0_ = bf16[8,48,128]{2,1,0:T(8,128)(2,1)S(1)} custom-call(bf16[2,32,256]{2,1,0:T(8,128)(2,1)S(1)} %pad_maximum_fusion.planes_ref, bf16[128,512]{1,0:T(8,128)(2,1)S(1)} %get-tuple-element.15.refs_0_.refs_1_, bf16[512,1536]{1,0:T(8,128)(2,1)S(1)} %get-tuple-element.16.refs_1_.refs_2_, ...), custom_call_target="tpu_custom_call" | custom-call | tf_op jit(solution)/shard_map/pallas_call | solution.py:347
  10.0 0.0 copy-start.5
  10.1 0.0 copy-start.2
  10.1 0.0 copy-start.3
  10.1 0.0 copy-start.4
  10.1 0.0 copy-start.6
  10.1 0.0 collective-permute-done.1.planes_ref
  10.1 4.4 %shard_map.120 = bf16[8,48,128]{2,1,0:T(8,128)(2,1)} custom-call(bf16[2,32,256]{2,1,0:T(8,128)(2,1)S(1)} %collective-permute-done.1.planes_ref, bf16[8,48,128]{2,1,0:T(8,128)(2,1)S(1)} %shard_map.119.refs_0_, bf16[128,512]{1,0:T(8,128)(2,1)S(1)} %get-tuple-element.15.refs_0_.refs_1_, bf16[512,1536]{1,0:T(8,128)(2,1)S(1)} %get-tuple-element.16.refs_1_.refs_2_, ...), custom_call_target="tpu_custom_call" | custom-call | tf_op jit(solution)/shard_map/pallas_call | solution.py:347
  14.5 9.9 %all-to-all-start = ((bf16[8,48,128]{2,1,0:T(8,128)(2,1)}), bf16[8,48,128]{2,1,0:T(8,128)(2,1)S(1)}, u32[]{:S(2)}, u32[]{:S(2)}) async-start(bf16[8,48,128]{2,1,0:T(8,128)(2,1)} %shard_map.120), calls=%async_computation | async-start | bytes 196608 | tf_op jit(solution)/shard_map/all_to_all | solution.py:450
  24.4 0.0 copy-done.5
  24.5 0.0 copy-done.2
  24.5 0.0 copy-done.3
  24.5 0.0 copy-done.4
  24.5 0.0 copy-done.6
  24.5 1.3 %shard_map.121 = (bf16[384,1152]{1,0:T(8,128)(2,1)S(1)}, bf16[3,256,768]{2,1,0:T(8,128)(2,1)S(1)}, bf16[3,256,1152]{2,1,0:T(8,128)(2,1)S(1)}) custom-call(bf16[800,16]{1,0:T(8,128)(2,1)S(1)} %pad_add_fusion.w_ref), custom_call_target="tpu_custom_call" | custom-call | tf_op jit(solution)/shard_map/pallas_call | solution.py:347
  25.9 0.0 copy-start
  25.9 0.9 %copy-done = bf16[384,1152]{1,0:T(8,128)(2,1)} copy-done((bf16[384,1152]{1,0:T(8,128)(2,1)}, bf16[384,1152]{1,0:T(8,128)(2,1)S(1)}, u32[]{:S(2)}) %copy-start) | copy-done | bytes 884760
  26.8 6.4 %all-to-all-done.v_ref = bf16[8,48,128]{2,1,0:T(8,128)(2,1)S(1)} async-done(((bf16[8,48,128]{2,1,0:T(8,128)(2,1)}), bf16[8,48,128]{2,1,0:T(8,128)(2,1)S(1)}, u32[]{:S(2)}, u32[]{:S(2)}) %all-to-all-start) | async-done | bytes 98336 | tf_op jit(solution)/shard_map/all_to_all | solution.py:450
  33.2 0.0 copy-start.1
  33.2 1.2 %copy-done.1 = bf16[384,1152]{1,0:T(8,128)(2,1)S(1)} copy-done((bf16[384,1152]{1,0:T(8,128)(2,1)S(1)}, bf16[384,1152]{1,0:T(8,128)(2,1)}, u32[]{:S(2)}) %copy-start.1) | copy-done | bytes 884760
  34.3 10.3 %shard_map.122 = bf16[8,16,512]{2,1,0:T(8,128)(2,1)S(1)} custom-call(bf16[8,48,128]{2,1,0:T(8,128)(2,1)S(1)} %all-to-all-done.v_ref, bf16[384,1152]{1,0:T(8,128)(2,1)S(1)} %copy-done.1, bf16[3,256,768]{2,1,0:T(8,128)(2,1)S(1)} %get-tuple-element.23.b_mid, bf16[3,256,1152]{2,1,0:T(8,128)(2,1)S(1)} %get-tuple-element.24.b_up), custom_call_target="tpu_custom_call" | custom-call | tf_op jit(solution)/shard_map/pallas_call | solution.py:347
  44.6 11.3 %all_to_all.10.parts_ref = bf16[8,16,512]{2,1,0:T(8,128)(2,1)S(1)} all-to-all(bf16[8,16,512]{2,1,0:T(8,128)(2,1)S(1)} %shard_map.122), channel_id=1, replica_groups=mesh['rep'=2,'i'=8,'z'=8,'c'=2] {'i'}, dimensions={0} | all-to-all | bytes 262144 | tf_op jit(solution)/shard_map/all_to_all | solution.py:477
  55.9 1.1 %shard_map.123 = f32[512,128]{1,0:T(8,128)} custom-call(bf16[8,16,512]{2,1,0:T(8,128)(2,1)S(1)} %all_to_all.10.parts_ref), custom_call_target="tpu_custom_call" | custom-call | tf_op jit(solution)/shard_map/pallas_call | solution.py:347
  (3 shorter events, 0.1 us)
Async XLA Ops:
  0.7 1.2 %collective-permute-start = (bf16[32,256]{1,0:T(8,128)(2,1)S(1)}, bf16[32,256]{1,0:T(8,128)(2,1)S(1)}, u32[]{:S(2)}, u32[]{:S(2)}) collective-permute-start(bf16[32,256]{1,0:T(8,128)(2,1)S(1)} %bitcast_select_fusion.1), channel_id=1, source_target_pairs={{0,1},{1,0},{2,3},{3,2},{4,5},{5,4},{6,7},{7,6},{8,9},{9,8},{10,11... | collective-permute-start | bytes 49160 | tf_op jit(solution)/shard_map/ppermute | solution.py:428
  2.7 7.4 %collective-permute-start.1 = (bf16[2,32,256]{2,1,0:T(8,128)(2,1)S(1)}, bf16[2,32,256]{2,1,0:T(8,128)(2,1)S(1)}, u32[]{:S(2)}, u32[]{:S(2)}) collective-permute-start(bf16[2,32,256]{2,1,0:T(8,128)(2,1)S(1)} %pad_maximum_fusion.planes_ref), channel_id=1, source_target_pairs={{16,0},{32,16},{48,32},{64,48},{80,64},{96,80},{112,96},{18,2},{34... | collective-permute-start | bytes 98312 | tf_op jit(solution)/shard_map/ppermute | solution.py:447
  10.0 14.4 %copy-start.5 = (bf16[8,1,3,3,3]{0,4,3,2,1:T(4,128)(2,1)S(1)}, bf16[8,1,3,3,3]{0,4,3,2,1:T(4,128)(2,1)}, u32[]{:S(2)}) copy-start(bf16[8,1,3,3,3]{0,4,3,2,1:T(4,128)(2,1)} %param.19) | copy-start | bytes 1300
  10.1 14.4 %copy-start.2 = (bf16[8,16,3,3,3]{1,0,4,3,2:T(8,128)(2,1)S(1)}, bf16[8,16,3,3,3]{1,0,4,3,2:T(8,128)(2,1)}, u32[]{:S(2)}) copy-start(bf16[8,16,3,3,3]{1,0,4,3,2:T(8,128)(2,1)} %param.22) | copy-start | bytes 20740
  10.1 14.4 %copy-start.3 = (bf16[8,8,3,3,3]{1,0,4,3,2:T(8,128)(2,1)S(1)}, bf16[8,8,3,3,3]{1,0,4,3,2:T(8,128)(2,1)}, u32[]{:S(2)}) copy-start(bf16[8,8,3,3,3]{1,0,4,3,2:T(8,128)(2,1)} %param.21) | copy-start | bytes 10372
  10.1 14.4 %copy-start.4 = (bf16[8,8,3,3,3]{1,0,4,3,2:T(8,128)(2,1)S(1)}, bf16[8,8,3,3,3]{1,0,4,3,2:T(8,128)(2,1)}, u32[]{:S(2)}) copy-start(bf16[8,8,3,3,3]{1,0,4,3,2:T(8,128)(2,1)} %param.20) | copy-start | bytes 10372
  10.1 14.4 %copy-start.6 = (bf16[8,8]{1,0:T(8,128)(2,1)S(1)}, bf16[8,8]{1,0:T(8,128)(2,1)}, u32[]{:S(2)}) copy-start(bf16[8,8]{1,0:T(8,128)(2,1)} %param.23) | copy-start | bytes 388
  14.5 18.6 %all-to-all-start = ((bf16[8,48,128]{2,1,0:T(8,128)(2,1)}), bf16[8,48,128]{2,1,0:T(8,128)(2,1)S(1)}, u32[]{:S(2)}, u32[]{:S(2)}) async-start(bf16[8,48,128]{2,1,0:T(8,128)(2,1)} %shard_map.120), calls=%async_computation | async-start | bytes 196608 | tf_op jit(solution)/shard_map/all_to_all | solution.py:450
  25.9 0.9 %copy-start = (bf16[384,1152]{1,0:T(8,128)(2,1)}, bf16[384,1152]{1,0:T(8,128)(2,1)S(1)}, u32[]{:S(2)}) copy-start(bf16[384,1152]{1,0:T(8,128)(2,1)S(1)} %get-tuple-element.22.b_rest) | copy-start | bytes 2654212
  33.2 1.2 %copy-start.1 = (bf16[384,1152]{1,0:T(8,128)(2,1)S(1)}, bf16[384,1152]{1,0:T(8,128)(2,1)}, u32[]{:S(2)}) copy-start(bf16[384,1152]{1,0:T(8,128)(2,1)} %copy-done) | copy-start | bytes 2654212

commit v2 on v1

--- a/solution.py
+++ b/solution.py
@@ -86,31 +86,28 @@
 
 
 def plane_weights_kernel(w_ref, b_in, b_mid, b_low, b_deep, b_up, b_pool, b_last):
-    w_mid_ref, w_low_ref, w_deep_ref, w_up_ref = (
-        w_ref.at[at * 144 : (at + 1) * 144] for at in range(4)
-    )
-    edge = nn(w_ref[576:640], lane_spread(32, 16, 0, 512))
-    w9, w_row = [edge[kx * 16 : kx * 16 + 3] for kx in range(3)], edge[48:49]
+    edge = [nn(w_ref[kx, 192:208], lane_spread(32, 16, 0, 512)) for kx in range(3)]
+    w_row = edge[0][3:4]
     xi = iota((32, 512), 0)
     xo = iota((32, 512), 1) // 16
     for ky in range(3):
         total = jnp.zeros((32, 512), F32)
         for kx in range(3):
-            total = jnp.where(xi == xo + (kx - 1), w9[kx][ky : ky + 1], total)
+            total = jnp.where(xi == xo + (kx - 1), edge[kx][ky : ky + 1], total)
         b_in[ky * 32 : (ky + 1) * 32] = total.astype(BF)
     b_in[96:128] = jnp.zeros((32, 512), BF)
     spread = lane_spread(32, 16, 0, 128)
-    for taps_ref, b_ref, blocks in ((w_mid_ref, b_mid, 4), (w_low_ref, b_low, 2), (w_deep_ref, b_deep, 2)):
-        w = nn(taps_ref[...], spread)
+    for at, b_ref, blocks in ((0, b_mid, 4), (48, b_low, 2), (96, b_deep, 2)):
+        w = [nn(w_ref[kx, at : at + 48], spread) for kx in range(3)]
         for ky in range(3):
-            taps = [stacked(w, kx * 3 + ky, 16) for kx in range(3)]
+            taps = [stacked(w[kx], ky, 16) for kx in range(3)]
             same_level(b_ref, (), ky * blocks * 128, blocks, taps, 16)
-    w_skip = nn(w_up_ref[...], lane_spread(32, 16, 0, 128))
-    w_rise = nn(w_up_ref[...], lane_spread(32, 16, 16, 128))
+    w_skip = [nn(w_ref[kx, 144:192], spread) for kx in range(3)]
+    w_rise = [nn(w_ref[kx, 144:192], lane_spread(32, 16, 16, 128)) for kx in range(3)]
     for ky in range(3):
-        taps = [stacked(w_skip, kx * 3 + ky, 16) for kx in range(3)]
+        taps = [stacked(w_skip[kx], ky, 16) for kx in range(3)]
         same_level(b_up, (), ky * 512, 4, taps, 16)
-        taps = [stacked(w_rise, kx * 3 + ky, 16) for kx in range(3)]
+        taps = [stacked(w_rise[kx], ky, 16) for kx in range(3)]
         from_coarse(b_up, (), 1536 + ky * 256, 4, 2, taps, 16)
     none = jnp.zeros((128, 128), BF)
     for out in range(2):
@@ -123,12 +120,12 @@
         b_last[q] = jnp.where(to_lane == q * 32 + cell, w_row, 0.0).astype(BF)
 
 
-def denoise_kernel(first_plane, continues, planes_ref, *refs):
-    before_ref = refs[0] if continues else None
-    refs = refs[continues:]
+def denoise_kernel(rim, planes_ref, *refs):
+    before_ref = refs[0] if rim else None
+    refs = refs[rim:]
     b_in, b_mid, b_low, b_deep, b_up, b_pool, b_last, out_ref = refs[:8]
     lhs, wide, coarse, half, raised, vol = refs[8:]
-    planes = planes_ref.shape[0]
+    planes = 2
     low_rows = planes * 128
 
     def place(ref, at, width, v, length):
@@ -140,9 +137,8 @@
             row == length - 1, 0.0, rolled(v, -1)
         ).astype(BF)
 
-    turned = planes_ref[...].astype(F32).reshape(planes * 32, 256).T
-    if planes < 4:
-        turned = jnp.concatenate([turned, jnp.zeros((256, 128 - planes * 32), F32)], axis=1)
+    turned = planes_ref[...].astype(F32).reshape(64, 256)
+    turned = jnp.concatenate([turned, jnp.zeros((64, 256), F32)], axis=0).T
     row = iota((256, 128), 0)
     lane = iota((256, 128), 1)
     before = jnp.where(row == 0, 0.0, rolled(turned, 1))
@@ -174,7 +170,7 @@
     joined = jnp.maximum(nt(wide[...], b_up[...]), 0.0).astype(BF)
     total = jnp.zeros((256, 128), F32)
     for q in range(planes):
-        total = total + nt(joined[q * 256 : (q + 1) * 256], b_last[first_plane + q])
+        total = total + nt(joined[q * 256 : (q + 1) * 256], b_last[2 * rim + q])
     vol[0:8] = jnp.zeros((8, 128), F32)
     vol[264:272] = jnp.zeros((8, 128), F32)
     vol[8:264] = total
@@ -186,10 +182,12 @@
 
 
 def volume_weights_kernel(w_ref, b_rest, b_mid, b_up):
-    edge = nn(w_ref[648:800], lane_spread(16, 8, 0, 256))
+    edge = [nn(w_ref[kxy, 72:88], lane_spread(16, 8, 0, 256)) for kxy in range(9)]
     spread = lane_spread(16, 8, 0, 128)
-    w_mid, w_low, w_skip = (nn(w_ref[at * 216 : (at + 1) * 216], spread) for at in range(3))
-    w_rise = nn(w_ref[432:648], lane_spread(16, 8, 8, 128))
+    w_mid, w_low, w_skip = (
+        [nn(w_ref[kxy, at : at + 24], spread) for kxy in range(9)] for at in (0, 24, 48)
+    )
+    w_rise = [nn(w_ref[kxy, 48:72], lane_spread(16, 8, 8, 128)) for kxy in range(9)]
     xi = iota((32, 256), 0)
     xo = iota((32, 256), 1) // 8
     for ky in range(3):
@@ -197,33 +195,32 @@
             plain = jnp.zeros((32, 256), F32)
             mirror = jnp.zeros((32, 256), F32)
             for kx in range(3):
-                at = (kx * 3 + ky) * 16 + kz
-                tap = edge[at : at + 1]
+                tap = edge[kx * 3 + ky][kz : kz + 1]
                 plain = jnp.where(xi == xo + (kx - 1), tap, plain)
                 mirror = jnp.where(xi == (32 - kx) - xo, tap, mirror)
-            at = ky * 128 + kz * 32
-            b_rest[at : at + 32, :256] = plain.astype(BF)
-            b_rest[at : at + 32, 256:512] = mirror.astype(BF)
-        b_rest[ky * 128 + 96 : ky * 128 + 128, :512] = jnp.zeros((32, 512), BF)
+            at = kz * 32
+            b_rest[ky, at : at + 32, :256] = plain.astype(BF)
+            b_rest[ky, at : at + 32, 256:512] = mirror.astype(BF)
+        b_rest[ky, 96:128, :512] = jnp.zeros((32, 512), BF)
     for ky in range(3):
         for kz in range(3):
             for w, b_ref, at, blocks in (
                 (w_mid, b_mid.at[ky], kz * 256, 2),
-                (w_low, b_rest.at[ky * 128 : ky * 128 + 128], 512 + kz * 128, 1),
+                (w_low, b_rest.at[ky], 512 + kz * 128, 1),
                 (w_skip, b_up.at[ky], kz * 256, 2),
             ):
-                taps = [stacked(w, (kx * 3 + ky) * 3 + kz, 8) for kx in range(3)]
+                taps = [stacked(w[kx * 3 + ky], kz, 8) for kx in range(3)]
                 same_level(b_ref, (), at, blocks, taps, 8)
-            taps = [stacked(w_rise, (kx * 3 + ky) * 3 + kz, 8) for kx in range(3)]
+            taps = [stacked(w_rise[kx * 3 + ky], kz, 8) for kx in range(3)]
             from_coarse(b_up, (ky,), 768 + kz * 128, 2, 1, taps, 8)
-    w_out = edge[144:152].astype(BF)
+    w_out = edge[0][8:16].astype(BF)
     row_r = iota((128, 256), 0)
     cell = iota((128, 256), 1) // 8
     pick = (iota((128, 8), 1) == (iota((128, 8), 0) // 4) % 4 + 4 * lax.axis_index("rep"))
     w_rows = nn(pick.astype(F32).astype(BF), w_out)
     x_row = (row_r // 16) * 4 + row_r % 4
-    b_rest[:128, 896:] = jnp.where(cell == x_row, w_rows, 0.0).astype(BF)
-    b_rest[128:256, 896:] = jnp.where(31 - cell == x_row, w_rows, 0.0).astype(BF)
+    b_rest[0, :, 896:] = jnp.where(cell == x_row, w_rows, 0.0).astype(BF)
+    b_rest[1, :, 896:] = jnp.where(31 - cell == x_row, w_rows, 0.0).astype(BF)
 
 
 def segment_kernel(v_ref, b_rest, b_mid, b_up, out_ref, vz, vl, h1l, pool, ql, rise, l4):
@@ -273,7 +270,7 @@
     for step in range(3):
         y0 = step * part
         n = part * 32
-        h1 = nn(vl[y0 : y0 + part].reshape(n, 384), b_rest[:, :512])
+        h1 = nn(vl[y0 : y0 + part].reshape(n, 384), b_rest[:, :, :512].reshape(384, 512))
         mask = inside(part, y_base - 5 + y0, 32, z_base, 256)
         for copy in range(2):
             h = masked(h1[:, copy * 256 : (copy + 1) * 256], mask)
@@ -308,7 +305,7 @@
             ql[:, :, kz * 128 : (kz + 1) * 128] = moved.astype(BF).reshape(20, 16, 128)
         acc = jnp.zeros((288, 128), F32)
         for ky in range(3):
-            acc = acc + nt(ql[ky : ky + 18].reshape(288, 384), b_rest[ky * 128 : ky * 128 + 128, 512:896])
+            acc = acc + nt(ql[ky : ky + 18].reshape(288, 384), b_rest[ky, :, 512:896])
         h3 = masked(
             acc, inside(18, 16 * at_z - 1, 16, 64 * at_c + 8 * at_i - 4, 128)
         )
@@ -323,7 +320,7 @@
         for ky in range(3):
             acc = acc + nt(l4[copy, ky : ky + 32].reshape(512, 1152), b_up[ky])
         h4 = jnp.maximum(acc, 0.0).astype(BF)
-        logits = logits + nt(b_rest[copy * 128 : copy * 128 + 128, 896:], h4)
+        logits = logits + nt(b_rest[copy, :, 896:], h4)
     out_ref[...] = (0.5 * logits).astype(BF).reshape(NI, 16, 512)
 
 
@@ -358,52 +355,51 @@
     return jax.ShapeDtypeStruct(shape, BF)
 
 
-def flat2(w):
-    return w.transpose(2, 3, 0, 1).reshape(-1, w.shape[1])
-
-
-def table(rows, width, *weights):
-    total, at = None, 0
-    for w in weights:
-        n = w.shape[0]
-        filled = jnp.pad(w, ((at, rows - at - n), (0, width - w.shape[1])))
-        total = filled if total is None else total + filled
-        at += n
+def table(lead, rows, width, *weights):
+    total = 0
+    for at, w in weights:
+        size = w.shape
+        total = total + jnp.pad(
+            w, ((0, lead - size[0]), (at, rows - at - size[1]), (0, width - size[2]))
+        )
     return total
 
 
-def flat3(w):
-    return w.transpose(2, 3, 4, 0, 1).reshape(-1, w.shape[1])
+def taps2(w):
+    return w.transpose(2, 3, 0, 1).reshape(3, -1, w.shape[1])
+
+
+def taps3(w):
+    return w.transpose(2, 3, 4, 0, 1).reshape(9, -1, w.shape[1])
 
 
 def rim_pairs():
-    pairs = []
-
     def index(i, z, c):
         return (i * NZ + z) * NC + c
 
-    for c in range(NC):
-        for z in range(NZ):
-            for i in range(NI):
-                if z >= 5:
-                    if i < NI - 1:
-                        pairs.append((index(i, z, c), index(i + 1, z, c)))
-                    elif c == 0:
-                        pairs.append((index(i, z, 0), index(0, z, 1)))
-                if z <= 2:
-                    if i > 0:
-                        pairs.append((index(i, z, c), index(i - 1, z, c)))
-                    elif c == 1:
-                        pairs.append((index(i, z, 1), index(NI - 1, z, 0)))
+    pairs = []
+    for z in range(NZ):
+        if z >= NZ - 3:
+            step, edge, wrapped = 1, NI - 1, 0
+        elif z <= 2:
+            step, edge, wrapped = -1, 0, 1
+        else:
+            continue
+        for i in range(NI):
+            for c in range(NC):
+                if i != edge:
+                    pairs.append((index(i, z, c), index(i + step, z, c)))
+                elif c == wrapped:
+                    pairs.append((index(i, z, c), index((i + step) % NI, z, 1 - c)))
     return pairs
 
 
-def denoise(first_plane, planes, before, *weights):
-    count = planes.shape[0]
-    args = (planes,) if before is None else (planes, before)
+def denoise(rim, planes, before, weights):
+    args = (planes, before) if rim else (planes,)
+    count = 2
     vmem = pltpu.VMEM
     return call(
-        functools.partial(denoise_kernel, first_plane, before is not None),
+        functools.partial(denoise_kernel, rim),
         bf(NZ, 48, 128),
         [
             vmem((count * 256, 1536), BF),
@@ -422,12 +418,11 @@
 def per_device(
     noisy, w2_in, w2_mid, w2_low, w2_deep, w2_up, w2_out, w3_in, w3_mid, w3_low, w3_up, w3_out
 ):
-    second = lax.axis_index("c") == 1
-    low_half, high_half = noisy[0, 0], noisy[1, 0]
-    sent = jnp.where(second, low_half, high_half)
-    got = lax.ppermute(sent, "c", [(0, 1), (1, 0)])
-    w_in = jnp.pad(w2_in.transpose(1, 2, 3, 0)[0], ((0, 0), (0, 13), (0, 0))).reshape(48, 16)
-    taps = (flat2(w2_mid), flat2(w2_low), flat2(w2_deep), flat2(w2_up), w_in, w2_out)
+    near = noisy.reshape(2, 32, 256)
+    far = lax.ppermute(near, "c", [(0, 1), (1, 0)])
+    kernels = ((0, w2_mid), (48, w2_low), (96, w2_deep), (144, w2_up))
+    taps = [(at, taps2(w)) for at, w in kernels]
+    taps += [(192, w2_in.transpose(1, 2, 3, 0)[0]), (195, w2_out[None])]
     weights = call(
         plane_weights_kernel,
         [
@@ -441,22 +436,18 @@
         ],
         [],
         16,
-        table(640, 32, *taps),
-    )
-    own = jnp.stack([jnp.where(second, got, low_half), jnp.where(second, high_half, got)])
+        table(3, 208, 32, *taps),
+    )
+    second = lax.axis_index("c") == 1
+    own = jnp.stack([jnp.where(second, far[1], near[0]), jnp.where(second, near[1], far[0])])
     rim = lax.ppermute(own, ("i", "z", "c"), rim_pairs())
-    volume = denoise(0, own, None, *weights)
-    volume = denoise(2, rim, volume, *weights)
+    volume = denoise(0, own, None, weights)
+    volume = denoise(1, rim, volume, weights)
+    taps = [(at, taps3(w)) for at, w in ((0, w3_mid), (24, w3_low), (48, w3_up))]
+    taps += [(72, w3_in.transpose(1, 2, 3, 4, 0).reshape(9, 3, 8)), (80, w3_out[None])]
+    bands = call(volume_weights_kernel, [bf(3, 128, 1152), bf(3, 256, 768), bf(3, 256, 1152)], [], 16, table(9, 88, 16, *taps))
+    volume, bands = lax.optimization_barrier((volume, bands))
     window = lax.all_to_all(volume, "z", 0, 0, tiled=True)
-    w_in = jnp.pad(w3_in.transpose(1, 2, 3, 4, 0)[0], ((0, 0), (0, 0), (0, 13), (0, 0)))
-    taps = (flat3(w3_mid), flat3(w3_low), flat3(w3_up), w_in.reshape(144, 8), w3_out)
-    volume_weights = call(
-        volume_weights_kernel,
-        [bf(384, 1152), bf(3, 256, 768), bf(3, 256, 1152)],
-        [],
-        16,
-        table(800, 16, *taps),
-    )
     vmem = pltpu.VMEM
     logits = call(
         segment_kernel,
@@ -472,7 +463,7 @@
         ],
         24,
         window,
-        *volume_weights,
+        *bands,
     )
     parts = lax.all_to_all(logits, "i", 0, 0, tiled=True)
     out = call(arrange_kernel, jax.ShapeDtypeStruct((512, 128), F32), [], 4, parts)

time: 57.7 us -> 56.2 us (0.974)
  blocking collectives: 11.3 us -> 29.8 us
  starting transfers between devices: 11.2 us -> 1.29 us
  waiting for transfers between devices: 6.86 us -> 0.47 us
  local copies, waits for them, and re-layouts: 2.81 us -> 0 us
  Pallas kernels: 22.3 us -> 21.7 us
    all_to_all x0 -> x1, blocking collectives: none -> 18.5 us  [per_device(): window = lax.all_to_all(volume, 'z', 0, 0, tiled=True)]
    all_to_all x1 -> x0, starting transfers between devices: 9.92 us -> none  [per_device(): window = lax.all_to_all(volume, 'z', 0, 0, tiled=True)]
    all_to_all x1 -> x0, waiting for transfers between devices: 6.36 us -> none  [per_device(): window = lax.all_to_all(volume, 'z', 0, 0, tiled=True)]
    unnamed x14 -> x0, local copies, waits for them, and re-layouts: 2.11 us -> none
    add x2, other arithmetic: 0.92 us -> 1.84 us  [table(): total + jnp.pad(w, ((0, lead - size[0]), (at, rows - at - size[1]), (0, w...]
    another operation x2 -> x1, other arithmetic: 0.75 us -> 0.01 us  [per_device(): jnp.stack([jnp.where(second, far[1], near[0]), jnp.where(second, near[1],...]
    pad x2 -> x0, local copies, waits for them, and re-layouts: 0.7 us -> none  [the longest x1 0.69 us: per_device(): jnp.pad(w2_in.transpose(1, 2, 3, 0)[0], ((0, 0), (0, 13), (0, 0)))]
    pallas_call x6, Pallas kernels: 22.3 us -> 21.7 us  [call(): pl.pallas_call(kernel, out_shape=out_shape, in_specs=[spec] * len(args),...]
  transfers between devices with their start and end apart: 3 -> 2, of which waited for: 2 -> 1; matrix products, arithmetic and copies ran while one was open for 3% -> 3% of each run, Pallas kernels for 11% -> 12%
where the time goes in v2:
time: 56.2 us; the launch traced here: 55.9 us
  blocking collectives  29.8 us (53%)
  Pallas kernels  21.7 us (39%)
  other arithmetic  2.59 us (5%)
  starting transfers between devices  1.29 us (2%)
    pallas_call x6, Pallas kernels, call(): pl.pallas_call(kernel, out_shape=out_shape, in_specs=[spec] * len(args),...  21.7 us
    all_to_all x1, blocking collectives, per_device(): window = lax.all_to_all(volume, 'z', 0, 0, tiled=True)  18.5 us
    all_to_all x1, blocking collectives, per_device(): parts = lax.all_to_all(logits, 'i', 0, 0, tiled=True)  11.3 us
    add x2, other arithmetic, table(): total + jnp.pad(w, ((0, lead - size[0]), (at, rows - at - size[1]), (0, w...  1.84 us
    ppermute x1, starting transfers between devices, per_device(): rim = lax.ppermute(own, ('i', 'z', 'c'), rim_pairs())  1.29 us
  transfers between devices with their start and end apart: 2, of which 1 were waited for; matrix products, arithmetic and copies ran while one was open for 3% of the time, Pallas kernels for 12%

profile of v2, /device:TPU:16, one launch (start us, length us, event | category | flops | bytes accessed | tf_op | source)
XLA Modules:
  0.0 55.9 jit_solution(6077616592551555282)
XLA Ops:
  0.0 0.0 collective-permute-start
  0.0 0.9 %pad_add_fusion.w_ref = bf16[9,88,16]{2,1,0:T(8,128)(2,1)S(1)} fusion(bf16[1,8,8]{2,1,0:T(8,128)(2,1)} %bitcast.45, bf16[9,3,8]{2,1,0:T(4,128)(2,1)} %bitcast.43, bf16[9,24,16]{2,1,0:T(8,128)(2,1)} %bitcast.35, bf16[9,24,8]{2,1,0:T(8,128)(2,1)} %bitcast.36, bf16[9,24,8]{2,1,0:T(8,128)(2,1)} %bitcast.37), kind=kLoop, calls=%fused_computation | loop fusion | flops 126720 | bytes 39728 | tf_op jit(solution)/shard_map/add | solution.py:362
  1.0 0.5 collective-permute-done
  1.4 0.7 %slice_select_fusion.1 = (bf16[1,32,256]{2,1,0:T(8,128)(2,1)S(1)}, bf16[1,32,256]{2,1,0:T(8,128)(2,1)S(1)}) fusion(bf16[2,32,256]{2,1,0:T(8,128)(2,1)S(1)} %collective-permute-done, bf16[2,1,32,256]{3,2,1,0:T(8,128)(2,1)} %param.12, pred[]{:T(512)S(6)} %eq.3), kind=kLoop, calls=%fused_computation.4 | loop fusion | flops 16384 | bytes 98305 | tf_op jit(solution)/shard_map/jit(_where)/select_n | solution.py:442
  2.2 1.3 %collective-permute-start.1 = (bf16[2,32,256]{2,1,0:T(8,128)(2,1)S(1)}, bf16[2,32,256]{2,1,0:T(8,128)(2,1)S(1)}, u32[]{:S(2)}, u32[]{:S(2)}) collective-permute-start(bf16[2,32,256]{2,1,0:T(8,128)(2,1)S(1)} %pad_maximum_fusion.planes_ref), channel_id=1, source_target_pairs={{1,112},{16,0},{17,1},{32,16},{33,17},{48,32},{49,33},{64,48},{65,... | collective-permute-start | bytes 98312 | tf_op jit(solution)/shard_map/ppermute | solution.py:443
  3.5 0.9 %pad_add_fusion.1.w_ref = bf16[3,208,32]{2,1,0:T(8,128)(2,1)S(1)} fusion(bf16[1,1,16]{2,1,0:T(2,128)(2,1)} %bitcast.46, bf16[3,3,16]{2,1,0:T(4,128)(2,1)} %bitcast.44, bf16[3,48,32]{2,1,0:T(8,128)(2,1)} %bitcast.38, bf16[3,48,16]{2,1,0:T(8,128)(2,1)} %bitcast.39, bf16[3,48,16]{2,1,0:T(8,128)(2,1)} %bitcast.40, bf16[3,48,16]{2,1,0:T(8,128)(2,1)} %bitcast.41), kind=kLoop, calls=%fused_computation.1 | loop fusion | flops 239616 | bytes 63296 | tf_op jit(solution)/shard_map/add | solution.py:362
  4.4 1.5 %shard_map.118 = (bf16[128,512]{1,0:T(8,128)(2,1)S(1)}, bf16[512,1536]{1,0:T(8,128)(2,1)S(1)}, bf16[256,768]{1,0:T(8,128)(2,1)S(1)}, bf16[256,768]{1,0:T(8,128)(...) custom-call(bf16[3,208,32]{2,1,0:T(8,128)(2,1)S(1)} %pad_add_fusion.1.w_ref), custom_call_target="tpu_custom_call" | custom-call | tf_op jit(solution)/shard_map/pallas_call | solution.py:344
  5.8 1.3 %shard_map.121 = (bf16[3,128,1152]{2,1,0:T(8,128)(2,1)S(1)}, bf16[3,256,768]{2,1,0:T(8,128)(2,1)S(1)}, bf16[3,256,1152]{2,1,0:T(8,128)(2,1)S(1)}) custom-call(bf16[9,88,16]{2,1,0:T(8,128)(2,1)S(1)} %pad_add_fusion.w_ref), custom_call_target="tpu_custom_call" | custom-call | tf_op jit(solution)/shard_map/pallas_call | solution.py:344
  7.2 3.7 %shard_map.119.refs_0_ = bf16[8,48,128]{2,1,0:T(8,128)(2,1)S(1)} custom-call(bf16[2,32,256]{2,1,0:T(8,128)(2,1)S(1)} %pad_maximum_fusion.planes_ref, bf16[128,512]{1,0:T(8,128)(2,1)S(1)} %get-tuple-element.19.refs_0_.refs_1_, bf16[512,1536]{1,0:T(8,128)(2,1)S(1)} %get-tuple-element.20.refs_1_.refs_2_, ...), custom_call_target="tpu_custom_call" | custom-call | tf_op jit(solution)/shard_map/pallas_call | solution.py:344
  10.9 0.0 collective-permute-done.1.planes_ref
  10.9 3.7 %shard_map.120 = bf16[8,48,128]{2,1,0:T(8,128)(2,1)S(1)} custom-call(bf16[2,32,256]{2,1,0:T(8,128)(2,1)S(1)} %collective-permute-done.1.planes_ref, bf16[8,48,128]{2,1,0:T(8,128)(2,1)S(1)} %shard_map.119.refs_0_, bf16[128,512]{1,0:T(8,128)(2,1)S(1)} %get-tuple-element.19.refs_0_.refs_1_, bf16[512,1536]{1,0:T(8,128)(2,1)S(1)} %get-tuple-element.20.refs_1_.refs_2_, ...), custom_call_target="tpu_custom_call" | custom-call | tf_op jit(solution)/shard_map/pallas_call | solution.py:344
  14.7 18.5 %all_to_all.10.v_ref = bf16[8,48,128]{2,1,0:T(8,128)(2,1)S(1)} all-to-all(bf16[8,48,128]{2,1,0:T(8,128)(2,1)S(1)} %shard_map.120), channel_id=1, replica_groups=mesh['rep'=2,'i'=8,'z'=8,'c'=2] {'z'}, dimensions={0} | all-to-all | bytes 196608 | tf_op jit(solution)/shard_map/all_to_all | solution.py:450
  33.1 10.3 %shard_map.122 = bf16[8,16,512]{2,1,0:T(8,128)(2,1)S(1)} custom-call(bf16[8,48,128]{2,1,0:T(8,128)(2,1)S(1)} %all_to_all.10.v_ref, bf16[3,128,1152]{2,1,0:T(8,128)(2,1)S(1)} %get-tuple-element.30.b_rest, bf16[3,256,768]{2,1,0:T(8,128)(2,1)S(1)} %get-tuple-element.31.b_mid, bf16[3,256,1152]{2,1,0:T(8,128)(2,1)S(1)} %get-tuple-element.32.b_up), custom_call_target="tpu_custom_call" | custom-call | tf_op jit(solution)/shard_map/pallas_call | solution.py:344
  43.4 11.3 %all_to_all.11.parts_ref = bf16[8,16,512]{2,1,0:T(8,128)(2,1)S(1)} all-to-all(bf16[8,16,512]{2,1,0:T(8,128)(2,1)S(1)} %shard_map.122), channel_id=1, replica_groups=mesh['rep'=2,'i'=8,'z'=8,'c'=2] {'i'}, dimensions={0} | all-to-all | bytes 262144 | tf_op jit(solution)/shard_map/all_to_all | solution.py:468
  54.7 1.1 %shard_map.123 = f32[512,128]{1,0:T(8,128)} custom-call(bf16[8,16,512]{2,1,0:T(8,128)(2,1)S(1)} %all_to_all.11.parts_ref), custom_call_target="tpu_custom_call" | custom-call | tf_op jit(solution)/shard_map/pallas_call | solution.py:344
  (1 shorter events, 0.0 us)
Async XLA Ops:
  0.0 1.4 %collective-permute-start = (bf16[2,32,256]{2,1,0:T(8,128)(2,1)}, bf16[2,32,256]{2,1,0:T(8,128)(2,1)S(1)}, u32[]{:S(2)}, u32[]{:S(2)}) collective-permute-start(bf16[2,32,256]{2,1,0:T(8,128)(2,1)} %bitcast.42), channel_id=1, source_target_pairs={{0,1},{1,0},{2,3},{3,2},{4,5},{5,4},{6,7},{7,6},{8,9},{9,8},{10,11... | collective-permute-start | bytes 98312 | tf_op jit(solution)/shard_map/ppermute | solution.py:422
  2.2 8.7 %collective-permute-start.1 = (bf16[2,32,256]{2,1,0:T(8,128)(2,1)S(1)}, bf16[2,32,256]{2,1,0:T(8,128)(2,1)S(1)}, u32[]{:S(2)}, u32[]{:S(2)}) collective-permute-start(bf16[2,32,256]{2,1,0:T(8,128)(2,1)S(1)} %pad_maximum_fusion.planes_ref), channel_id=1, source_target_pairs={{1,112},{16,0},{17,1},{32,16},{33,17},{48,32},{49,33},{64,48},{65,... | collective-permute-start | bytes 98312 | tf_op jit(solution)/shard_map/ppermute | solution.py:443

commit v3 on v2

--- a/solution.py
+++ b/solution.py
@@ -35,16 +35,20 @@
     return jnp.concatenate([taps[at * channels : (at + 1) * channels]] * (128 // channels), axis=0)
 
 
-def same_level(ref, lead, at, blocks, taps, channels):
+def band_parts(taps, channels):
     cells = 128 // channels
     gap = iota((128, 128), 1) // channels - iota((128, 128), 0) // channels
     zero = jnp.zeros((128, 128), F32)
     own = jnp.where(
         gap == 0, taps[1], jnp.where(gap == -1, taps[0], jnp.where(gap == 1, taps[2], zero))
-    ).astype(BF)
-    if blocks > 1:
-        later = jnp.where(gap == 1 - cells, taps[2], zero).astype(BF)
-        earlier = jnp.where(gap == cells - 1, taps[0], zero).astype(BF)
+    )
+    later = jnp.where(gap == 1 - cells, taps[2], zero)
+    earlier = jnp.where(gap == cells - 1, taps[0], zero)
+    return [part.astype(BF) for part in (own, later, earlier)]
+
+
+def same_level(ref, at, blocks, taps, channels):
+    own, later, earlier = band_parts(taps, channels)
     for out in range(blocks):
         for inp in range(blocks):
             if inp == out:
@@ -55,7 +59,16 @@
                 block = earlier
             else:
                 block = jnp.zeros((128, 128), BF)
-            ref[lead + (pl.ds(out * 128, 128), pl.ds(at + inp * 128, 128))] = block
+            ref[out * 128 : (out + 1) * 128, at + inp * 128 : at + (inp + 1) * 128] = block
+
+
+def two_blocks(ref, ky):
+    parts = [ref[ky, :, at * 128 : (at + 1) * 128] for at in range(9)]
+    rows = [[], []]
+    for own, later, earlier in (parts[0:3], parts[3:6], parts[6:9]):
+        rows[0] += [own, later]
+        rows[1] += [earlier, own]
+    return jnp.concatenate([jnp.concatenate(row, axis=1) for row in rows], axis=0)
 
 
 def from_coarse(ref, lead, at, out_blocks, in_blocks, taps, channels):
@@ -101,12 +114,12 @@
         w = [nn(w_ref[kx, at : at + 48], spread) for kx in range(3)]
         for ky in range(3):
             taps = [stacked(w[kx], ky, 16) for kx in range(3)]
-            same_level(b_ref, (), ky * blocks * 128, blocks, taps, 16)
+            same_level(b_ref, ky * blocks * 128, blocks, taps, 16)
     w_skip = [nn(w_ref[kx, 144:192], spread) for kx in range(3)]
     w_rise = [nn(w_ref[kx, 144:192], lane_spread(32, 16, 16, 128)) for kx in range(3)]
     for ky in range(3):
         taps = [stacked(w_skip[kx], ky, 16) for kx in range(3)]
-        same_level(b_up, (), ky * 512, 4, taps, 16)
+        same_level(b_up, ky * 512, 4, taps, 16)
         taps = [stacked(w_rise[kx], ky, 16) for kx in range(3)]
         from_coarse(b_up, (), 1536 + ky * 256, 4, 2, taps, 16)
     none = jnp.zeros((128, 128), BF)
@@ -181,7 +194,7 @@
         out_ref[z] = window.astype(BF)
 
 
-def volume_weights_kernel(w_ref, b_rest, b_mid, b_up):
+def volume_weights_kernel(w_ref, b_rest, b_mid, b_skip, b_rise):
     edge = [nn(w_ref[kxy, 72:88], lane_spread(16, 8, 0, 256)) for kxy in range(9)]
     spread = lane_spread(16, 8, 0, 128)
     w_mid, w_low, w_skip = (
@@ -204,15 +217,15 @@
         b_rest[ky, 96:128, :512] = jnp.zeros((32, 512), BF)
     for ky in range(3):
         for kz in range(3):
-            for w, b_ref, at, blocks in (
-                (w_mid, b_mid.at[ky], kz * 256, 2),
-                (w_low, b_rest.at[ky], 512 + kz * 128, 1),
-                (w_skip, b_up.at[ky], kz * 256, 2),
-            ):
+            for w, b_ref in ((w_mid, b_mid), (w_skip, b_skip)):
                 taps = [stacked(w[kx * 3 + ky], kz, 8) for kx in range(3)]
-                same_level(b_ref, (), at, blocks, taps, 8)
+                for side, part in enumerate(band_parts(taps, 8)):
+                    at = (kz * 3 + side) * 128
+                    b_ref[ky, :, at : at + 128] = part
+            taps = [stacked(w_low[kx * 3 + ky], kz, 8) for kx in range(3)]
+            same_level(b_rest.at[ky], 512 + kz * 128, 1, taps, 8)
             taps = [stacked(w_rise[kx * 3 + ky], kz, 8) for kx in range(3)]
-            from_coarse(b_up, (ky,), 768 + kz * 128, 2, 1, taps, 8)
+            from_coarse(b_rise, (ky,), kz * 128, 2, 1, taps, 8)
     w_out = edge[0][8:16].astype(BF)
     row_r = iota((128, 256), 0)
     cell = iota((128, 256), 1) // 8
@@ -223,7 +236,7 @@
     b_rest[1, :, 896:] = jnp.where(31 - cell == x_row, w_rows, 0.0).astype(BF)
 
 
-def segment_kernel(v_ref, b_rest, b_mid, b_up, out_ref, vz, vl, h1l, pool, ql, rise, l4):
+def segment_kernel(v_ref, b_rest, b_mid, b_skip, b_rise, out_ref, vz, vl, h1l, pool, ql, rise, l4):
     at_i, at_z, at_c = (lax.axis_index(name) for name in ("i", "z", "c"))
     out_lane = iota((128, 512), 1)
     select = (
@@ -289,7 +302,9 @@
             y0 = step * part
             acc = jnp.zeros((n, 256), F32)
             for ky in range(3):
-                acc = acc + nt(h1l[copy, y0 + ky : y0 + ky + part].reshape(n, 768), b_mid[ky])
+                acc = acc + nt(
+                    h1l[copy, y0 + ky : y0 + ky + part].reshape(n, 768), two_blocks(b_mid, ky)
+                )
             h2 = masked(acc, inside(part, y_base - 4 + y0, 32, z_base, 256))
             fine = nt(h2.astype(BF), pool_t).reshape(part // 2, 2, 32, 128)
             pool[y0 * 16 : y0 * 16 + n // 2] = (fine[:, 0] + fine[:, 1]).reshape(n // 2, 128)
@@ -318,7 +333,8 @@
                 l4[copy, slot, :, 768 + kz * 128 : 896 + kz * 128] = moved[(slot + 3) // 2 - 1]
         acc = jnp.zeros((512, 256), F32)
         for ky in range(3):
-            acc = acc + nt(l4[copy, ky : ky + 32].reshape(512, 1152), b_up[ky])
+            bands = jnp.concatenate([two_blocks(b_skip, ky), b_rise[ky]], axis=1)
+            acc = acc + nt(l4[copy, ky : ky + 32].reshape(512, 1152), bands)
         h4 = jnp.maximum(acc, 0.0).astype(BF)
         logits = logits + nt(b_rest[copy, :, 896:], h4)
     out_ref[...] = (0.5 * logits).astype(BF).reshape(NI, 16, 512)
@@ -445,8 +461,7 @@
     volume = denoise(1, rim, volume, weights)
     taps = [(at, taps3(w)) for at, w in ((0, w3_mid), (24, w3_low), (48, w3_up))]
     taps += [(72, w3_in.transpose(1, 2, 3, 4, 0).reshape(9, 3, 8)), (80, w3_out[None])]
-    bands = call(volume_weights_kernel, [bf(3, 128, 1152), bf(3, 256, 768), bf(3, 256, 1152)], [], 16, table(9, 88, 16, *taps))
-    volume, bands = lax.optimization_barrier((volume, bands))
+    bands = call(volume_weights_kernel, [bf(3, 128, 1152), bf(3, 128, 1152), bf(3, 128, 1152), bf(3, 256, 384)], [], 16, table(9, 88, 16, *taps))
     window = lax.all_to_all(volume, "z", 0, 0, tiled=True)
     vmem = pltpu.VMEM
     logits = call(

time: 56.2 us -> 55.9 us (level)
  blocking collectives: 29.8 us -> 11.3 us
  starting transfers between devices: 1.29 us -> 11.2 us
  waiting for transfers between devices: 0.47 us -> 8.75 us
  other arithmetic: 2.59 us -> 1.69 us
  Pallas kernels: 21.7 us -> 22.3 us
    all_to_all x1 -> x0, blocking collectives: 18.5 us -> none  [per_device(): window = lax.all_to_all(volume, 'z', 0, 0, tiled=True)]
    all_to_all x0 -> x1, starting transfers between devices: none -> 9.92 us  [per_device(): window = lax.all_to_all(volume, 'z', 0, 0, tiled=True)]
    all_to_all x0 -> x1, waiting for transfers between devices: none -> 7.33 us  [per_device(): window = lax.all_to_all(volume, 'z', 0, 0, tiled=True)]
    ppermute x1, waiting for transfers between devices: 0.47 us -> 1.42 us  [per_device(): far = lax.ppermute(near, 'c', [(0, 1), (1, 0)])]
    add x2, other arithmetic: 1.84 us -> 0.94 us  [table(): total + jnp.pad(w, ((0, lead - size[0]), (at, rows - at - size[1]), (0, w...]
    pallas_call x6, Pallas kernels: 21.7 us -> 22.3 us  [call(): pl.pallas_call(kernel, out_shape=out_shape, in_specs=[spec] * len(args),...]
  transfers between devices with their start and end apart: 2 -> 3, of which waited for: 1 -> 2; matrix products, arithmetic and copies ran while one was open for 3% -> 2% of each run, Pallas kernels for 12% -> 12%
where the time goes in v3:
time: 55.9 us; the launch traced here: 55.4 us
  Pallas kernels  22.3 us (40%)
  blocking collectives  11.3 us (20%)
  starting transfers between devices  11.2 us (20%)
  waiting for transfers between devices  8.75 us (16%)
  other arithmetic  1.69 us (3%)
    pallas_call x6, Pallas kernels, call(): pl.pallas_call(kernel, out_shape=out_shape, in_specs=[spec] * len(args),...  22.3 us
    all_to_all x1, blocking collectives, per_device(): parts = lax.all_to_all(logits, 'i', 0, 0, tiled=True)  11.3 us
    all_to_all x1, starting transfers between devices, per_device(): window = lax.all_to_all(volume, 'z', 0, 0, tiled=True)  9.92 us
    all_to_all x1, waiting for transfers between devices, per_device(): window = lax.all_to_all(volume, 'z', 0, 0, tiled=True)  7.33 us
    ppermute x1, waiting for transfers between devices, per_device(): far = lax.ppermute(near, 'c', [(0, 1), (1, 0)])  1.42 us
    ppermute x1, starting transfers between devices, per_device(): rim = lax.ppermute(own, ('i', 'z', 'c'), rim_pairs())  1.29 us
  transfers between devices with their start and end apart: 3, of which 2 were waited for; matrix products, arithmetic and copies ran while one was open for 2% of the time, Pallas kernels for 12%

profile of v3, /device:TPU:16, one launch (start us, length us, event | category | flops | bytes accessed | tf_op | source)
XLA Modules:
  0.0 55.4 jit_solution(5801003831515246491)
XLA Ops:
  0.0 0.0 collective-permute-start
  0.0 1.4 %collective-permute-done = bf16[2,32,256]{2,1,0:T(8,128)(2,1)S(1)} collective-permute-done((bf16[2,32,256]{2,1,0:T(8,128)(2,1)}, bf16[2,32,256]{2,1,0:T(8,128)(2,1)S(1)}, u32[]{:S(2)}, u32[]{:S(2)}) %collective-permute-start) | collective-permute-done | bytes 32800 | tf_op jit(solution)/shard_map/ppermute | solution.py:438
  1.4 0.7 %slice_select_fusion.1 = (bf16[1,32,256]{2,1,0:T(8,128)(2,1)S(1)}, bf16[1,32,256]{2,1,0:T(8,128)(2,1)S(1)}) fusion(bf16[2,32,256]{2,1,0:T(8,128)(2,1)S(1)} %collective-permute-done, bf16[2,1,32,256]{3,2,1,0:T(8,128)(2,1)} %param.12, pred[]{:T(512)S(6)} %eq.3), kind=kLoop, calls=%fused_computation.4 | loop fusion | flops 16384 | bytes 98305 | tf_op jit(solution)/shard_map/jit(_where)/select_n | solution.py:458
  2.2 1.3 %collective-permute-start.1 = (bf16[2,32,256]{2,1,0:T(8,128)(2,1)S(1)}, bf16[2,32,256]{2,1,0:T(8,128)(2,1)S(1)}, u32[]{:S(2)}, u32[]{:S(2)}) collective-permute-start(bf16[2,32,256]{2,1,0:T(8,128)(2,1)S(1)} %pad_maximum_fusion.planes_ref), channel_id=1, source_target_pairs={{1,112},{16,0},{17,1},{32,16},{33,17},{48,32},{49,33},{64,48},{65,... | collective-permute-start | bytes 98312 | tf_op jit(solution)/shard_map/ppermute | solution.py:459
  3.5 0.9 %pad_add_fusion.1.w_ref = bf16[3,208,32]{2,1,0:T(8,128)(2,1)S(1)} fusion(bf16[1,1,16]{2,1,0:T(2,128)(2,1)} %bitcast.46, bf16[3,3,16]{2,1,0:T(4,128)(2,1)} %bitcast.44, bf16[3,48,32]{2,1,0:T(8,128)(2,1)} %bitcast.38, bf16[3,48,16]{2,1,0:T(8,128)(2,1)} %bitcast.39, bf16[3,48,16]{2,1,0:T(8,128)(2,1)} %bitcast.40, bf16[3,48,16]{2,1,0:T(8,128)(2,1)} %bitcast.41), kind=kLoop, calls=%fused_computation.1 | loop fusion | flops 239616 | bytes 63296 | tf_op jit(solution)/shard_map/add | solution.py:378
  4.4 1.5 %shard_map.118 = (bf16[128,512]{1,0:T(8,128)(2,1)S(1)}, bf16[512,1536]{1,0:T(8,128)(2,1)S(1)}, bf16[256,768]{1,0:T(8,128)(2,1)S(1)}, bf16[256,768]{1,0:T(8,128)(...) custom-call(bf16[3,208,32]{2,1,0:T(8,128)(2,1)S(1)} %pad_add_fusion.1.w_ref), custom_call_target="tpu_custom_call" | custom-call | tf_op jit(solution)/shard_map/pallas_call | solution.py:360
  5.8 3.7 %shard_map.119.refs_0_ = bf16[8,48,128]{2,1,0:T(8,128)(2,1)S(1)} custom-call(bf16[2,32,256]{2,1,0:T(8,128)(2,1)S(1)} %pad_maximum_fusion.planes_ref, bf16[128,512]{1,0:T(8,128)(2,1)S(1)} %get-tuple-element.16.refs_0_.refs_1_, bf16[512,1536]{1,0:T(8,128)(2,1)S(1)} %get-tuple-element.17.refs_1_.refs_2_, ...), custom_call_target="tpu_custom_call" | custom-call | tf_op jit(solution)/shard_map/pallas_call | solution.py:360
  9.6 0.0 copy-start
  9.6 0.0 copy-start.1
  9.6 0.0 copy-start.2
  9.6 0.0 copy-start.3
  9.6 0.0 copy-start.4
  9.6 0.0 collective-permute-done.1.planes_ref
  9.6 4.4 %shard_map.120 = bf16[8,48,128]{2,1,0:T(8,128)(2,1)} custom-call(bf16[2,32,256]{2,1,0:T(8,128)(2,1)S(1)} %collective-permute-done.1.planes_ref, bf16[8,48,128]{2,1,0:T(8,128)(2,1)S(1)} %shard_map.119.refs_0_, bf16[128,512]{1,0:T(8,128)(2,1)S(1)} %get-tuple-element.16.refs_0_.refs_1_, bf16[512,1536]{1,0:T(8,128)(2,1)S(1)} %get-tuple-element.17.refs_1_.refs_2_, ...), custom_call_target="tpu_custom_call" | custom-call | tf_op jit(solution)/shard_map/pallas_call | solution.py:360
  14.0 9.9 %all-to-all-start = ((bf16[8,48,128]{2,1,0:T(8,128)(2,1)}), bf16[8,48,128]{2,1,0:T(8,128)(2,1)S(1)}, u32[]{:S(2)}, u32[]{:S(2)}) async-start(bf16[8,48,128]{2,1,0:T(8,128)(2,1)} %shard_map.120), calls=%async_computation | async-start | bytes 196608 | tf_op jit(solution)/shard_map/all_to_all | solution.py:465
  23.9 0.0 copy-done
  23.9 0.0 copy-done.1
  24.0 0.0 copy-done.2
  24.0 0.0 copy-done.3
  24.0 0.0 copy-done.4
  24.0 1.3 %shard_map.121 = (bf16[3,128,1152]{2,1,0:T(8,128)(2,1)S(1)}, bf16[3,128,1152]{2,1,0:T(8,128)(2,1)S(1)}, bf16[3,128,1152]{2,1,0:T(8,128)(2,1)S(1)}, bf16[3,256,384]{2,1,0:T(8,128)(2,1)S(1)}) custom-call(bf16[9,88,16]{2,1,0:T(8,128)(2,1)S(1)} %pad_add_fusion.w_ref), custom_call_target="tpu_custom_call" | custom-call | tf_op jit(solution)/shard_map/pallas_call | solution.py:360
  25.3 7.3 %all-to-all-done.v_ref = bf16[8,48,128]{2,1,0:T(8,128)(2,1)S(1)} async-done(((bf16[8,48,128]{2,1,0:T(8,128)(2,1)}), bf16[8,48,128]{2,1,0:T(8,128)(2,1)S(1)}, u32[]{:S(2)}, u32[]{:S(2)}) %all-to-all-start) | async-done | bytes 98336 | tf_op jit(solution)/shard_map/all_to_all | solution.py:465
  32.7 10.3 %shard_map.122 = bf16[8,16,512]{2,1,0:T(8,128)(2,1)S(1)} custom-call(bf16[8,48,128]{2,1,0:T(8,128)(2,1)S(1)} %all-to-all-done.v_ref, bf16[3,128,1152]{2,1,0:T(8,128)(2,1)S(1)} %get-tuple-element.23.b_rest, bf16[3,128,1152]{2,1,0:T(8,128)(2,1)S(1)} %get-tuple-element.24.b_mid, bf16[3,128,1152]{2,1,0:T(8,128)(2,1)S(1)} %get-tuple-element.25.b_skip, ...), custom_call_target="tpu_custom_call" | custom-call | tf_op jit(solution)/shard_map/pallas_call | solution.py:360
  43.0 11.3 %all_to_all.10.parts_ref = bf16[8,16,512]{2,1,0:T(8,128)(2,1)S(1)} all-to-all(bf16[8,16,512]{2,1,0:T(8,128)(2,1)S(1)} %shard_map.122), channel_id=1, replica_groups=mesh['rep'=2,'i'=8,'z'=8,'c'=2] {'i'}, dimensions={0} | all-to-all | bytes 262144 | tf_op jit(solution)/shard_map/all_to_all | solution.py:483
  54.3 1.1 %shard_map.123 = f32[512,128]{1,0:T(8,128)} custom-call(bf16[8,16,512]{2,1,0:T(8,128)(2,1)S(1)} %all_to_all.10.parts_ref), custom_call_target="tpu_custom_call" | custom-call | tf_op jit(solution)/shard_map/pallas_call | solution.py:360
  (2 shorter events, 0.1 us)
Async XLA Ops:
  0.0 1.4 %collective-permute-start = (bf16[2,32,256]{2,1,0:T(8,128)(2,1)}, bf16[2,32,256]{2,1,0:T(8,128)(2,1)S(1)}, u32[]{:S(2)}, u32[]{:S(2)}) collective-permute-start(bf16[2,32,256]{2,1,0:T(8,128)(2,1)} %bitcast.42), channel_id=1, source_target_pairs={{0,1},{1,0},{2,3},{3,2},{4,5},{5,4},{6,7},{7,6},{8,9},{9,8},{10,11... | collective-permute-start | bytes 98312 | tf_op jit(solution)/shard_map/ppermute | solution.py:438
  2.2 7.5 %collective-permute-start.1 = (bf16[2,32,256]{2,1,0:T(8,128)(2,1)S(1)}, bf16[2,32,256]{2,1,0:T(8,128)(2,1)S(1)}, u32[]{:S(2)}, u32[]{:S(2)}) collective-permute-start(bf16[2,32,256]{2,1,0:T(8,128)(2,1)S(1)} %pad_maximum_fusion.planes_ref), channel_id=1, source_target_pairs={{1,112},{16,0},{17,1},{32,16},{33,17},{48,32},{49,33},{64,48},{65,... | collective-permute-start | bytes 98312 | tf_op jit(solution)/shard_map/ppermute | solution.py:459
  9.6 14.4 %copy-start = (bf16[8,16,3,3,3]{1,0,4,3,2:T(8,128)(2,1)S(1)}, bf16[8,16,3,3,3]{1,0,4,3,2:T(8,128)(2,1)}, u32[]{:S(2)}) copy-start(bf16[8,16,3,3,3]{1,0,4,3,2:T(8,128)(2,1)} %param.22) | copy-start | bytes 20740
  9.6 14.4 %copy-start.1 = (bf16[8,8,3,3,3]{1,0,4,3,2:T(8,128)(2,1)S(1)}, bf16[8,8,3,3,3]{1,0,4,3,2:T(8,128)(2,1)}, u32[]{:S(2)}) copy-start(bf16[8,8,3,3,3]{1,0,4,3,2:T(8,128)(2,1)} %param.21) | copy-start | bytes 10372
  9.6 14.4 %copy-start.2 = (bf16[8,8,3,3,3]{1,0,4,3,2:T(8,128)(2,1)S(1)}, bf16[8,8,3,3,3]{1,0,4,3,2:T(8,128)(2,1)}, u32[]{:S(2)}) copy-start(bf16[8,8,3,3,3]{1,0,4,3,2:T(8,128)(2,1)} %param.20) | copy-start | bytes 10372
  9.6 14.4 %copy-start.3 = (bf16[8,1,3,3,3]{0,4,3,2,1:T(4,128)(2,1)S(1)}, bf16[8,1,3,3,3]{0,4,3,2,1:T(4,128)(2,1)}, u32[]{:S(2)}) copy-start(bf16[8,1,3,3,3]{0,4,3,2,1:T(4,128)(2,1)} %param.19) | copy-start | bytes 1300
  9.6 14.4 %copy-start.4 = (bf16[8,8]{1,0:T(8,128)(2,1)S(1)}, bf16[8,8]{1,0:T(8,128)(2,1)}, u32[]{:S(2)}) copy-start(bf16[8,8]{1,0:T(8,128)(2,1)} %param.23) | copy-start | bytes 388
  14.0 18.6 %all-to-all-start = ((bf16[8,48,128]{2,1,0:T(8,128)(2,1)}), bf16[8,48,128]{2,1,0:T(8,128)(2,1)S(1)}, u32[]{:S(2)}, u32[]{:S(2)}) async-start(bf16[8,48,128]{2,1,0:T(8,128)(2,1)} %shard_map.120), calls=%async_computation | async-start | bytes 196608 | tf_op jit(solution)/shard_map/all_to_all | solution.py:465

commit v4 on v3

--- a/solution.py
+++ b/solution.py
@@ -98,36 +98,59 @@
     return pltpu.roll(v, steps % v.shape[0], 0)
 
 
+def edge_rows(w, first):
+    group = iota((16, 128), 1) // 16
+    total = jnp.zeros((16, 128), F32)
+    for ky in range(3):
+        total = jnp.where(group == first + ky, w[ky * 16 : ky * 16 + 16], total)
+    return total
+
+
 def plane_weights_kernel(w_ref, b_in, b_mid, b_low, b_deep, b_up, b_pool, b_last):
     edge = [nn(w_ref[kx, 192:208], lane_spread(32, 16, 0, 512)) for kx in range(3)]
     w_row = edge[0][3:4]
     xi = iota((32, 512), 0)
     xo = iota((32, 512), 1) // 16
+    group = iota((32, 128), 1) // 16
+    cell = jnp.where(group % 4 == 3, -9, jnp.where(group < 4, 16, 15))
     for ky in range(3):
         total = jnp.zeros((32, 512), F32)
+        extra = jnp.zeros((32, 128), F32)
         for kx in range(3):
-            total = jnp.where(xi == xo + (kx - 1), edge[kx][ky : ky + 1], total)
-        b_in[ky * 32 : (ky + 1) * 32] = total.astype(BF)
-    b_in[96:128] = jnp.zeros((32, 512), BF)
+            tap = edge[kx][ky : ky + 1]
+            total = jnp.where(xi == xo + (kx - 1), tap, total)
+            extra = jnp.where(xi[:, :128] == cell + (kx - 1), tap[:, :128], extra)
+        b_in[ky * 32 : (ky + 1) * 32, :512] = total.astype(BF)
+        b_in[ky * 32 : (ky + 1) * 32, 512:] = extra.astype(BF)
+    b_in[96:128] = jnp.zeros((32, 640), BF)
     spread = lane_spread(32, 16, 0, 128)
-    for at, b_ref, blocks in ((0, b_mid, 4), (48, b_low, 2), (96, b_deep, 2)):
-        w = [nn(w_ref[kx, at : at + 48], spread) for kx in range(3)]
-        for ky in range(3):
-            taps = [stacked(w[kx], ky, 16) for kx in range(3)]
-            same_level(b_ref, ky * blocks * 128, blocks, taps, 16)
-    w_skip = [nn(w_ref[kx, 144:192], spread) for kx in range(3)]
+    w_mid, w_low, w_deep, w_skip = (
+        [nn(w_ref[kx, at : at + 48], spread) for kx in range(3)] for at in (0, 48, 96, 144)
+    )
     w_rise = [nn(w_ref[kx, 144:192], lane_spread(32, 16, 16, 128)) for kx in range(3)]
     for ky in range(3):
-        taps = [stacked(w_skip[kx], ky, 16) for kx in range(3)]
-        same_level(b_up, ky * 512, 4, taps, 16)
+        for w, b_ref in ((w_mid, b_mid), (w_low, b_low), (w_deep, b_deep), (w_skip, b_up)):
+            same_level(b_ref, ky * 256, 2, [stacked(w[kx], ky, 16) for kx in range(3)], 16)
         taps = [stacked(w_rise[kx], ky, 16) for kx in range(3)]
-        from_coarse(b_up, (), 1536 + ky * 256, 4, 2, taps, 16)
+        from_coarse(b_up, (), 768 + ky * 128, 2, 1, taps, 16)
+    b_mid[:, 768:] = jnp.zeros((256, 256), BF)
+    b_mid[240:256, 768:896] = edge_rows(w_mid[2], 0).astype(BF)
+    b_mid[0:16, 896:1024] = edge_rows(w_mid[0], 4).astype(BF)
+    b_up[:, 1152:] = jnp.zeros((256, 256), BF)
+    b_up[240:256, 1152:1280] = (edge_rows(w_skip[2], 0) + edge_rows(w_rise[2], 4)).astype(BF)
+    b_up[0:16, 1280:1408] = (edge_rows(w_skip[0], 0) + edge_rows(w_rise[0], 4)).astype(BF)
     none = jnp.zeros((128, 128), BF)
     for out in range(2):
         for inp in range(4):
             b_pool[out * 128 : (out + 1) * 128, inp * 128 : (inp + 1) * 128] = (
                 pool_matrix(16, inp % 2) if inp // 2 == out else none
             )
+    o = iota((256, 512), 0)
+    group = o % 128 // 16
+    place = 128 - o // 128 * 16 + o % 16
+    place = jnp.where(group < 4, place, place + 256)
+    picks = (iota((256, 512), 1) == place) & (group % 4 < 3)
+    b_pool[256:512] = picks.astype(F32).astype(BF)
     to_lane, cell = iota((128, 512), 0), iota((128, 512), 1) // 16
     for q in range(4):
         b_last[q] = jnp.where(to_lane == q * 32 + cell, w_row, 0.0).astype(BF)
@@ -156,15 +179,31 @@
     lane = iota((256, 128), 1)
     before = jnp.where(row == 0, 0.0, rolled(turned, 1))
     after = jnp.where(row == 255, 0.0, rolled(turned, -1))
+    def taps_apart(v, length):
+        r, group = iota(v.shape, 0) % length, iota(v.shape, 1) // 16 % 4
+        down = jnp.where(r == 0, 0.0, rolled(v, 1))
+        up = jnp.where(r == length - 1, 0.0, rolled(v, -1))
+        return jnp.where(group == 0, down, jnp.where(group == 1, v, up)).astype(BF)
+
+    def lanes(ref, *pieces):
+        return jnp.concatenate([ref[:, at : at + size] for at, size in pieces], axis=1)
+
     for q in range(planes):
         three = jnp.zeros((256, 128), F32)
         for g, v in enumerate((before, turned, after)):
             three = jnp.where(lane // 32 == g, pltpu.roll(v, ((g - q) * 32) % 128, 1), three)
         first = jnp.maximum(nn(three.astype(BF), b_in[...]), 0.0)
-        place(lhs.at[q * 256 : (q + 1) * 256], 0, 512, first, 256)
-    skip = jnp.maximum(nt(lhs[...], b_mid[...]), 0.0)
+        rows_q = slice(q * 256, (q + 1) * 256)
+        place(lhs.at[rows_q], 0, 512, first[:, :512], 256)
+        lhs[rows_q, 1536:] = taps_apart(first[:, 512:], 256)
+    halves = []
+    for x in range(2):
+        cells = [(ky * 512 + x * 256, 256) for ky in range(3)]
+        bands = lanes(b_mid, (0, 768), (768 + x * 128, 128))
+        halves.append(jnp.maximum(nt(lanes(lhs, *cells, (1536, 128)), bands), 0.0))
+    skip = jnp.concatenate(halves, axis=1)
     place(wide, 0, 512, skip, 256)
-    fine = nt(skip.astype(BF), b_pool[...])
+    fine = nt(skip.astype(BF), b_pool[:256])
     for c in range(2):
         half[...] = fine[:, c * 128 : (c + 1) * 128]
         coarse[:, c * 128 : (c + 1) * 128] = 0.25 * (
@@ -180,7 +219,14 @@
         half[pl.ds(1, low_rows, stride=2), :] = part
         raised[:, c * 128 : (c + 1) * 128] = half[...]
     place(wide, 1536, 256, raised[...], 256)
-    joined = jnp.maximum(nt(wide[...], b_up[...]), 0.0).astype(BF)
+    wide[:, 2304:] = taps_apart(nt(lanes(wide, (640, 256), (1792, 256)), b_pool[256:]), 256)
+    halves = []
+    for x in range(2):
+        cells = [(ky * 512 + x * 256, 256) for ky in range(3)]
+        cells += [(1536 + ky * 256 + x * 128, 128) for ky in range(3)]
+        bands = lanes(b_up, (0, 1152), (1152 + x * 128, 128))
+        halves.append(jnp.maximum(nt(lanes(wide, *cells, (2304 + x * 128, 128)), bands), 0.0))
+    joined = jnp.concatenate(halves, axis=1).astype(BF)
     total = jnp.zeros((256, 128), F32)
     for q in range(planes):
         total = total + nt(joined[q * 256 : (q + 1) * 256], b_last[2 * rim + q])
@@ -418,8 +464,8 @@
         functools.partial(denoise_kernel, rim),
         bf(NZ, 48, 128),
         [
-            vmem((count * 256, 1536), BF),
-            vmem((count * 256, 2304), BF),
+            vmem((count * 256, 1664), BF),
+            vmem((count * 256, 2560), BF),
             vmem((count * 128, 256), F32),
             vmem((count * 256, 128), F32),
             vmem((count * 256, 256), F32),
@@ -442,12 +488,12 @@
     weights = call(
         plane_weights_kernel,
         [
-            bf(128, 512),
-            bf(512, 1536),
+            bf(128, 640),
+            bf(256, 1024),
             bf(256, 768),
             bf(256, 768),
-            bf(512, 2304),
-            bf(256, 512),
+            bf(256, 1408),
+            bf(512, 512),
             bf(4, 128, 512),
         ],
         [],

time: 55.9 us -> 54.7 us (0.979)
  Pallas kernels: 22.3 us -> 21 us
  local copies, waits for them, and re-layouts: 0.03 us -> 1.32 us
  other arithmetic: 1.69 us -> 0.84 us
  waiting for transfers between devices: 8.75 us -> 8.1 us
    pallas_call x6, Pallas kernels: 22.3 us -> 21 us  [call(): pl.pallas_call(kernel, out_shape=out_shape, in_specs=[spec] * len(args),...]
    unnamed x10 -> x22, local copies, waits for them, and re-layouts: 0.03 us -> 1.32 us
    add x2, other arithmetic: 0.94 us -> 0.08 us  [table(): total + jnp.pad(w, ((0, lead - size[0]), (at, rows - at - size[1]), (0, w...]
    all_to_all x1, waiting for transfers between devices: 7.33 us -> 6.68 us  [per_device(): window = lax.all_to_all(volume, 'z', 0, 0, tiled=True)]
  transfers between devices with their start and end apart: 3 -> 3, of which waited for: 2 -> 2; matrix products, arithmetic and copies ran while one was open for 2% -> 0% of each run, Pallas kernels for 12% -> 10%
where the time goes in v4:
time: 54.7 us; the launch traced here: 54.2 us
  Pallas kernels  21 us (38%)
  starting transfers between devices  11.5 us (21%)
  blocking collectives  11.3 us (21%)
  waiting for transfers between devices  8.1 us (15%)
  local copies, waits for them, and re-layouts  1.32 us (2%)
  other arithmetic  0.84 us (2%)
    pallas_call x6, Pallas kernels, call(): pl.pallas_call(kernel, out_shape=out_shape, in_specs=[spec] * len(args),...  21 us
    all_to_all x1, blocking collectives, per_device(): parts = lax.all_to_all(logits, 'i', 0, 0, tiled=True)  11.3 us
    all_to_all x1, starting transfers between devices, per_device(): window = lax.all_to_all(volume, 'z', 0, 0, tiled=True)  10.1 us
    all_to_all x1, waiting for transfers between devices, per_device(): window = lax.all_to_all(volume, 'z', 0, 0, tiled=True)  6.68 us
    ppermute x1, starting transfers between devices, per_device(): rim = lax.ppermute(own, ('i', 'z', 'c'), rim_pairs())  1.42 us
    ppermute x1, waiting for transfers between devices, per_device(): far = lax.ppermute(near, 'c', [(0, 1), (1, 0)])  1.42 us
    unnamed x22, local copies, waits for them, and re-layouts  1.32 us
  transfers between devices with their start and end apart: 3, of which 2 were waited for; matrix products, arithmetic and copies ran while one was open for 0% of the time, Pallas kernels for 10%

profile of v4, /device:TPU:16, one launch (start us, length us, event | category | flops | bytes accessed | tf_op | source)
XLA Modules:
  0.0 54.2 jit_solution(16768646227959379678)
XLA Ops:
  0.0 0.0 collective-permute-start
  0.0 1.4 %collective-permute-done = bf16[2,32,256]{2,1,0:T(8,128)(2,1)S(1)} collective-permute-done((bf16[2,32,256]{2,1,0:T(8,128)(2,1)}, bf16[2,32,256]{2,1,0:T(8,128)(2,1)S(1)}, u32[]{:S(2)}, u32[]{:S(2)}) %collective-permute-start) | collective-permute-done | bytes 32800 | tf_op jit(solution)/shard_map/ppermute | solution.py:484
  1.4 0.0 copy-start.5
  1.4 0.0 copy-start.6
  1.4 0.7 %slice_select_fusion.1 = (bf16[1,32,256]{2,1,0:T(8,128)(2,1)S(1)}, bf16[1,32,256]{2,1,0:T(8,128)(2,1)S(1)}) fusion(bf16[2,32,256]{2,1,0:T(8,128)(2,1)S(1)} %collective-permute-done, bf16[2,1,32,256]{3,2,1,0:T(8,128)(2,1)} %param.12, pred[]{:T(512)S(6)} %eq.3), kind=kLoop, calls=%fused_computation.4 | loop fusion | flops 16384 | bytes 98305 | tf_op jit(solution)/shard_map/jit(_where)/select_n | solution.py:504
  2.2 0.0 copy-start.10
  2.2 0.0 copy-start.3
  2.2 0.0 copy-start.4
  2.2 1.4 %collective-permute-start.1 = (bf16[2,32,256]{2,1,0:T(8,128)(2,1)S(1)}, bf16[2,32,256]{2,1,0:T(8,128)(2,1)S(1)}, u32[]{:S(2)}, u32[]{:S(2)}) collective-permute-start(bf16[2,32,256]{2,1,0:T(8,128)(2,1)S(1)} %pad_maximum_fusion.planes_ref), channel_id=1, source_target_pairs={{1,112},{16,0},{17,1},{32,16},{33,17},{48,32},{49,33},{64,48},{65,... | collective-permute-start | bytes 98312 | tf_op jit(solution)/shard_map/ppermute | solution.py:505
  3.6 0.0 copy-start.8
  3.7 0.0 copy-done.5
  3.7 0.0 copy-done.6
  3.7 0.0 copy-done.10
  3.7 0.0 copy-done.3
  3.7 0.0 copy-done.4
  3.7 0.6 %copy-done.8 = bf16[16,1,3,3]{0,3,2,1:T(4,128)(2,1)S(1)} copy-done((bf16[16,1,3,3]{0,3,2,1:T(4,128)(2,1)S(1)}, bf16[16,1,3,3]{0,3,2,1:T(4,128)(2,1)}, u32[]{:S(2)}) %copy-start.8) | copy-done | bytes 312
  4.4 0.9 %shard_map.118 = (bf16[128,640]{1,0:T(8,128)(2,1)S(1)}, bf16[256,1024]{1,0:T(8,128)(2,1)S(1)}, bf16[256,768]{1,0:T(8,128)(2,1)S(1)}, bf16[256,768]{1,0:T(8,128)(...) custom-call(bf16[3,208,32]{2,1,0:T(8,128)(2,1)S(1)} %pad_add_fusion.1.w_ref), custom_call_target="tpu_custom_call" | custom-call | tf_op jit(solution)/shard_map/pallas_call | solution.py:406
  5.3 3.4 %shard_map.119.refs_0_ = bf16[8,48,128]{2,1,0:T(8,128)(2,1)S(1)} custom-call(bf16[2,32,256]{2,1,0:T(8,128)(2,1)S(1)} %pad_maximum_fusion.planes_ref, bf16[128,640]{1,0:T(8,128)(2,1)S(1)} %get-tuple-element.16.refs_0_.refs_1_, bf16[256,1024]{1,0:T(8,128)(2,1)S(1)} %get-tuple-element.17.refs_1_.refs_2_, ...), custom_call_target="tpu_custom_call" | custom-call | tf_op jit(solution)/shard_map/pallas_call | solution.py:406
  8.7 0.0 collective-permute-done.1.planes_ref
  8.7 3.9 %shard_map.120 = bf16[8,48,128]{2,1,0:T(8,128)(2,1)} custom-call(bf16[2,32,256]{2,1,0:T(8,128)(2,1)S(1)} %collective-permute-done.1.planes_ref, bf16[8,48,128]{2,1,0:T(8,128)(2,1)S(1)} %shard_map.119.refs_0_, bf16[128,640]{1,0:T(8,128)(2,1)S(1)} %get-tuple-element.16.refs_0_.refs_1_, bf16[256,1024]{1,0:T(8,128)(2,1)S(1)} %get-tuple-element.17.refs_1_.refs_2_, ...), custom_call_target="tpu_custom_call" | custom-call | tf_op jit(solution)/shard_map/pallas_call | solution.py:406
  12.7 0.0 copy-start
  12.7 0.0 copy-start.1
  12.7 0.0 copy-start.2
  12.7 0.0 copy-start.9
  12.7 10.1 %all-to-all-start = ((bf16[8,48,128]{2,1,0:T(8,128)(2,1)}), bf16[8,48,128]{2,1,0:T(8,128)(2,1)S(1)}, u32[]{:S(2)}, u32[]{:S(2)}) async-start(bf16[8,48,128]{2,1,0:T(8,128)(2,1)} %shard_map.120), calls=%async_computation | async-start | bytes 196608 | tf_op jit(solution)/shard_map/all_to_all | solution.py:511
  22.7 0.0 copy-start.7
  22.7 0.0 copy-done
  22.7 0.0 copy-done.1
  22.8 0.0 copy-done.2
  22.8 0.0 copy-done.9
  22.8 0.7 %copy-done.7 = bf16[8,1,3,3,3]{0,4,3,2,1:T(4,128)(2,1)S(1)} copy-done((bf16[8,1,3,3,3]{0,4,3,2,1:T(4,128)(2,1)S(1)}, bf16[8,1,3,3,3]{0,4,3,2,1:T(4,128)(2,1)}, u32[]{:S(2)}) %copy-start.7) | copy-done | bytes 456
  23.5 1.3 %shard_map.121 = (bf16[3,128,1152]{2,1,0:T(8,128)(2,1)S(1)}, bf16[3,128,1152]{2,1,0:T(8,128)(2,1)S(1)}, bf16[3,128,1152]{2,1,0:T(8,128)(2,1)S(1)}, bf16[3,256,384]{2,1,0:T(8,128)(2,1)S(1)}) custom-call(bf16[9,88,16]{2,1,0:T(8,128)(2,1)S(1)} %pad_add_fusion.w_ref), custom_call_target="tpu_custom_call" | custom-call | tf_op jit(solution)/shard_map/pallas_call | solution.py:406
  24.8 6.7 %all-to-all-done.v_ref = bf16[8,48,128]{2,1,0:T(8,128)(2,1)S(1)} async-done(((bf16[8,48,128]{2,1,0:T(8,128)(2,1)}), bf16[8,48,128]{2,1,0:T(8,128)(2,1)S(1)}, u32[]{:S(2)}, u32[]{:S(2)}) %all-to-all-start) | async-done | bytes 98336 | tf_op jit(solution)/shard_map/all_to_all | solution.py:511
  31.5 10.3 %shard_map.122 = bf16[8,16,512]{2,1,0:T(8,128)(2,1)S(1)} custom-call(bf16[8,48,128]{2,1,0:T(8,128)(2,1)S(1)} %all-to-all-done.v_ref, bf16[3,128,1152]{2,1,0:T(8,128)(2,1)S(1)} %get-tuple-element.23.b_rest, bf16[3,128,1152]{2,1,0:T(8,128)(2,1)S(1)} %get-tuple-element.24.b_mid, bf16[3,128,1152]{2,1,0:T(8,128)(2,1)S(1)} %get-tuple-element.25.b_skip, ...), custom_call_target="tpu_custom_call" | custom-call | tf_op jit(solution)/shard_map/pallas_call | solution.py:406
  41.8 11.3 %all_to_all.10.parts_ref = bf16[8,16,512]{2,1,0:T(8,128)(2,1)S(1)} all-to-all(bf16[8,16,512]{2,1,0:T(8,128)(2,1)S(1)} %shard_map.122), channel_id=1, replica_groups=mesh['rep'=2,'i'=8,'z'=8,'c'=2] {'i'}, dimensions={0} | all-to-all | bytes 262144 | tf_op jit(solution)/shard_map/all_to_all | solution.py:529
  53.1 1.1 %shard_map.123 = f32[512,128]{1,0:T(8,128)} custom-call(bf16[8,16,512]{2,1,0:T(8,128)(2,1)S(1)} %all_to_all.10.parts_ref), custom_call_target="tpu_custom_call" | custom-call | tf_op jit(solution)/shard_map/pallas_call | solution.py:406
  (3 shorter events, 0.1 us)
Async XLA Ops:
  0.0 1.4 %collective-permute-start = (bf16[2,32,256]{2,1,0:T(8,128)(2,1)}, bf16[2,32,256]{2,1,0:T(8,128)(2,1)S(1)}, u32[]{:S(2)}, u32[]{:S(2)}) collective-permute-start(bf16[2,32,256]{2,1,0:T(8,128)(2,1)} %bitcast.42), channel_id=1, source_target_pairs={{0,1},{1,0},{2,3},{3,2},{4,5},{5,4},{6,7},{7,6},{8,9},{9,8},{10,11... | collective-permute-start | bytes 98312 | tf_op jit(solution)/shard_map/ppermute | solution.py:484
  1.4 2.2 %copy-start.5 = (bf16[16,16,3,3]{1,0,3,2:T(8,128)(2,1)S(1)}, bf16[16,16,3,3]{1,0,3,2:T(8,128)(2,1)}, u32[]{:S(2)}) copy-start(bf16[16,16,3,3]{1,0,3,2:T(8,128)(2,1)} %param.15) | copy-start | bytes 13828
  1.4 2.2 %copy-start.6 = (bf16[16,16,3,3]{1,0,3,2:T(8,128)(2,1)S(1)}, bf16[16,16,3,3]{1,0,3,2:T(8,128)(2,1)}, u32[]{:S(2)}) copy-start(bf16[16,16,3,3]{1,0,3,2:T(8,128)(2,1)} %param.14) | copy-start | bytes 13828
  2.2 1.5 %copy-start.10 = (bf16[1,16]{1,0:T(2,128)(2,1)S(1)}, bf16[1,16]{1,0:T(2,128)(2,1)}, u32[]{:S(2)}) copy-start(bf16[1,16]{1,0:T(2,128)(2,1)} %param.18) | copy-start | bytes 100
  2.2 1.5 %copy-start.3 = (bf16[16,32,3,3]{1,0,3,2:T(8,128)(2,1)S(1)}, bf16[16,32,3,3]{1,0,3,2:T(8,128)(2,1)}, u32[]{:S(2)}) copy-start(bf16[16,32,3,3]{1,0,3,2:T(8,128)(2,1)} %param.17) | copy-start | bytes 27652
  2.2 1.5 %copy-start.4 = (bf16[16,16,3,3]{1,0,3,2:T(8,128)(2,1)S(1)}, bf16[16,16,3,3]{1,0,3,2:T(8,128)(2,1)}, u32[]{:S(2)}) copy-start(bf16[16,16,3,3]{1,0,3,2:T(8,128)(2,1)} %param.16) | copy-start | bytes 13828
  2.2 6.5 %collective-permute-start.1 = (bf16[2,32,256]{2,1,0:T(8,128)(2,1)S(1)}, bf16[2,32,256]{2,1,0:T(8,128)(2,1)S(1)}, u32[]{:S(2)}, u32[]{:S(2)}) collective-permute-start(bf16[2,32,256]{2,1,0:T(8,128)(2,1)S(1)} %pad_maximum_fusion.planes_ref), channel_id=1, source_target_pairs={{1,112},{16,0},{17,1},{32,16},{33,17},{48,32},{49,33},{64,48},{65,... | collective-permute-start | bytes 98312 | tf_op jit(solution)/shard_map/ppermute | solution.py:505
  3.6 0.7 %copy-start.8 = (bf16[16,1,3,3]{0,3,2,1:T(4,128)(2,1)S(1)}, bf16[16,1,3,3]{0,3,2,1:T(4,128)(2,1)}, u32[]{:S(2)}) copy-start(bf16[16,1,3,3]{0,3,2,1:T(4,128)(2,1)} %param.13) | copy-start | bytes 868
  12.7 10.1 %copy-start = (bf16[8,16,3,3,3]{1,0,4,3,2:T(8,128)(2,1)S(1)}, bf16[8,16,3,3,3]{1,0,4,3,2:T(8,128)(2,1)}, u32[]{:S(2)}) copy-start(bf16[8,16,3,3,3]{1,0,4,3,2:T(8,128)(2,1)} %param.22) | copy-start | bytes 20740
  12.7 10.1 %copy-start.1 = (bf16[8,8,3,3,3]{1,0,4,3,2:T(8,128)(2,1)S(1)}, bf16[8,8,3,3,3]{1,0,4,3,2:T(8,128)(2,1)}, u32[]{:S(2)}) copy-start(bf16[8,8,3,3,3]{1,0,4,3,2:T(8,128)(2,1)} %param.21) | copy-start | bytes 10372
  12.7 10.1 %copy-start.2 = (bf16[8,8,3,3,3]{1,0,4,3,2:T(8,128)(2,1)S(1)}, bf16[8,8,3,3,3]{1,0,4,3,2:T(8,128)(2,1)}, u32[]{:S(2)}) copy-start(bf16[8,8,3,3,3]{1,0,4,3,2:T(8,128)(2,1)} %param.20) | copy-start | bytes 10372
  12.7 10.1 %copy-start.9 = (bf16[8,8]{1,0:T(8,128)(2,1)S(1)}, bf16[8,8]{1,0:T(8,128)(2,1)}, u32[]{:S(2)}) copy-start(bf16[8,8]{1,0:T(8,128)(2,1)} %param.23) | copy-start | bytes 388
  12.7 18.8 %all-to-all-start = ((bf16[8,48,128]{2,1,0:T(8,128)(2,1)}), bf16[8,48,128]{2,1,0:T(8,128)(2,1)S(1)}, u32[]{:S(2)}, u32[]{:S(2)}) async-start(bf16[8,48,128]{2,1,0:T(8,128)(2,1)} %shard_map.120), calls=%async_computation | async-start | bytes 196608 | tf_op jit(solution)/shard_map/all_to_all | solution.py:511
  22.7 0.7 %copy-start.7 = (bf16[8,1,3,3,3]{0,4,3,2,1:T(4,128)(2,1)S(1)}, bf16[8,1,3,3,3]{0,4,3,2,1:T(4,128)(2,1)}, u32[]{:S(2)}) copy-start(bf16[8,1,3,3,3]{0,4,3,2,1:T(4,128)(2,1)} %param.19) | copy-start | bytes 1300

commit v5 on v4

--- a/solution.py
+++ b/solution.py
@@ -333,30 +333,31 @@
         mask = inside(part, y_base - 5 + y0, 32, z_base, 256)
         for copy in range(2):
             h = masked(h1[:, copy * 256 : (copy + 1) * 256], mask)
-            for kz, steps in enumerate((1, 0, -1)):
-                moved = rolled(h, steps) if steps else h
-                h1l[copy, y0 : y0 + part, :, kz * 256 : (kz + 1) * 256] = moved.astype(BF).reshape(
-                    part, 32, 256
-                )
+            for kz in range(3):
+                moved = rolled(h, -(3 + kz)).reshape(part, 32, 256)[:, :24].reshape(part * 24, 256)
+                rows = slice(y0 * 24, (y0 + part) * 24)
+                h1l[copy, rows, kz * 256 : (kz + 1) * 256] = moved.astype(BF)
 
     pool_t = jnp.concatenate([pool_matrix(8, 0), pool_matrix(8, 1)], axis=1)
     logits = jnp.zeros((128, 512), F32)
     for copy in range(2):
         part = 20
-        n = part * 32
+        n = part * 24
         for step in range(2):
             y0 = step * part
             acc = jnp.zeros((n, 256), F32)
             for ky in range(3):
-                acc = acc + nt(
-                    h1l[copy, y0 + ky : y0 + ky + part].reshape(n, 768), two_blocks(b_mid, ky)
-                )
-            h2 = masked(acc, inside(part, y_base - 4 + y0, 32, z_base, 256))
-            fine = nt(h2.astype(BF), pool_t).reshape(part // 2, 2, 32, 128)
-            pool[y0 * 16 : y0 * 16 + n // 2] = (fine[:, 0] + fine[:, 1]).reshape(n // 2, 128)
+                first = (y0 + ky) * 24
+                acc = acc + nt(h1l[copy, first : first + n], two_blocks(b_mid, ky))
+            h2 = masked(acc, inside(part, y_base - 4 + y0, 24, z_base + 4, 256))
+            fine = nt(h2.astype(BF), pool_t).reshape(part // 2, 2, 24, 128)
+            filled = [fine[:, 0] + fine[:, 1], jnp.zeros((part // 2, 8, 128), F32)]
+            pool[y0 * 16 : (y0 + part) * 16] = jnp.concatenate(filled, axis=1).reshape(
+                part * 16, 128
+            )
             first, last = max(y0, 3), min(y0 + part, 37)
             for kz in range(3):
-                moved = rolled(h2, -(7 + kz)).reshape(part, 32, 256)
+                moved = rolled(h2, -(3 + kz)).reshape(part, 24, 256)
                 l4[copy, first - 3 : last - 3, :, kz * 256 : (kz + 1) * 256] = moved[
                     first - y0 : last - y0, :16
                 ].astype(BF)
@@ -368,13 +369,13 @@
         for ky in range(3):
             acc = acc + nt(ql[ky : ky + 18].reshape(288, 384), b_rest[ky, :, 512:896])
         h3 = masked(
-            acc, inside(18, 16 * at_z - 1, 16, 64 * at_c + 8 * at_i - 4, 128)
+            acc, inside(18, 16 * at_z - 1, 16, 64 * at_c + 8 * at_i - 2, 128)
         )
         rise[pl.ds(0, 288, stride=2), :] = h3
         rise[pl.ds(1, 288, stride=2), :] = h3
         r = rise[...]
         for kz in range(3):
-            moved = rolled(r, -(7 + kz)).reshape(18, 32, 128)[:, :16].astype(BF)
+            moved = rolled(r, -(3 + kz)).reshape(18, 32, 128)[:, :16].astype(BF)
             for slot in range(34):
                 l4[copy, slot, :, 768 + kz * 128 : 896 + kz * 128] = moved[(slot + 3) // 2 - 1]
         acc = jnp.zeros((512, 256), F32)
@@ -500,6 +501,7 @@
         16,
         table(3, 208, 32, *taps),
     )
+    far, weights = lax.optimization_barrier((far, weights))
     second = lax.axis_index("c") == 1
     own = jnp.stack([jnp.where(second, far[1], near[0]), jnp.where(second, near[1], far[0])])
     rim = lax.ppermute(own, ("i", "z", "c"), rim_pairs())
@@ -516,7 +518,7 @@
         [
             vmem((48 * 32, 128), F32),
             vmem((42, 32, 384), BF),
-            vmem((2, 42, 32, 768), BF),
+            vmem((2, 42 * 24, 768), BF),
             vmem((640, 128), F32),
             vmem((20, 16, 384), BF),
             vmem((576, 128), F32),

time: 54.7 us -> 53.4 us (0.976)
  starting transfers between devices: 11.5 us -> 10.3 us
  blocking collectives: 11.3 us -> 10.4 us
  waiting for transfers between devices: 8.1 us -> 8.74 us
    ppermute x1, waiting for transfers between devices: 1.42 us -> 0.01 us  [per_device(): far = lax.ppermute(near, 'c', [(0, 1), (1, 0)])]
    ppermute x1, waiting for transfers between devices: 0.01 us -> 1.08 us  [per_device(): rim = lax.ppermute(own, ('i', 'z', 'c'), rim_pairs())]
    all_to_all x1, starting transfers between devices: 10.1 us -> 9 us  [per_device(): window = lax.all_to_all(volume, 'z', 0, 0, tiled=True)]
    all_to_all x1, waiting for transfers between devices: 6.68 us -> 7.66 us  [per_device(): window = lax.all_to_all(volume, 'z', 0, 0, tiled=True)]
    all_to_all x1, blocking collectives: 11.3 us -> 10.4 us  [per_device(): parts = lax.all_to_all(logits, 'i', 0, 0, tiled=True)]
    add x2, other arithmetic: 0.08 us -> 0.9 us  [table(): total + jnp.pad(w, ((0, lead - size[0]), (at, rows - at - size[1]), (0, w...]
    select_n x1, other arithmetic: 0.75 us -> 0.01 us  [per_device(): jnp.where(second, far[1], near[0])]
    unnamed x22 -> x16, local copies, waits for them, and re-layouts: 1.32 us -> 1.36 us
  transfers between devices with their start and end apart: 3 -> 3, of which waited for: 2 -> 2; matrix products, arithmetic and copies ran while one was open for 0% -> 2% of each run, Pallas kernels for 10% -> 11%
where the time goes in v5:
time: 53.4 us; the launch traced here: 53 us
  Pallas kernels  21.1 us (40%)
  blocking collectives  10.4 us (19%)
  starting transfers between devices  10.3 us (19%)
  waiting for transfers between devices  8.74 us (16%)
  local copies, waits for them, and re-layouts  1.36 us (3%)
  other arithmetic  0.92 us (2%)
    pallas_call x6, Pallas kernels, call(): pl.pallas_call(kernel, out_shape=out_shape, in_specs=[spec] * len(args),...  21.1 us
    all_to_all x1, blocking collectives, per_device(): parts = lax.all_to_all(logits, 'i', 0, 0, tiled=True)  10.4 us
    all_to_all x1, starting transfers between devices, per_device(): window = lax.all_to_all(volume, 'z', 0, 0, tiled=True)  9 us
    all_to_all x1, waiting for transfers between devices, per_device(): window = lax.all_to_all(volume, 'z', 0, 0, tiled=True)  7.66 us
    unnamed x16, local copies, waits for them, and re-layouts  1.36 us
    ppermute x1, starting transfers between devices, per_device(): rim = lax.ppermute(own, ('i', 'z', 'c'), rim_pairs())  1.29 us
    ppermute x1, waiting for transfers between devices, per_device(): rim = lax.ppermute(own, ('i', 'z', 'c'), rim_pairs())  1.08 us
  transfers between devices with their start and end apart: 3, of which 2 were waited for; matrix products, arithmetic and copies ran while one was open for 2% of the time, Pallas kernels for 11%

profile of v5, /device:TPU:16, one launch (start us, length us, event | category | flops | bytes accessed | tf_op | source)
XLA Modules:
  0.0 53.0 jit_solution(1829739739891317271)
XLA Ops:
  0.0 0.0 collective-permute-start
  0.0 0.0 copy-start.5
  0.0 0.0 copy-start.7
  0.0 0.7 %copy-done.5 = bf16[16,1,3,3]{0,3,2,1:T(4,128)(2,1)S(1)} copy-done((bf16[16,1,3,3]{0,3,2,1:T(4,128)(2,1)S(1)}, bf16[16,1,3,3]{0,3,2,1:T(4,128)(2,1)}, u32[]{:S(2)}) %copy-start.5) | copy-done | bytes 312
  0.7 0.0 copy-done.7
  0.7 0.9 %pad_add_fusion.1.w_ref = bf16[3,208,32]{2,1,0:T(8,128)(2,1)S(1)} fusion(bf16[1,1,16]{2,1,0:T(2,128)(2,1)S(1)} %bitcast.46, bf16[3,3,16]{2,1,0:T(4,128)(2,1)S(1)} %bitcast.44, bf16[3,48,32]{2,1,0:T(8,128)(2,1)} %bitcast.38, bf16[3,48,16]{2,1,0:T(8,128)(2,1)} %bitcast.39, bf16[3,48,16]{2,1,0:T(8,128)(2,1)} %bitcast.40, bf16[3,48,16]{2,1,0:T(8,128)(2,1)} %bitcast.41), kind=kLoop, calls=%fused_computation.1 | loop fusion | flops 239616 | bytes 63296 | tf_op jit(solution)/shard_map/add | solution.py:425
  1.6 0.0 copy-start.3
  1.6 0.9 %shard_map.118 = (bf16[128,640]{1,0:T(8,128)(2,1)S(1)}, bf16[256,1024]{1,0:T(8,128)(2,1)S(1)}, bf16[256,768]{1,0:T(8,128)(2,1)S(1)}, bf16[256,768]{1,0:T(8,128)(...) custom-call(bf16[3,208,32]{2,1,0:T(8,128)(2,1)S(1)} %pad_add_fusion.1.w_ref), custom_call_target="tpu_custom_call" | custom-call | tf_op jit(solution)/shard_map/pallas_call | solution.py:407
  2.5 0.0 collective-permute-done
  2.5 0.0 copy-done.3
  2.5 1.3 %collective-permute-start.1 = (bf16[2,32,256]{2,1,0:T(8,128)(2,1)S(1)}, bf16[2,32,256]{2,1,0:T(8,128)(2,1)S(1)}, u32[]{:S(2)}, u32[]{:S(2)}) collective-permute-start(bf16[2,32,256]{2,1,0:T(8,128)(2,1)S(1)} %pad_maximum_fusion.planes_ref), channel_id=1, source_target_pairs={{1,112},{16,0},{17,1},{32,16},{33,17},{48,32},{49,33},{64,48},{65,... | collective-permute-start | bytes 98312 | tf_op jit(solution)/shard_map/ppermute | solution.py:507
  3.8 3.4 %shard_map.119.refs_0_ = bf16[8,48,128]{2,1,0:T(8,128)(2,1)S(1)} custom-call(bf16[2,32,256]{2,1,0:T(8,128)(2,1)S(1)} %pad_maximum_fusion.planes_ref, bf16[128,640]{1,0:T(8,128)(2,1)S(1)} %get-tuple-element.32.refs_0_.refs_1_, bf16[256,1024]{1,0:T(8,128)(2,1)S(1)} %get-tuple-element.33.refs_1_.refs_2_, ...), custom_call_target="tpu_custom_call" | custom-call | tf_op jit(solution)/shard_map/pallas_call | solution.py:407
  7.3 1.1 %collective-permute-done.1.planes_ref = bf16[2,32,256]{2,1,0:T(8,128)(2,1)S(1)} collective-permute-done((bf16[2,32,256]{2,1,0:T(8,128)(2,1)S(1)}, bf16[2,32,256]{2,1,0:T(8,128)(2,1)S(1)}, u32[]{:S(2)}, u32[]{:S(2)}) %collective-permute-start.1) | collective-permute-done | bytes 32800 | tf_op jit(solution)/shard_map/ppermute | solution.py:507
  8.3 3.9 %shard_map.120 = bf16[8,48,128]{2,1,0:T(8,128)(2,1)} custom-call(bf16[2,32,256]{2,1,0:T(8,128)(2,1)S(1)} %collective-permute-done.1.planes_ref, bf16[8,48,128]{2,1,0:T(8,128)(2,1)S(1)} %shard_map.119.refs_0_, bf16[128,640]{1,0:T(8,128)(2,1)S(1)} %get-tuple-element.32.refs_0_.refs_1_, bf16[256,1024]{1,0:T(8,128)(2,1)S(1)} %get-tuple-element.33.refs_1_.refs_2_, ...), custom_call_target="tpu_custom_call" | custom-call | tf_op jit(solution)/shard_map/pallas_call | solution.py:407
  12.3 0.0 copy-start
  12.3 0.0 copy-start.1
  12.3 0.0 copy-start.2
  12.3 0.0 copy-start.6
  12.3 9.0 %all-to-all-start = ((bf16[8,48,128]{2,1,0:T(8,128)(2,1)}), bf16[8,48,128]{2,1,0:T(8,128)(2,1)S(1)}, u32[]{:S(2)}, u32[]{:S(2)}) async-start(bf16[8,48,128]{2,1,0:T(8,128)(2,1)} %shard_map.120), calls=%async_computation | async-start | bytes 196608 | tf_op jit(solution)/shard_map/all_to_all | solution.py:513
  21.3 0.0 copy-start.4
  21.3 0.0 copy-done
  21.3 0.0 copy-done.1
  21.3 0.0 copy-done.2
  21.3 0.0 copy-done.6
  21.3 0.7 %copy-done.4 = bf16[8,1,3,3,3]{0,4,3,2,1:T(4,128)(2,1)S(1)} copy-done((bf16[8,1,3,3,3]{0,4,3,2,1:T(4,128)(2,1)S(1)}, bf16[8,1,3,3,3]{0,4,3,2,1:T(4,128)(2,1)}, u32[]{:S(2)}) %copy-start.4) | copy-done | bytes 456
  22.0 1.3 %shard_map.121 = (bf16[3,128,1152]{2,1,0:T(8,128)(2,1)S(1)}, bf16[3,128,1152]{2,1,0:T(8,128)(2,1)S(1)}, bf16[3,128,1152]{2,1,0:T(8,128)(2,1)S(1)}, bf16[3,256,384]{2,1,0:T(8,128)(2,1)S(1)}) custom-call(bf16[9,88,16]{2,1,0:T(8,128)(2,1)S(1)} %pad_add_fusion.w_ref), custom_call_target="tpu_custom_call" | custom-call | tf_op jit(solution)/shard_map/pallas_call | solution.py:407
  23.4 7.7 %all-to-all-done.v_ref = bf16[8,48,128]{2,1,0:T(8,128)(2,1)S(1)} async-done(((bf16[8,48,128]{2,1,0:T(8,128)(2,1)}), bf16[8,48,128]{2,1,0:T(8,128)(2,1)S(1)}, u32[]{:S(2)}, u32[]{:S(2)}) %all-to-all-start) | async-done | bytes 98336 | tf_op jit(solution)/shard_map/all_to_all | solution.py:513
  31.0 10.4 %shard_map.122 = bf16[8,16,512]{2,1,0:T(8,128)(2,1)S(1)} custom-call(bf16[8,48,128]{2,1,0:T(8,128)(2,1)S(1)} %all-to-all-done.v_ref, bf16[3,128,1152]{2,1,0:T(8,128)(2,1)S(1)} %get-tuple-element.39.b_rest, bf16[3,128,1152]{2,1,0:T(8,128)(2,1)S(1)} %get-tuple-element.40.b_mid, bf16[3,128,1152]{2,1,0:T(8,128)(2,1)S(1)} %get-tuple-element.41.b_skip, ...), custom_call_target="tpu_custom_call" | custom-call | tf_op jit(solution)/shard_map/pallas_call | solution.py:407
  41.4 10.4 %all_to_all.10.parts_ref = bf16[8,16,512]{2,1,0:T(8,128)(2,1)S(1)} all-to-all(bf16[8,16,512]{2,1,0:T(8,128)(2,1)S(1)} %shard_map.122), channel_id=1, replica_groups=mesh['rep'=2,'i'=8,'z'=8,'c'=2] {'i'}, dimensions={0} | all-to-all | bytes 262144 | tf_op jit(solution)/shard_map/all_to_all | solution.py:531
  51.9 1.1 %shard_map.123 = f32[512,128]{1,0:T(8,128)} custom-call(bf16[8,16,512]{2,1,0:T(8,128)(2,1)S(1)} %all_to_all.10.parts_ref), custom_call_target="tpu_custom_call" | custom-call | tf_op jit(solution)/shard_map/pallas_call | solution.py:407
  (3 shorter events, 0.1 us)
Async XLA Ops:
  0.0 2.5 %collective-permute-start = (bf16[2,32,256]{2,1,0:T(8,128)(2,1)}, bf16[2,32,256]{2,1,0:T(8,128)(2,1)S(1)}, u32[]{:S(2)}, u32[]{:S(2)}) collective-permute-start(bf16[2,32,256]{2,1,0:T(8,128)(2,1)} %bitcast.42), channel_id=1, source_target_pairs={{0,1},{1,0},{2,3},{3,2},{4,5},{5,4},{6,7},{7,6},{8,9},{9,8},{10,11... | collective-permute-start | bytes 98312 | tf_op jit(solution)/shard_map/ppermute | solution.py:485
  0.0 0.7 %copy-start.5 = (bf16[16,1,3,3]{0,3,2,1:T(4,128)(2,1)S(1)}, bf16[16,1,3,3]{0,3,2,1:T(4,128)(2,1)}, u32[]{:S(2)}) copy-start(bf16[16,1,3,3]{0,3,2,1:T(4,128)(2,1)} %param.13) | copy-start | bytes 868
  0.0 0.7 %copy-start.7 = (bf16[1,16]{1,0:T(2,128)(2,1)S(1)}, bf16[1,16]{1,0:T(2,128)(2,1)}, u32[]{:S(2)}) copy-start(bf16[1,16]{1,0:T(2,128)(2,1)} %param.18) | copy-start | bytes 100
  1.6 0.9 %copy-start.3 = (bf16[2,1,32,256]{3,2,1,0:T(8,128)(2,1)S(1)}, bf16[2,1,32,256]{3,2,1,0:T(8,128)(2,1)}, u32[]{:S(2)}) copy-start(bf16[2,1,32,256]{3,2,1,0:T(8,128)(2,1)} %param.12) | copy-start | bytes 98308
  2.5 5.8 %collective-permute-start.1 = (bf16[2,32,256]{2,1,0:T(8,128)(2,1)S(1)}, bf16[2,32,256]{2,1,0:T(8,128)(2,1)S(1)}, u32[]{:S(2)}, u32[]{:S(2)}) collective-permute-start(bf16[2,32,256]{2,1,0:T(8,128)(2,1)S(1)} %pad_maximum_fusion.planes_ref), channel_id=1, source_target_pairs={{1,112},{16,0},{17,1},{32,16},{33,17},{48,32},{49,33},{64,48},{65,... | collective-permute-start | bytes 98312 | tf_op jit(solution)/shard_map/ppermute | solution.py:507
  12.3 9.0 %copy-start = (bf16[8,16,3,3,3]{1,0,4,3,2:T(8,128)(2,1)S(1)}, bf16[8,16,3,3,3]{1,0,4,3,2:T(8,128)(2,1)}, u32[]{:S(2)}) copy-start(bf16[8,16,3,3,3]{1,0,4,3,2:T(8,128)(2,1)} %param.22) | copy-start | bytes 20740
  12.3 9.0 %copy-start.1 = (bf16[8,8,3,3,3]{1,0,4,3,2:T(8,128)(2,1)S(1)}, bf16[8,8,3,3,3]{1,0,4,3,2:T(8,128)(2,1)}, u32[]{:S(2)}) copy-start(bf16[8,8,3,3,3]{1,0,4,3,2:T(8,128)(2,1)} %param.21) | copy-start | bytes 10372
  12.3 9.0 %copy-start.2 = (bf16[8,8,3,3,3]{1,0,4,3,2:T(8,128)(2,1)S(1)}, bf16[8,8,3,3,3]{1,0,4,3,2:T(8,128)(2,1)}, u32[]{:S(2)}) copy-start(bf16[8,8,3,3,3]{1,0,4,3,2:T(8,128)(2,1)} %param.20) | copy-start | bytes 10372
  12.3 9.0 %copy-start.6 = (bf16[8,8]{1,0:T(8,128)(2,1)S(1)}, bf16[8,8]{1,0:T(8,128)(2,1)}, u32[]{:S(2)}) copy-start(bf16[8,8]{1,0:T(8,128)(2,1)} %param.23) | copy-start | bytes 388
  12.3 18.7 %all-to-all-start = ((bf16[8,48,128]{2,1,0:T(8,128)(2,1)}), bf16[8,48,128]{2,1,0:T(8,128)(2,1)S(1)}, u32[]{:S(2)}, u32[]{:S(2)}) async-start(bf16[8,48,128]{2,1,0:T(8,128)(2,1)} %shard_map.120), calls=%async_computation | async-start | bytes 196608 | tf_op jit(solution)/shard_map/all_to_all | solution.py:513
  21.3 0.7 %copy-start.4 = (bf16[8,1,3,3,3]{0,4,3,2,1:T(4,128)(2,1)S(1)}, bf16[8,1,3,3,3]{0,4,3,2,1:T(4,128)(2,1)}, u32[]{:S(2)}) copy-start(bf16[8,1,3,3,3]{0,4,3,2,1:T(4,128)(2,1)} %param.19) | copy-start | bytes 1300

commit v6 on v5

--- a/solution.py
+++ b/solution.py
@@ -341,26 +341,15 @@
     pool_t = jnp.concatenate([pool_matrix(8, 0), pool_matrix(8, 1)], axis=1)
     logits = jnp.zeros((128, 512), F32)
     for copy in range(2):
-        part = 20
-        n = part * 24
-        for step in range(2):
-            y0 = step * part
-            acc = jnp.zeros((n, 256), F32)
-            for ky in range(3):
-                first = (y0 + ky) * 24
-                acc = acc + nt(h1l[copy, first : first + n], two_blocks(b_mid, ky))
-            h2 = masked(acc, inside(part, y_base - 4 + y0, 24, z_base + 4, 256))
-            fine = nt(h2.astype(BF), pool_t).reshape(part // 2, 2, 24, 128)
-            filled = [fine[:, 0] + fine[:, 1], jnp.zeros((part // 2, 8, 128), F32)]
-            pool[y0 * 16 : (y0 + part) * 16] = jnp.concatenate(filled, axis=1).reshape(
-                part * 16, 128
-            )
-            first, last = max(y0, 3), min(y0 + part, 37)
-            for kz in range(3):
-                moved = rolled(h2, -(3 + kz)).reshape(part, 24, 256)
-                l4[copy, first - 3 : last - 3, :, kz * 256 : (kz + 1) * 256] = moved[
-                    first - y0 : last - y0, :16
-                ].astype(BF)
+        rows = jnp.concatenate([h1l[copy, ky * 24 : ky * 24 + 960] for ky in range(3)], axis=1)
+        bands = jnp.concatenate([two_blocks(b_mid, ky) for ky in range(3)], axis=1)
+        h2 = masked(nt(rows, bands), inside(40, y_base - 4, 24, z_base + 4, 256))
+        fine = nt(h2.astype(BF), pool_t).reshape(20, 2, 24, 128)
+        filled = [fine[:, 0] + fine[:, 1], jnp.zeros((20, 8, 128), F32)]
+        pool[...] = jnp.concatenate(filled, axis=1).reshape(640, 128)
+        for kz in range(3):
+            moved = rolled(h2, -(3 + kz)).reshape(40, 24, 256)
+            l4[copy, :, :, kz * 256 : (kz + 1) * 256] = moved[3:37, :16].astype(BF)
         q = 0.125 * (pool[pl.ds(0, 320, stride=2), :] + pool[pl.ds(1, 320, stride=2), :])
         for kz, steps in enumerate((1, 0, -1)):
             moved = rolled(q, steps) if steps else q
@@ -378,11 +367,12 @@
             moved = rolled(r, -(3 + kz)).reshape(18, 32, 128)[:, :16].astype(BF)
             for slot in range(34):
                 l4[copy, slot, :, 768 + kz * 128 : 896 + kz * 128] = moved[(slot + 3) // 2 - 1]
-        acc = jnp.zeros((512, 256), F32)
-        for ky in range(3):
-            bands = jnp.concatenate([two_blocks(b_skip, ky), b_rise[ky]], axis=1)
-            acc = acc + nt(l4[copy, ky : ky + 32].reshape(512, 1152), bands)
-        h4 = jnp.maximum(acc, 0.0).astype(BF)
+        at_rows = [slice(ky, ky + 32) for ky in range(3)]
+        rows = [l4[copy, at, :, :768].reshape(512, 768) for at in at_rows]
+        rows += [l4[copy, at, :, 768:].reshape(512, 384) for at in at_rows]
+        bands = [two_blocks(b_skip, ky) for ky in range(3)] + [b_rise[ky] for ky in range(3)]
+        h4 = nt(jnp.concatenate(rows, axis=1), jnp.concatenate(bands, axis=1))
+        h4 = jnp.maximum(h4, 0.0).astype(BF)
         logits = logits + nt(b_rest[copy, :, 896:], h4)
     out_ref[...] = (0.5 * logits).astype(BF).reshape(NI, 16, 512)
 

time: 53.4 us -> 52.4 us (0.981)
  Pallas kernels: 21.1 us -> 20.1 us
    pallas_call x6, Pallas kernels: 21.1 us -> 20.1 us  [call(): pl.pallas_call(kernel, out_shape=out_shape, in_specs=[spec] * len(args),...]
where the time goes in v6:
time: 52.4 us; the launch traced here: 52 us
  Pallas kernels  20.1 us (38%)
  blocking collectives  10.4 us (20%)
  starting transfers between devices  10.3 us (20%)
  waiting for transfers between devices  8.74 us (17%)
  local copies, waits for them, and re-layouts  1.36 us (3%)
  other arithmetic  0.92 us (2%)
    pallas_call x6, Pallas kernels, call(): pl.pallas_call(kernel, out_shape=out_shape, in_specs=[spec] * len(args),...  20.1 us
    all_to_all x1, blocking collectives, per_device(): parts = lax.all_to_all(logits, 'i', 0, 0, tiled=True)  10.4 us
    all_to_all x1, starting transfers between devices, per_device(): window = lax.all_to_all(volume, 'z', 0, 0, tiled=True)  9 us
    all_to_all x1, waiting for transfers between devices, per_device(): window = lax.all_to_all(volume, 'z', 0, 0, tiled=True)  7.66 us
    unnamed x16, local copies, waits for them, and re-layouts  1.36 us
    ppermute x1, starting transfers between devices, per_device(): rim = lax.ppermute(own, ('i', 'z', 'c'), rim_pairs())  1.29 us
    ppermute x1, waiting for transfers between devices, per_device(): rim = lax.ppermute(own, ('i', 'z', 'c'), rim_pairs())  1.08 us
  transfers between devices with their start and end apart: 3, of which 2 were waited for; matrix products, arithmetic and copies ran while one was open for 2% of the time, Pallas kernels for 11%

profile of v6, /device:TPU:16, one launch (start us, length us, event | category | flops | bytes accessed | tf_op | source)
XLA Modules:
  0.0 52.0 jit_solution(7755295253424725055)
XLA Ops:
  0.0 0.0 collective-permute-start
  0.0 0.0 copy-start.5
  0.0 0.0 copy-start.7
  0.0 0.7 %copy-done.5 = bf16[16,1,3,3]{0,3,2,1:T(4,128)(2,1)S(1)} copy-done((bf16[16,1,3,3]{0,3,2,1:T(4,128)(2,1)S(1)}, bf16[16,1,3,3]{0,3,2,1:T(4,128)(2,1)}, u32[]{:S(2)}) %copy-start.5) | copy-done | bytes 312
  0.7 0.0 copy-done.7
  0.7 0.9 %pad_add_fusion.1.w_ref = bf16[3,208,32]{2,1,0:T(8,128)(2,1)S(1)} fusion(bf16[1,1,16]{2,1,0:T(2,128)(2,1)S(1)} %bitcast.46, bf16[3,3,16]{2,1,0:T(4,128)(2,1)S(1)} %bitcast.44, bf16[3,48,32]{2,1,0:T(8,128)(2,1)} %bitcast.38, bf16[3,48,16]{2,1,0:T(8,128)(2,1)} %bitcast.39, bf16[3,48,16]{2,1,0:T(8,128)(2,1)} %bitcast.40, bf16[3,48,16]{2,1,0:T(8,128)(2,1)} %bitcast.41), kind=kLoop, calls=%fused_computation.1 | loop fusion | flops 239616 | bytes 63296 | tf_op jit(solution)/shard_map/add | solution.py:415
  1.6 0.0 copy-start.3
  1.6 0.9 %shard_map.118 = (bf16[128,640]{1,0:T(8,128)(2,1)S(1)}, bf16[256,1024]{1,0:T(8,128)(2,1)S(1)}, bf16[256,768]{1,0:T(8,128)(2,1)S(1)}, bf16[256,768]{1,0:T(8,128)(...) custom-call(bf16[3,208,32]{2,1,0:T(8,128)(2,1)S(1)} %pad_add_fusion.1.w_ref), custom_call_target="tpu_custom_call" | custom-call | tf_op jit(solution)/shard_map/pallas_call | solution.py:397
  2.5 0.0 collective-permute-done
  2.5 0.0 copy-done.3
  2.5 1.3 %collective-permute-start.1 = (bf16[2,32,256]{2,1,0:T(8,128)(2,1)S(1)}, bf16[2,32,256]{2,1,0:T(8,128)(2,1)S(1)}, u32[]{:S(2)}, u32[]{:S(2)}) collective-permute-start(bf16[2,32,256]{2,1,0:T(8,128)(2,1)S(1)} %pad_maximum_fusion.planes_ref), channel_id=1, source_target_pairs={{1,112},{16,0},{17,1},{32,16},{33,17},{48,32},{49,33},{64,48},{65,... | collective-permute-start | bytes 98312 | tf_op jit(solution)/shard_map/ppermute | solution.py:497
  3.8 3.4 %shard_map.119.refs_0_ = bf16[8,48,128]{2,1,0:T(8,128)(2,1)S(1)} custom-call(bf16[2,32,256]{2,1,0:T(8,128)(2,1)S(1)} %pad_maximum_fusion.planes_ref, bf16[128,640]{1,0:T(8,128)(2,1)S(1)} %get-tuple-element.32.refs_0_.refs_1_, bf16[256,1024]{1,0:T(8,128)(2,1)S(1)} %get-tuple-element.33.refs_1_.refs_2_, ...), custom_call_target="tpu_custom_call" | custom-call | tf_op jit(solution)/shard_map/pallas_call | solution.py:397
  7.3 1.1 %collective-permute-done.1.planes_ref = bf16[2,32,256]{2,1,0:T(8,128)(2,1)S(1)} collective-permute-done((bf16[2,32,256]{2,1,0:T(8,128)(2,1)S(1)}, bf16[2,32,256]{2,1,0:T(8,128)(2,1)S(1)}, u32[]{:S(2)}, u32[]{:S(2)}) %collective-permute-start.1) | collective-permute-done | bytes 32800 | tf_op jit(solution)/shard_map/ppermute | solution.py:497
  8.3 3.9 %shard_map.120 = bf16[8,48,128]{2,1,0:T(8,128)(2,1)} custom-call(bf16[2,32,256]{2,1,0:T(8,128)(2,1)S(1)} %collective-permute-done.1.planes_ref, bf16[8,48,128]{2,1,0:T(8,128)(2,1)S(1)} %shard_map.119.refs_0_, bf16[128,640]{1,0:T(8,128)(2,1)S(1)} %get-tuple-element.32.refs_0_.refs_1_, bf16[256,1024]{1,0:T(8,128)(2,1)S(1)} %get-tuple-element.33.refs_1_.refs_2_, ...), custom_call_target="tpu_custom_call" | custom-call | tf_op jit(solution)/shard_map/pallas_call | solution.py:397
  12.3 0.0 copy-start
  12.3 0.0 copy-start.1
  12.3 0.0 copy-start.2
  12.3 0.0 copy-start.6
  12.3 9.0 %all-to-all-start = ((bf16[8,48,128]{2,1,0:T(8,128)(2,1)}), bf16[8,48,128]{2,1,0:T(8,128)(2,1)S(1)}, u32[]{:S(2)}, u32[]{:S(2)}) async-start(bf16[8,48,128]{2,1,0:T(8,128)(2,1)} %shard_map.120), calls=%async_computation | async-start | bytes 196608 | tf_op jit(solution)/shard_map/all_to_all | solution.py:503
  21.3 0.0 copy-start.4
  21.3 0.0 copy-done
  21.3 0.0 copy-done.1
  21.3 0.0 copy-done.2
  21.3 0.0 copy-done.6
  21.3 0.7 %copy-done.4 = bf16[8,1,3,3,3]{0,4,3,2,1:T(4,128)(2,1)S(1)} copy-done((bf16[8,1,3,3,3]{0,4,3,2,1:T(4,128)(2,1)S(1)}, bf16[8,1,3,3,3]{0,4,3,2,1:T(4,128)(2,1)}, u32[]{:S(2)}) %copy-start.4) | copy-done | bytes 456
  22.0 1.3 %shard_map.121 = (bf16[3,128,1152]{2,1,0:T(8,128)(2,1)S(1)}, bf16[3,128,1152]{2,1,0:T(8,128)(2,1)S(1)}, bf16[3,128,1152]{2,1,0:T(8,128)(2,1)S(1)}, bf16[3,256,384]{2,1,0:T(8,128)(2,1)S(1)}) custom-call(bf16[9,88,16]{2,1,0:T(8,128)(2,1)S(1)} %pad_add_fusion.w_ref), custom_call_target="tpu_custom_call" | custom-call | tf_op jit(solution)/shard_map/pallas_call | solution.py:397
  23.4 7.7 %all-to-all-done.v_ref = bf16[8,48,128]{2,1,0:T(8,128)(2,1)S(1)} async-done(((bf16[8,48,128]{2,1,0:T(8,128)(2,1)}), bf16[8,48,128]{2,1,0:T(8,128)(2,1)S(1)}, u32[]{:S(2)}, u32[]{:S(2)}) %all-to-all-start) | async-done | bytes 98336 | tf_op jit(solution)/shard_map/all_to_all | solution.py:503
  31.0 9.4 %shard_map.122 = bf16[8,16,512]{2,1,0:T(8,128)(2,1)S(1)} custom-call(bf16[8,48,128]{2,1,0:T(8,128)(2,1)S(1)} %all-to-all-done.v_ref, bf16[3,128,1152]{2,1,0:T(8,128)(2,1)S(1)} %get-tuple-element.39.b_rest, bf16[3,128,1152]{2,1,0:T(8,128)(2,1)S(1)} %get-tuple-element.40.b_mid, bf16[3,128,1152]{2,1,0:T(8,128)(2,1)S(1)} %get-tuple-element.41.b_skip, ...), custom_call_target="tpu_custom_call" | custom-call | tf_op jit(solution)/shard_map/pallas_call | solution.py:397
  40.4 10.4 %all_to_all.10.parts_ref = bf16[8,16,512]{2,1,0:T(8,128)(2,1)S(1)} all-to-all(bf16[8,16,512]{2,1,0:T(8,128)(2,1)S(1)} %shard_map.122), channel_id=1, replica_groups=mesh['rep'=2,'i'=8,'z'=8,'c'=2] {'i'}, dimensions={0} | all-to-all | bytes 262144 | tf_op jit(solution)/shard_map/all_to_all | solution.py:521
  50.9 1.1 %shard_map.123 = f32[512,128]{1,0:T(8,128)} custom-call(bf16[8,16,512]{2,1,0:T(8,128)(2,1)S(1)} %all_to_all.10.parts_ref), custom_call_target="tpu_custom_call" | custom-call | tf_op jit(solution)/shard_map/pallas_call | solution.py:397
  (3 shorter events, 0.1 us)
Async XLA Ops:
  0.0 2.5 %collective-permute-start = (bf16[2,32,256]{2,1,0:T(8,128)(2,1)}, bf16[2,32,256]{2,1,0:T(8,128)(2,1)S(1)}, u32[]{:S(2)}, u32[]{:S(2)}) collective-permute-start(bf16[2,32,256]{2,1,0:T(8,128)(2,1)} %bitcast.42), channel_id=1, source_target_pairs={{0,1},{1,0},{2,3},{3,2},{4,5},{5,4},{6,7},{7,6},{8,9},{9,8},{10,11... | collective-permute-start | bytes 98312 | tf_op jit(solution)/shard_map/ppermute | solution.py:475
  0.0 0.7 %copy-start.5 = (bf16[16,1,3,3]{0,3,2,1:T(4,128)(2,1)S(1)}, bf16[16,1,3,3]{0,3,2,1:T(4,128)(2,1)}, u32[]{:S(2)}) copy-start(bf16[16,1,3,3]{0,3,2,1:T(4,128)(2,1)} %param.13) | copy-start | bytes 868
  0.0 0.7 %copy-start.7 = (bf16[1,16]{1,0:T(2,128)(2,1)S(1)}, bf16[1,16]{1,0:T(2,128)(2,1)}, u32[]{:S(2)}) copy-start(bf16[1,16]{1,0:T(2,128)(2,1)} %param.18) | copy-start | bytes 100
  1.6 0.9 %copy-start.3 = (bf16[2,1,32,256]{3,2,1,0:T(8,128)(2,1)S(1)}, bf16[2,1,32,256]{3,2,1,0:T(8,128)(2,1)}, u32[]{:S(2)}) copy-start(bf16[2,1,32,256]{3,2,1,0:T(8,128)(2,1)} %param.12) | copy-start | bytes 98308
  2.5 5.8 %collective-permute-start.1 = (bf16[2,32,256]{2,1,0:T(8,128)(2,1)S(1)}, bf16[2,32,256]{2,1,0:T(8,128)(2,1)S(1)}, u32[]{:S(2)}, u32[]{:S(2)}) collective-permute-start(bf16[2,32,256]{2,1,0:T(8,128)(2,1)S(1)} %pad_maximum_fusion.planes_ref), channel_id=1, source_target_pairs={{1,112},{16,0},{17,1},{32,16},{33,17},{48,32},{49,33},{64,48},{65,... | collective-permute-start | bytes 98312 | tf_op jit(solution)/shard_map/ppermute | solution.py:497
  12.3 9.0 %copy-start = (bf16[8,16,3,3,3]{1,0,4,3,2:T(8,128)(2,1)S(1)}, bf16[8,16,3,3,3]{1,0,4,3,2:T(8,128)(2,1)}, u32[]{:S(2)}) copy-start(bf16[8,16,3,3,3]{1,0,4,3,2:T(8,128)(2,1)} %param.22) | copy-start | bytes 20740
  12.3 9.0 %copy-start.1 = (bf16[8,8,3,3,3]{1,0,4,3,2:T(8,128)(2,1)S(1)}, bf16[8,8,3,3,3]{1,0,4,3,2:T(8,128)(2,1)}, u32[]{:S(2)}) copy-start(bf16[8,8,3,3,3]{1,0,4,3,2:T(8,128)(2,1)} %param.21) | copy-start | bytes 10372
  12.3 9.0 %copy-start.2 = (bf16[8,8,3,3,3]{1,0,4,3,2:T(8,128)(2,1)S(1)}, bf16[8,8,3,3,3]{1,0,4,3,2:T(8,128)(2,1)}, u32[]{:S(2)}) copy-start(bf16[8,8,3,3,3]{1,0,4,3,2:T(8,128)(2,1)} %param.20) | copy-start | bytes 10372
  12.3 9.0 %copy-start.6 = (bf16[8,8]{1,0:T(8,128)(2,1)S(1)}, bf16[8,8]{1,0:T(8,128)(2,1)}, u32[]{:S(2)}) copy-start(bf16[8,8]{1,0:T(8,128)(2,1)} %param.23) | copy-start | bytes 388
  12.3 18.7 %all-to-all-start = ((bf16[8,48,128]{2,1,0:T(8,128)(2,1)}), bf16[8,48,128]{2,1,0:T(8,128)(2,1)S(1)}, u32[]{:S(2)}, u32[]{:S(2)}) async-start(bf16[8,48,128]{2,1,0:T(8,128)(2,1)} %shard_map.120), calls=%async_computation | async-start | bytes 196608 | tf_op jit(solution)/shard_map/all_to_all | solution.py:503
  21.3 0.7 %copy-start.4 = (bf16[8,1,3,3,3]{0,4,3,2,1:T(4,128)(2,1)S(1)}, bf16[8,1,3,3,3]{0,4,3,2,1:T(4,128)(2,1)}, u32[]{:S(2)}) copy-start(bf16[8,1,3,3,3]{0,4,3,2,1:T(4,128)(2,1)} %param.19) | copy-start | bytes 1300

commit v7 on v6

--- a/solution.py
+++ b/solution.py
@@ -133,9 +133,9 @@
             same_level(b_ref, ky * 256, 2, [stacked(w[kx], ky, 16) for kx in range(3)], 16)
         taps = [stacked(w_rise[kx], ky, 16) for kx in range(3)]
         from_coarse(b_up, (), 768 + ky * 128, 2, 1, taps, 16)
-    b_mid[:, 768:] = jnp.zeros((256, 256), BF)
-    b_mid[240:256, 768:896] = edge_rows(w_mid[2], 0).astype(BF)
-    b_mid[0:16, 896:1024] = edge_rows(w_mid[0], 4).astype(BF)
+    b_mid[:, 768:] = jnp.zeros((256, 128), BF)
+    b_mid[240:256, 768:] = edge_rows(w_mid[2], 0).astype(BF)
+    b_mid[0:16, 768:] = edge_rows(w_mid[0], 4).astype(BF)
     b_up[:, 1152:] = jnp.zeros((256, 256), BF)
     b_up[240:256, 1152:1280] = (edge_rows(w_skip[2], 0) + edge_rows(w_rise[2], 4)).astype(BF)
     b_up[0:16, 1280:1408] = (edge_rows(w_skip[0], 0) + edge_rows(w_rise[0], 4)).astype(BF)
@@ -183,7 +183,7 @@
         r, group = iota(v.shape, 0) % length, iota(v.shape, 1) // 16 % 4
         down = jnp.where(r == 0, 0.0, rolled(v, 1))
         up = jnp.where(r == length - 1, 0.0, rolled(v, -1))
-        return jnp.where(group == 0, down, jnp.where(group == 1, v, up)).astype(BF)
+        return jnp.where(group == 0, down, jnp.where(group == 1, v, up))
 
     def lanes(ref, *pieces):
         return jnp.concatenate([ref[:, at : at + size] for at, size in pieces], axis=1)
@@ -195,13 +195,15 @@
         first = jnp.maximum(nn(three.astype(BF), b_in[...]), 0.0)
         rows_q = slice(q * 256, (q + 1) * 256)
         place(lhs.at[rows_q], 0, 512, first[:, :512], 256)
-        lhs[rows_q, 1536:] = taps_apart(first[:, 512:], 256)
+        apart = taps_apart(first[:, 512:], 256)
+        lhs[rows_q, 1536:1664] = jnp.where(lane < 64, apart, 0.0).astype(BF)
+        lhs[rows_q, 1664:] = jnp.where(lane < 64, 0.0, apart).astype(BF)
     halves = []
     for x in range(2):
         cells = [(ky * 512 + x * 256, 256) for ky in range(3)]
-        bands = lanes(b_mid, (0, 768), (768 + x * 128, 128))
-        halves.append(jnp.maximum(nt(lanes(lhs, *cells, (1536, 128)), bands), 0.0))
-    skip = jnp.concatenate(halves, axis=1)
+        halves.append(lanes(lhs, *cells, (1536 + x * 128, 128)))
+    skip = jnp.maximum(nt(jnp.concatenate(halves, axis=0), b_mid[...]), 0.0)
+    skip = jnp.concatenate([skip[: planes * 256], skip[planes * 256 :]], axis=1)
     place(wide, 0, 512, skip, 256)
     fine = nt(skip.astype(BF), b_pool[:256])
     for c in range(2):
@@ -219,7 +221,7 @@
         half[pl.ds(1, low_rows, stride=2), :] = part
         raised[:, c * 128 : (c + 1) * 128] = half[...]
     place(wide, 1536, 256, raised[...], 256)
-    wide[:, 2304:] = taps_apart(nt(lanes(wide, (640, 256), (1792, 256)), b_pool[256:]), 256)
+    wide[:, 2304:] = taps_apart(nt(lanes(wide, (640, 256), (1792, 256)), b_pool[256:]), 256).astype(BF)
     halves = []
     for x in range(2):
         cells = [(ky * 512 + x * 256, 256) for ky in range(3)]
@@ -455,7 +457,7 @@
         functools.partial(denoise_kernel, rim),
         bf(NZ, 48, 128),
         [
-            vmem((count * 256, 1664), BF),
+            vmem((count * 256, 1792), BF),
             vmem((count * 256, 2560), BF),
             vmem((count * 128, 256), F32),
             vmem((count * 256, 128), F32),
@@ -480,7 +482,7 @@
         plane_weights_kernel,
         [
             bf(128, 640),
-            bf(256, 1024),
+            bf(256, 896),
             bf(256, 768),
             bf(256, 768),
             bf(256, 1408),

time: 52.4 us -> 53.5 us (1.021)
  waiting for transfers between devices: 8.74 us -> 7.56 us
  Pallas kernels: 20.1 us -> 21.2 us
  blocking collectives: 10.4 us -> 11 us
  starting transfers between devices: 10.3 us -> 10.9 us
    pallas_call x6, Pallas kernels: 20.1 us -> 21.2 us  [call(): pl.pallas_call(kernel, out_shape=out_shape, in_specs=[spec] * len(args),...]
    ppermute x1, waiting for transfers between devices: 1.08 us -> 0.47 us  [per_device(): rim = lax.ppermute(own, ('i', 'z', 'c'), rim_pairs())]
    all_to_all x1, blocking collectives: 10.4 us -> 11 us  [per_device(): parts = lax.all_to_all(logits, 'i', 0, 0, tiled=True)]
    all_to_all x1, starting transfers between devices: 9 us -> 9.6 us  [per_device(): window = lax.all_to_all(volume, 'z', 0, 0, tiled=True)]
    all_to_all x1, waiting for transfers between devices: 7.66 us -> 7.08 us  [per_device(): window = lax.all_to_all(volume, 'z', 0, 0, tiled=True)]
  transfers between devices with their start and end apart: 3 -> 3, of which waited for: 2 -> 2; matrix products, arithmetic and copies ran while one was open for 2% -> 2% of each run, Pallas kernels for 11% -> 12%
where the time goes in v7:
time: 53.5 us; the launch traced here: 53.1 us
  Pallas kernels  21.2 us (40%)
  blocking collectives  11 us (21%)
  starting transfers between devices  10.9 us (20%)
  waiting for transfers between devices  7.56 us (14%)
  local copies, waits for them, and re-layouts  1.36 us (3%)
  other arithmetic  0.92 us (2%)
    pallas_call x6, Pallas kernels, call(): pl.pallas_call(kernel, out_shape=out_shape, in_specs=[spec] * len(args),...  21.2 us
    all_to_all x1, blocking collectives, per_device(): parts = lax.all_to_all(logits, 'i', 0, 0, tiled=True)  11 us
    all_to_all x1, starting transfers between devices, per_device(): window = lax.all_to_all(volume, 'z', 0, 0, tiled=True)  9.6 us
    all_to_all x1, waiting for transfers between devices, per_device(): window = lax.all_to_all(volume, 'z', 0, 0, tiled=True)  7.08 us
    unnamed x16, local copies, waits for them, and re-layouts  1.36 us
    ppermute x1, starting transfers between devices, per_device(): rim = lax.ppermute(own, ('i', 'z', 'c'), rim_pairs())  1.29 us
  transfers between devices with their start and end apart: 3, of which 2 were waited for; matrix products, arithmetic and copies ran while one was open for 2% of the time, Pallas kernels for 12%

profile of v7, /device:TPU:16, one launch (start us, length us, event | category | flops | bytes accessed | tf_op | source)
XLA Modules:
  0.0 53.1 jit_solution(3015861428290155693)
XLA Ops:
  0.0 0.0 collective-permute-start
  0.0 0.0 copy-start.5
  0.0 0.0 copy-start.7
  0.0 0.7 %copy-done.5 = bf16[16,1,3,3]{0,3,2,1:T(4,128)(2,1)S(1)} copy-done((bf16[16,1,3,3]{0,3,2,1:T(4,128)(2,1)S(1)}, bf16[16,1,3,3]{0,3,2,1:T(4,128)(2,1)}, u32[]{:S(2)}) %copy-start.5) | copy-done | bytes 312
  0.7 0.0 copy-done.7
  0.7 0.9 %pad_add_fusion.1.w_ref = bf16[3,208,32]{2,1,0:T(8,128)(2,1)S(1)} fusion(bf16[1,1,16]{2,1,0:T(2,128)(2,1)S(1)} %bitcast.46, bf16[3,3,16]{2,1,0:T(4,128)(2,1)S(1)} %bitcast.44, bf16[3,48,32]{2,1,0:T(8,128)(2,1)} %bitcast.38, bf16[3,48,16]{2,1,0:T(8,128)(2,1)} %bitcast.39, bf16[3,48,16]{2,1,0:T(8,128)(2,1)} %bitcast.40, bf16[3,48,16]{2,1,0:T(8,128)(2,1)} %bitcast.41), kind=kLoop, calls=%fused_computation.1 | loop fusion | flops 239616 | bytes 63296 | tf_op jit(solution)/shard_map/add | solution.py:417
  1.6 0.0 copy-start.3
  1.6 0.9 %shard_map.118 = (bf16[128,640]{1,0:T(8,128)(2,1)S(1)}, bf16[256,896]{1,0:T(8,128)(2,1)S(1)}, bf16[256,768]{1,0:T(8,128)(2,1)S(1)}, bf16[256,768]{1,0:T(8,128)(2...) custom-call(bf16[3,208,32]{2,1,0:T(8,128)(2,1)S(1)} %pad_add_fusion.1.w_ref), custom_call_target="tpu_custom_call" | custom-call | tf_op jit(solution)/shard_map/pallas_call | solution.py:399
  2.5 0.0 collective-permute-done
  2.5 0.0 copy-done.3
  2.5 1.3 %collective-permute-start.1 = (bf16[2,32,256]{2,1,0:T(8,128)(2,1)S(1)}, bf16[2,32,256]{2,1,0:T(8,128)(2,1)S(1)}, u32[]{:S(2)}, u32[]{:S(2)}) collective-permute-start(bf16[2,32,256]{2,1,0:T(8,128)(2,1)S(1)} %pad_maximum_fusion.planes_ref), channel_id=1, source_target_pairs={{1,112},{16,0},{17,1},{32,16},{33,17},{48,32},{49,33},{64,48},{65,... | collective-permute-start | bytes 98312 | tf_op jit(solution)/shard_map/ppermute | solution.py:499
  3.8 4.0 %shard_map.119.refs_0_ = bf16[8,48,128]{2,1,0:T(8,128)(2,1)S(1)} custom-call(bf16[2,32,256]{2,1,0:T(8,128)(2,1)S(1)} %pad_maximum_fusion.planes_ref, bf16[128,640]{1,0:T(8,128)(2,1)S(1)} %get-tuple-element.32.refs_0_.refs_1_, bf16[256,896]{1,0:T(8,128)(2,1)S(1)} %get-tuple-element.33.refs_1_.refs_2_, bf16[256,768]{1,0:T(8,128)(2,1)S(1)} %get-tuple-element.34.refs_2_.refs_3_, ...), custom_call_target="tpu_custom_call" | custom-call | tf_op jit(solution)/shard_map/pallas_call | solution.py:399
  7.9 0.5 collective-permute-done.1.planes_ref
  8.3 4.4 %shard_map.120 = bf16[8,48,128]{2,1,0:T(8,128)(2,1)} custom-call(bf16[2,32,256]{2,1,0:T(8,128)(2,1)S(1)} %collective-permute-done.1.planes_ref, bf16[8,48,128]{2,1,0:T(8,128)(2,1)S(1)} %shard_map.119.refs_0_, bf16[128,640]{1,0:T(8,128)(2,1)S(1)} %get-tuple-element.32.refs_0_.refs_1_, bf16[256,896]{1,0:T(8,128)(2,1)S(1)} %get-tuple-element.33.refs_1_.refs_2_, ...), custom_call_target="tpu_custom_call" | custom-call | tf_op jit(solution)/shard_map/pallas_call | solution.py:399
  12.8 0.0 copy-start
  12.8 0.0 copy-start.1
  12.8 0.0 copy-start.2
  12.8 0.0 copy-start.6
  12.8 9.6 %all-to-all-start = ((bf16[8,48,128]{2,1,0:T(8,128)(2,1)}), bf16[8,48,128]{2,1,0:T(8,128)(2,1)S(1)}, u32[]{:S(2)}, u32[]{:S(2)}) async-start(bf16[8,48,128]{2,1,0:T(8,128)(2,1)} %shard_map.120), calls=%async_computation | async-start | bytes 196608 | tf_op jit(solution)/shard_map/all_to_all | solution.py:505
  22.4 0.0 copy-start.4
  22.4 0.0 copy-done
  22.4 0.0 copy-done.1
  22.4 0.0 copy-done.2
  22.4 0.0 copy-done.6
  22.4 0.7 %copy-done.4 = bf16[8,1,3,3,3]{0,4,3,2,1:T(4,128)(2,1)S(1)} copy-done((bf16[8,1,3,3,3]{0,4,3,2,1:T(4,128)(2,1)S(1)}, bf16[8,1,3,3,3]{0,4,3,2,1:T(4,128)(2,1)}, u32[]{:S(2)}) %copy-start.4) | copy-done | bytes 456
  23.1 1.3 %shard_map.121 = (bf16[3,128,1152]{2,1,0:T(8,128)(2,1)S(1)}, bf16[3,128,1152]{2,1,0:T(8,128)(2,1)S(1)}, bf16[3,128,1152]{2,1,0:T(8,128)(2,1)S(1)}, bf16[3,256,384]{2,1,0:T(8,128)(2,1)S(1)}) custom-call(bf16[9,88,16]{2,1,0:T(8,128)(2,1)S(1)} %pad_add_fusion.w_ref), custom_call_target="tpu_custom_call" | custom-call | tf_op jit(solution)/shard_map/pallas_call | solution.py:399
  24.4 7.1 %all-to-all-done.v_ref = bf16[8,48,128]{2,1,0:T(8,128)(2,1)S(1)} async-done(((bf16[8,48,128]{2,1,0:T(8,128)(2,1)}), bf16[8,48,128]{2,1,0:T(8,128)(2,1)S(1)}, u32[]{:S(2)}, u32[]{:S(2)}) %all-to-all-start) | async-done | bytes 98336 | tf_op jit(solution)/shard_map/all_to_all | solution.py:505
  31.5 9.4 %shard_map.122 = bf16[8,16,512]{2,1,0:T(8,128)(2,1)S(1)} custom-call(bf16[8,48,128]{2,1,0:T(8,128)(2,1)S(1)} %all-to-all-done.v_ref, bf16[3,128,1152]{2,1,0:T(8,128)(2,1)S(1)} %get-tuple-element.39.b_rest, bf16[3,128,1152]{2,1,0:T(8,128)(2,1)S(1)} %get-tuple-element.40.b_mid, bf16[3,128,1152]{2,1,0:T(8,128)(2,1)S(1)} %get-tuple-element.41.b_skip, ...), custom_call_target="tpu_custom_call" | custom-call | tf_op jit(solution)/shard_map/pallas_call | solution.py:399
  40.9 11.0 %all_to_all.10.parts_ref = bf16[8,16,512]{2,1,0:T(8,128)(2,1)S(1)} all-to-all(bf16[8,16,512]{2,1,0:T(8,128)(2,1)S(1)} %shard_map.122), channel_id=1, replica_groups=mesh['rep'=2,'i'=8,'z'=8,'c'=2] {'i'}, dimensions={0} | all-to-all | bytes 262144 | tf_op jit(solution)/shard_map/all_to_all | solution.py:523
  52.0 1.1 %shard_map.123 = f32[512,128]{1,0:T(8,128)} custom-call(bf16[8,16,512]{2,1,0:T(8,128)(2,1)S(1)} %all_to_all.10.parts_ref), custom_call_target="tpu_custom_call" | custom-call | tf_op jit(solution)/shard_map/pallas_call | solution.py:399
  (3 shorter events, 0.1 us)
Async XLA Ops:
  0.0 2.5 %collective-permute-start = (bf16[2,32,256]{2,1,0:T(8,128)(2,1)}, bf16[2,32,256]{2,1,0:T(8,128)(2,1)S(1)}, u32[]{:S(2)}, u32[]{:S(2)}) collective-permute-start(bf16[2,32,256]{2,1,0:T(8,128)(2,1)} %bitcast.42), channel_id=1, source_target_pairs={{0,1},{1,0},{2,3},{3,2},{4,5},{5,4},{6,7},{7,6},{8,9},{9,8},{10,11... | collective-permute-start | bytes 98312 | tf_op jit(solution)/shard_map/ppermute | solution.py:477
  0.0 0.7 %copy-start.5 = (bf16[16,1,3,3]{0,3,2,1:T(4,128)(2,1)S(1)}, bf16[16,1,3,3]{0,3,2,1:T(4,128)(2,1)}, u32[]{:S(2)}) copy-start(bf16[16,1,3,3]{0,3,2,1:T(4,128)(2,1)} %param.13) | copy-start | bytes 868
  0.0 0.7 %copy-start.7 = (bf16[1,16]{1,0:T(2,128)(2,1)S(1)}, bf16[1,16]{1,0:T(2,128)(2,1)}, u32[]{:S(2)}) copy-start(bf16[1,16]{1,0:T(2,128)(2,1)} %param.18) | copy-start | bytes 100
  1.6 0.9 %copy-start.3 = (bf16[2,1,32,256]{3,2,1,0:T(8,128)(2,1)S(1)}, bf16[2,1,32,256]{3,2,1,0:T(8,128)(2,1)}, u32[]{:S(2)}) copy-start(bf16[2,1,32,256]{3,2,1,0:T(8,128)(2,1)} %param.12) | copy-start | bytes 98308
  2.5 5.8 %collective-permute-start.1 = (bf16[2,32,256]{2,1,0:T(8,128)(2,1)S(1)}, bf16[2,32,256]{2,1,0:T(8,128)(2,1)S(1)}, u32[]{:S(2)}, u32[]{:S(2)}) collective-permute-start(bf16[2,32,256]{2,1,0:T(8,128)(2,1)S(1)} %pad_maximum_fusion.planes_ref), channel_id=1, source_target_pairs={{1,112},{16,0},{17,1},{32,16},{33,17},{48,32},{49,33},{64,48},{65,... | collective-permute-start | bytes 98312 | tf_op jit(solution)/shard_map/ppermute | solution.py:499
  12.8 9.6 %copy-start = (bf16[8,16,3,3,3]{1,0,4,3,2:T(8,128)(2,1)S(1)}, bf16[8,16,3,3,3]{1,0,4,3,2:T(8,128)(2,1)}, u32[]{:S(2)}) copy-start(bf16[8,16,3,3,3]{1,0,4,3,2:T(8,128)(2,1)} %param.22) | copy-start | bytes 20740
  12.8 9.6 %copy-start.1 = (bf16[8,8,3,3,3]{1,0,4,3,2:T(8,128)(2,1)S(1)}, bf16[8,8,3,3,3]{1,0,4,3,2:T(8,128)(2,1)}, u32[]{:S(2)}) copy-start(bf16[8,8,3,3,3]{1,0,4,3,2:T(8,128)(2,1)} %param.21) | copy-start | bytes 10372
  12.8 9.6 %copy-start.2 = (bf16[8,8,3,3,3]{1,0,4,3,2:T(8,128)(2,1)S(1)}, bf16[8,8,3,3,3]{1,0,4,3,2:T(8,128)(2,1)}, u32[]{:S(2)}) copy-start(bf16[8,8,3,3,3]{1,0,4,3,2:T(8,128)(2,1)} %param.20) | copy-start | bytes 10372
  12.8 9.6 %copy-start.6 = (bf16[8,8]{1,0:T(8,128)(2,1)S(1)}, bf16[8,8]{1,0:T(8,128)(2,1)}, u32[]{:S(2)}) copy-start(bf16[8,8]{1,0:T(8,128)(2,1)} %param.23) | copy-start | bytes 388
  12.8 18.7 %all-to-all-start = ((bf16[8,48,128]{2,1,0:T(8,128)(2,1)}), bf16[8,48,128]{2,1,0:T(8,128)(2,1)S(1)}, u32[]{:S(2)}, u32[]{:S(2)}) async-start(bf16[8,48,128]{2,1,0:T(8,128)(2,1)} %shard_map.120), calls=%async_computation | async-start | bytes 196608 | tf_op jit(solution)/shard_map/all_to_all | solution.py:505
  22.4 0.7 %copy-start.4 = (bf16[8,1,3,3,3]{0,4,3,2,1:T(4,128)(2,1)S(1)}, bf16[8,1,3,3,3]{0,4,3,2,1:T(4,128)(2,1)}, u32[]{:S(2)}) copy-start(bf16[8,1,3,3,3]{0,4,3,2,1:T(4,128)(2,1)} %param.19) | copy-start | bytes 1300

commit v8 on v6

--- a/solution.py
+++ b/solution.py
@@ -354,9 +354,8 @@
         for kz, steps in enumerate((1, 0, -1)):
             moved = rolled(q, steps) if steps else q
             ql[:, :, kz * 128 : (kz + 1) * 128] = moved.astype(BF).reshape(20, 16, 128)
-        acc = jnp.zeros((288, 128), F32)
-        for ky in range(3):
-            acc = acc + nt(ql[ky : ky + 18].reshape(288, 384), b_rest[ky, :, 512:896])
+        rows = jnp.concatenate([ql[ky : ky + 18].reshape(288, 384) for ky in range(3)], axis=1)
+        acc = nt(rows, jnp.concatenate([b_rest[ky, :, 512:896] for ky in range(3)], axis=1))
         h3 = masked(
             acc, inside(18, 16 * at_z - 1, 16, 64 * at_c + 8 * at_i - 2, 128)
         )

time: 52.4 us -> 52.5 us (level)
  no operation moved by 1% of the time
where the time goes in v8:
time: 52.5 us; the launch traced here: 52.1 us
  Pallas kernels  20.2 us (38%)
  blocking collectives  10.4 us (20%)
  starting transfers between devices  10.3 us (20%)
  waiting for transfers between devices  8.74 us (17%)
  local copies, waits for them, and re-layouts  1.36 us (3%)
  other arithmetic  0.92 us (2%)
    pallas_call x6, Pallas kernels, call(): pl.pallas_call(kernel, out_shape=out_shape, in_specs=[spec] * len(args),...  20.2 us
    all_to_all x1, blocking collectives, per_device(): parts = lax.all_to_all(logits, 'i', 0, 0, tiled=True)  10.4 us
    all_to_all x1, starting transfers between devices, per_device(): window = lax.all_to_all(volume, 'z', 0, 0, tiled=True)  9 us
    all_to_all x1, waiting for transfers between devices, per_device(): window = lax.all_to_all(volume, 'z', 0, 0, tiled=True)  7.66 us
    unnamed x16, local copies, waits for them, and re-layouts  1.36 us
    ppermute x1, starting transfers between devices, per_device(): rim = lax.ppermute(own, ('i', 'z', 'c'), rim_pairs())  1.29 us
    ppermute x1, waiting for transfers between devices, per_device(): rim = lax.ppermute(own, ('i', 'z', 'c'), rim_pairs())  1.08 us
  transfers between devices with their start and end apart: 3, of which 2 were waited for; matrix products, arithmetic and copies ran while one was open for 2% of the time, Pallas kernels for 11%

profile of v8, /device:TPU:16, one launch (start us, length us, event | category | flops | bytes accessed | tf_op | source)
XLA Modules:
  0.0 52.1 jit_solution(3188726949232414907)
XLA Ops:
  0.0 0.0 collective-permute-start
  0.0 0.0 copy-start.5
  0.0 0.0 copy-start.7
  0.0 0.7 %copy-done.5 = bf16[16,1,3,3]{0,3,2,1:T(4,128)(2,1)S(1)} copy-done((bf16[16,1,3,3]{0,3,2,1:T(4,128)(2,1)S(1)}, bf16[16,1,3,3]{0,3,2,1:T(4,128)(2,1)}, u32[]{:S(2)}) %copy-start.5) | copy-done | bytes 312
  0.7 0.0 copy-done.7
  0.7 0.9 %pad_add_fusion.1.w_ref = bf16[3,208,32]{2,1,0:T(8,128)(2,1)S(1)} fusion(bf16[1,1,16]{2,1,0:T(2,128)(2,1)S(1)} %bitcast.46, bf16[3,3,16]{2,1,0:T(4,128)(2,1)S(1)} %bitcast.44, bf16[3,48,32]{2,1,0:T(8,128)(2,1)} %bitcast.38, bf16[3,48,16]{2,1,0:T(8,128)(2,1)} %bitcast.39, bf16[3,48,16]{2,1,0:T(8,128)(2,1)} %bitcast.40, bf16[3,48,16]{2,1,0:T(8,128)(2,1)} %bitcast.41), kind=kLoop, calls=%fused_computation.1 | loop fusion | flops 239616 | bytes 63296 | tf_op jit(solution)/shard_map/add | solution.py:414
  1.6 0.0 copy-start.3
  1.6 0.9 %shard_map.118 = (bf16[128,640]{1,0:T(8,128)(2,1)S(1)}, bf16[256,1024]{1,0:T(8,128)(2,1)S(1)}, bf16[256,768]{1,0:T(8,128)(2,1)S(1)}, bf16[256,768]{1,0:T(8,128)(...) custom-call(bf16[3,208,32]{2,1,0:T(8,128)(2,1)S(1)} %pad_add_fusion.1.w_ref), custom_call_target="tpu_custom_call" | custom-call | tf_op jit(solution)/shard_map/pallas_call | solution.py:396
  2.5 0.0 collective-permute-done
  2.5 0.0 copy-done.3
  2.5 1.3 %collective-permute-start.1 = (bf16[2,32,256]{2,1,0:T(8,128)(2,1)S(1)}, bf16[2,32,256]{2,1,0:T(8,128)(2,1)S(1)}, u32[]{:S(2)}, u32[]{:S(2)}) collective-permute-start(bf16[2,32,256]{2,1,0:T(8,128)(2,1)S(1)} %pad_maximum_fusion.planes_ref), channel_id=1, source_target_pairs={{1,112},{16,0},{17,1},{32,16},{33,17},{48,32},{49,33},{64,48},{65,... | collective-permute-start | bytes 98312 | tf_op jit(solution)/shard_map/ppermute | solution.py:496
  3.8 3.4 %shard_map.119.refs_0_ = bf16[8,48,128]{2,1,0:T(8,128)(2,1)S(1)} custom-call(bf16[2,32,256]{2,1,0:T(8,128)(2,1)S(1)} %pad_maximum_fusion.planes_ref, bf16[128,640]{1,0:T(8,128)(2,1)S(1)} %get-tuple-element.32.refs_0_.refs_1_, bf16[256,1024]{1,0:T(8,128)(2,1)S(1)} %get-tuple-element.33.refs_1_.refs_2_, ...), custom_call_target="tpu_custom_call" | custom-call | tf_op jit(solution)/shard_map/pallas_call | solution.py:396
  7.3 1.1 %collective-permute-done.1.planes_ref = bf16[2,32,256]{2,1,0:T(8,128)(2,1)S(1)} collective-permute-done((bf16[2,32,256]{2,1,0:T(8,128)(2,1)S(1)}, bf16[2,32,256]{2,1,0:T(8,128)(2,1)S(1)}, u32[]{:S(2)}, u32[]{:S(2)}) %collective-permute-start.1) | collective-permute-done | bytes 32800 | tf_op jit(solution)/shard_map/ppermute | solution.py:496
  8.3 3.9 %shard_map.120 = bf16[8,48,128]{2,1,0:T(8,128)(2,1)} custom-call(bf16[2,32,256]{2,1,0:T(8,128)(2,1)S(1)} %collective-permute-done.1.planes_ref, bf16[8,48,128]{2,1,0:T(8,128)(2,1)S(1)} %shard_map.119.refs_0_, bf16[128,640]{1,0:T(8,128)(2,1)S(1)} %get-tuple-element.32.refs_0_.refs_1_, bf16[256,1024]{1,0:T(8,128)(2,1)S(1)} %get-tuple-element.33.refs_1_.refs_2_, ...), custom_call_target="tpu_custom_call" | custom-call | tf_op jit(solution)/shard_map/pallas_call | solution.py:396
  12.3 0.0 copy-start
  12.3 0.0 copy-start.1
  12.3 0.0 copy-start.2
  12.3 0.0 copy-start.6
  12.3 9.0 %all-to-all-start = ((bf16[8,48,128]{2,1,0:T(8,128)(2,1)}), bf16[8,48,128]{2,1,0:T(8,128)(2,1)S(1)}, u32[]{:S(2)}, u32[]{:S(2)}) async-start(bf16[8,48,128]{2,1,0:T(8,128)(2,1)} %shard_map.120), calls=%async_computation | async-start | bytes 196608 | tf_op jit(solution)/shard_map/all_to_all | solution.py:502
  21.3 0.0 copy-start.4
  21.3 0.0 copy-done
  21.3 0.0 copy-done.1
  21.3 0.0 copy-done.2
  21.3 0.0 copy-done.6
  21.3 0.7 %copy-done.4 = bf16[8,1,3,3,3]{0,4,3,2,1:T(4,128)(2,1)S(1)} copy-done((bf16[8,1,3,3,3]{0,4,3,2,1:T(4,128)(2,1)S(1)}, bf16[8,1,3,3,3]{0,4,3,2,1:T(4,128)(2,1)}, u32[]{:S(2)}) %copy-start.4) | copy-done | bytes 456
  22.0 1.3 %shard_map.121 = (bf16[3,128,1152]{2,1,0:T(8,128)(2,1)S(1)}, bf16[3,128,1152]{2,1,0:T(8,128)(2,1)S(1)}, bf16[3,128,1152]{2,1,0:T(8,128)(2,1)S(1)}, bf16[3,256,384]{2,1,0:T(8,128)(2,1)S(1)}) custom-call(bf16[9,88,16]{2,1,0:T(8,128)(2,1)S(1)} %pad_add_fusion.w_ref), custom_call_target="tpu_custom_call" | custom-call | tf_op jit(solution)/shard_map/pallas_call | solution.py:396
  23.4 7.7 %all-to-all-done.v_ref = bf16[8,48,128]{2,1,0:T(8,128)(2,1)S(1)} async-done(((bf16[8,48,128]{2,1,0:T(8,128)(2,1)}), bf16[8,48,128]{2,1,0:T(8,128)(2,1)S(1)}, u32[]{:S(2)}, u32[]{:S(2)}) %all-to-all-start) | async-done | bytes 98336 | tf_op jit(solution)/shard_map/all_to_all | solution.py:502
  31.0 9.5 %shard_map.122 = bf16[8,16,512]{2,1,0:T(8,128)(2,1)S(1)} custom-call(bf16[8,48,128]{2,1,0:T(8,128)(2,1)S(1)} %all-to-all-done.v_ref, bf16[3,128,1152]{2,1,0:T(8,128)(2,1)S(1)} %get-tuple-element.39.b_rest, bf16[3,128,1152]{2,1,0:T(8,128)(2,1)S(1)} %get-tuple-element.40.b_mid, bf16[3,128,1152]{2,1,0:T(8,128)(2,1)S(1)} %get-tuple-element.41.b_skip, ...), custom_call_target="tpu_custom_call" | custom-call | tf_op jit(solution)/shard_map/pallas_call | solution.py:396
  40.6 10.4 %all_to_all.10.parts_ref = bf16[8,16,512]{2,1,0:T(8,128)(2,1)S(1)} all-to-all(bf16[8,16,512]{2,1,0:T(8,128)(2,1)S(1)} %shard_map.122), channel_id=1, replica_groups=mesh['rep'=2,'i'=8,'z'=8,'c'=2] {'i'}, dimensions={0} | all-to-all | bytes 262144 | tf_op jit(solution)/shard_map/all_to_all | solution.py:520
  51.0 1.1 %shard_map.123 = f32[512,128]{1,0:T(8,128)} custom-call(bf16[8,16,512]{2,1,0:T(8,128)(2,1)S(1)} %all_to_all.10.parts_ref), custom_call_target="tpu_custom_call" | custom-call | tf_op jit(solution)/shard_map/pallas_call | solution.py:396
  (3 shorter events, 0.1 us)
Async XLA Ops:
  0.0 2.5 %collective-permute-start = (bf16[2,32,256]{2,1,0:T(8,128)(2,1)}, bf16[2,32,256]{2,1,0:T(8,128)(2,1)S(1)}, u32[]{:S(2)}, u32[]{:S(2)}) collective-permute-start(bf16[2,32,256]{2,1,0:T(8,128)(2,1)} %bitcast.42), channel_id=1, source_target_pairs={{0,1},{1,0},{2,3},{3,2},{4,5},{5,4},{6,7},{7,6},{8,9},{9,8},{10,11... | collective-permute-start | bytes 98312 | tf_op jit(solution)/shard_map/ppermute | solution.py:474
  0.0 0.7 %copy-start.5 = (bf16[16,1,3,3]{0,3,2,1:T(4,128)(2,1)S(1)}, bf16[16,1,3,3]{0,3,2,1:T(4,128)(2,1)}, u32[]{:S(2)}) copy-start(bf16[16,1,3,3]{0,3,2,1:T(4,128)(2,1)} %param.13) | copy-start | bytes 868
  0.0 0.7 %copy-start.7 = (bf16[1,16]{1,0:T(2,128)(2,1)S(1)}, bf16[1,16]{1,0:T(2,128)(2,1)}, u32[]{:S(2)}) copy-start(bf16[1,16]{1,0:T(2,128)(2,1)} %param.18) | copy-start | bytes 100
  1.6 0.9 %copy-start.3 = (bf16[2,1,32,256]{3,2,1,0:T(8,128)(2,1)S(1)}, bf16[2,1,32,256]{3,2,1,0:T(8,128)(2,1)}, u32[]{:S(2)}) copy-start(bf16[2,1,32,256]{3,2,1,0:T(8,128)(2,1)} %param.12) | copy-start | bytes 98308
  2.5 5.8 %collective-permute-start.1 = (bf16[2,32,256]{2,1,0:T(8,128)(2,1)S(1)}, bf16[2,32,256]{2,1,0:T(8,128)(2,1)S(1)}, u32[]{:S(2)}, u32[]{:S(2)}) collective-permute-start(bf16[2,32,256]{2,1,0:T(8,128)(2,1)S(1)} %pad_maximum_fusion.planes_ref), channel_id=1, source_target_pairs={{1,112},{16,0},{17,1},{32,16},{33,17},{48,32},{49,33},{64,48},{65,... | collective-permute-start | bytes 98312 | tf_op jit(solution)/shard_map/ppermute | solution.py:496
  12.3 9.0 %copy-start = (bf16[8,16,3,3,3]{1,0,4,3,2:T(8,128)(2,1)S(1)}, bf16[8,16,3,3,3]{1,0,4,3,2:T(8,128)(2,1)}, u32[]{:S(2)}) copy-start(bf16[8,16,3,3,3]{1,0,4,3,2:T(8,128)(2,1)} %param.22) | copy-start | bytes 20740
  12.3 9.0 %copy-start.1 = (bf16[8,8,3,3,3]{1,0,4,3,2:T(8,128)(2,1)S(1)}, bf16[8,8,3,3,3]{1,0,4,3,2:T(8,128)(2,1)}, u32[]{:S(2)}) copy-start(bf16[8,8,3,3,3]{1,0,4,3,2:T(8,128)(2,1)} %param.21) | copy-start | bytes 10372
  12.3 9.0 %copy-start.2 = (bf16[8,8,3,3,3]{1,0,4,3,2:T(8,128)(2,1)S(1)}, bf16[8,8,3,3,3]{1,0,4,3,2:T(8,128)(2,1)}, u32[]{:S(2)}) copy-start(bf16[8,8,3,3,3]{1,0,4,3,2:T(8,128)(2,1)} %param.20) | copy-start | bytes 10372
  12.3 9.0 %copy-start.6 = (bf16[8,8]{1,0:T(8,128)(2,1)S(1)}, bf16[8,8]{1,0:T(8,128)(2,1)}, u32[]{:S(2)}) copy-start(bf16[8,8]{1,0:T(8,128)(2,1)} %param.23) | copy-start | bytes 388
  12.3 18.7 %all-to-all-start = ((bf16[8,48,128]{2,1,0:T(8,128)(2,1)}), bf16[8,48,128]{2,1,0:T(8,128)(2,1)S(1)}, u32[]{:S(2)}, u32[]{:S(2)}) async-start(bf16[8,48,128]{2,1,0:T(8,128)(2,1)} %shard_map.120), calls=%async_computation | async-start | bytes 196608 | tf_op jit(solution)/shard_map/all_to_all | solution.py:502
  21.3 0.7 %copy-start.4 = (bf16[8,1,3,3,3]{0,4,3,2,1:T(4,128)(2,1)S(1)}, bf16[8,1,3,3,3]{0,4,3,2,1:T(4,128)(2,1)}, u32[]{:S(2)}) copy-start(bf16[8,1,3,3,3]{0,4,3,2,1:T(4,128)(2,1)} %param.19) | copy-start | bytes 1300
